TPU v7x, 32 devices: a whole 2x2x4 slice. The times are simulated.
32 devices in a mesh: dp: 8 (over z, x), mp: 4 (over y, core).
Axes of the slice: x: 2, y: 2, z: 4, core: 2. Of those that a mesh axis runs over, the one named last changes fastest.
Arguments:
- inputs: bfloat16 [24576, 768], P(('dp', 'mp')), may hold values from -6 to 6
- cotangent: bfloat16 [24576, 768], P(('dp', 'mp')), may hold values from -6 to 6
- routes: int32 [24576, 1], P('dp'), may hold values from 0 to 7; in each aligned block of 768 rows (0 to 767, 768 to 1535, ...) at most 120 rows name the same one
- domains: int32 [24], P('dp'), may hold values from 0 to 7
- domain_counts: int32 [8], replicated, may hold values from 5 to 15
- domain_weights: float32 [8], replicated, may hold values from 0.5 to 2
- keep_mask: int32 [24], P('dp'), may hold values 0 or 1
- gain_one: float32 [768], replicated, may hold values from 0.5 to 1.5
- shift_one: float32 [768], replicated, may hold values from -1.8 to 1.8
- w_qkv: bfloat16 [768, 3, 768], P(None, None, 'mp'), may hold values from -0.21875 to 0.21875
- w_proj: bfloat16 [768, 768], P('mp'), may hold values from -0.625 to 0.625
- gain_two: float32 [768], replicated, may hold values from 0.5 to 1.5
- shift_two: float32 [768], replicated, may hold values from -1.8 to 1.8
- w_router: bfloat16 [768, 8], replicated, may hold values from -0.15625 to 0.15625
- w_in: bfloat16 [8, 768, 3072], P('dp', None, 'mp'), may hold values from -0.21875 to 0.21875
- w_out: bfloat16 [8, 3072, 768], P('dp', 'mp'), may hold values from -0.21875 to 0.21875
Outputs:
- output: bfloat16 [24576, 768], P(('dp', 'mp'))
- input_grad: bfloat16 [24576, 768], P(('dp', 'mp'))
- grad_gain_one: float32 [768], replicated
- grad_shift_one: float32 [768], replicated
- grad_w_qkv: float32 [768, 3, 768], P(None, None, 'mp')
- grad_w_proj: float32 [768, 768], P('mp')
- grad_gain_two: float32 [768], replicated
- grad_shift_two: float32 [768], replicated
- grad_router: float32 [768, 8], replicated
- grad_w_in: float32 [8, 768, 3072], P('dp', None, 'mp')
- grad_w_out: float32 [8, 3072, 768], P('dp', 'mp')
Inputs may be any that keep to these rules, and one draw needn't show every extreme that they name: `routes`: within the rows of one device (aligned blocks of 768 tokens) each expert is named by at most 120 rows, a bound that some block reaches.
All inputs are finite; a program needn't handle non-finite values. No bound on the sum of `keep_mask` on one device may be relied on, other than what follows from the above.
Results may differ from a plain program's by a relative error of at most 0.015.
Values may be sent and summed in bfloat16 or wider, within the bound.
A program may use at most 192 MiB of HBM per device.

v0:
```python
import jax
import jax.numpy as jnp
from jax import lax
from jax.sharding import PartitionSpec as P

HEAD_DIM = 64
LEN = 1024


norm_epsilon = 1e-05
count_scale = 10.0
masked_score = -1e30


def norm_forward(features, gain_vec, shift_vec):
    centre = features - jnp.mean(features, axis=-1, keepdims=True)
    inverse = lax.rsqrt(jnp.mean(centre * centre, axis=-1, keepdims=True) + norm_epsilon)
    scaled = centre * inverse
    return (scaled * gain_vec + shift_vec, scaled, inverse)


def norm_backward(d_normed, scaled, inverse, gain_vec):
    d_scaled = d_normed * gain_vec
    correction = jnp.mean(d_scaled, axis=-1, keepdims=True) + scaled * jnp.mean(
        d_scaled * scaled, axis=-1, keepdims=True
    )
    return (
        inverse * (d_scaled - correction),
        jnp.sum(d_normed * scaled, axis=0),
        jnp.sum(d_normed, axis=0),
    )


def causal_scores(queries, keys_all):
    scale_qk = queries.shape[-1] ** (-0.5)
    raw_scores = (
        jnp.einsum("qhd,khd->hqk", queries, keys_all, preferred_element_type=jnp.float32) * scale_qk
    )
    places = jnp.arange(queries.shape[0])
    return jnp.where(places[None, :, None] >= places[None, None, :], raw_scores, masked_score)


def attend_forward(packed):
    scores = causal_scores(packed[:, 0], packed[:, 1])
    largest = jnp.max(scores, axis=-1, keepdims=True)
    expo_vals = jnp.exp(scores - largest)
    totals = jnp.sum(expo_vals, axis=-1, keepdims=True)
    attn_probs = (expo_vals / totals).astype(jnp.bfloat16)
    mixture = jnp.einsum(
        "hqk,khd->qhd", attn_probs, packed[:, 2], preferred_element_type=jnp.float32
    )
    return (mixture.astype(jnp.bfloat16), largest + jnp.log(totals))


def attend_backward(operands):
    packed, d_mixture, log_total = operands
    queries, keys_all, values_all = (packed[:, 0], packed[:, 1], packed[:, 2])
    scale_qk = queries.shape[-1] ** (-0.5)
    scores = causal_scores(queries, keys_all)
    attn_probs = jnp.exp(scores - log_total)
    d_values = jnp.einsum(
        "hqk,qhd->khd",
        attn_probs.astype(jnp.bfloat16),
        d_mixture,
        preferred_element_type=jnp.float32,
    )
    d_probs = jnp.einsum("qhd,khd->hqk", d_mixture, values_all, preferred_element_type=jnp.float32)
    d_scores = (
        attn_probs * (d_probs - jnp.sum(attn_probs * d_probs, axis=-1, keepdims=True))
    ).astype(jnp.bfloat16)
    d_queries = (
        jnp.einsum("hqk,khd->qhd", d_scores, keys_all, preferred_element_type=jnp.float32)
        * scale_qk
    )
    d_keys = (
        jnp.einsum("hqk,qhd->khd", d_scores, queries, preferred_element_type=jnp.float32) * scale_qk
    )
    return jnp.stack([d_queries, d_keys, d_values], axis=1).astype(jnp.bfloat16)


def shard_ranks(chosen, expert_ids):
    onehot_int = (chosen[:, :, None] == expert_ids[None, None, :]).astype(jnp.int32)
    running = jnp.cumsum(onehot_int, axis=1)
    return jnp.sum(running * onehot_int, axis=2) - 1


def to_experts(buffer):
    arrived = lax.all_to_all(buffer, "dp", split_axis=0, concat_axis=0, tiled=True)
    return arrived


def from_experts(expert_result):
    return lax.all_to_all(
        expert_result.astype(jnp.bfloat16), "dp", split_axis=0, concat_axis=0, tiled=True
    )


def shards(
    inputs,
    cotangent,
    routes,
    domains,
    domain_counts,
    domain_weights,
    keep_mask,
    gain_one,
    shift_one,
    w_qkv,
    w_proj,
    gain_two,
    shift_two,
    w_router,
    w_in,
    w_out,
):
    tok_rows = inputs.shape[0]
    model_width = inputs.shape[1]
    experts_all = w_router.shape[1]
    capacity = max(2, tok_rows * 5 // (4 * experts_all))
    mp_index = lax.axis_index("mp")
    group_rows = routes.shape[0]
    seq_count = group_rows // LEN
    local_heads = w_qkv.shape[2] // HEAD_DIM
    inputs_wide = inputs.astype(jnp.float32)
    normed_one, scaled_one, inverse_one = norm_forward(inputs_wide, gain_one, shift_one)
    gathered = lax.all_gather(normed_one.astype(jnp.bfloat16), "mp", axis=0, tiled=True)
    projected = jnp.einsum(
        "td,dcf->tcf", gathered, w_qkv, preferred_element_type=jnp.float32
    ).astype(jnp.bfloat16)
    packed = projected.reshape(seq_count, LEN, 3, local_heads, HEAD_DIM)
    mixture, log_total = lax.map(attend_forward, packed)
    attended = mixture.reshape(group_rows, local_heads * HEAD_DIM)
    branch = lax.psum_scatter(
        jnp.dot(attended, w_proj, preferred_element_type=jnp.float32),
        "mp",
        scatter_dimension=0,
        tiled=True,
    )
    hidden = inputs_wide + branch
    normed_two, scaled_two, inverse_two = norm_forward(hidden, gain_two, shift_two)
    normed_two_low = normed_two.astype(jnp.bfloat16)
    logits = jnp.dot(normed_two_low, w_router, preferred_element_type=jnp.float32)
    group_routes = routes[:, 0]
    own_routes = lax.dynamic_slice_in_dim(group_routes, mp_index * tok_rows, tok_rows, 0)
    expert_ids = jnp.arange(experts_all, dtype=jnp.int32)
    picked = own_routes[:, None] == expert_ids[None, :]
    gate_value = jax.nn.sigmoid(jnp.sum(jnp.where(picked, logits, 0.0), axis=1))
    own_slots = own_routes * capacity + shard_ranks(own_routes[None, :], expert_ids)[0]
    send_rows = (
        jnp.zeros((experts_all * capacity, model_width), jnp.bfloat16)
        .at[own_slots]
        .set(normed_two_low)
    )
    expert_rows = to_experts(send_rows.reshape(experts_all, 1, capacity, model_width))
    full_in, full_out = (
        lax.all_gather(w_in[0], "mp", axis=1, tiled=True),
        lax.all_gather(w_out[0], "mp", axis=0, tiled=True),
    )
    flat_rows = expert_rows.reshape(-1, model_width)
    pre_act = jnp.dot(flat_rows, full_in, preferred_element_type=jnp.float32)
    activity = jax.nn.gelu(pre_act, approximate=True).astype(jnp.bfloat16)
    expert_part = jnp.dot(activity, full_out, preferred_element_type=jnp.float32).reshape(
        expert_rows.shape
    )
    came_back = from_experts(expert_part)
    returned = jnp.take(
        came_back.reshape(experts_all * capacity, model_width), own_slots, axis=0
    ).astype(jnp.float32)
    output = hidden + gate_value[:, None] * returned
    seq_ids = jnp.arange(seq_count, dtype=jnp.int32)
    domain_ids = jnp.arange(domain_weights.shape[0], dtype=jnp.int32)
    same_domain = domains[:, None] == domain_ids[None, :]
    seq_weight = jnp.sum(jnp.where(same_domain, domain_weights[None, :], 0.0), axis=1)
    seq_counts = jnp.sum(jnp.where(same_domain, domain_counts[None, :], 0), axis=1).astype(
        jnp.float32
    )
    factor = keep_mask.astype(jnp.float32) * seq_weight * count_scale / seq_counts
    row_seq = (mp_index * tok_rows + jnp.arange(tok_rows, dtype=jnp.int32)) // LEN
    row_factor = jnp.sum(
        jnp.where(row_seq[:, None] == seq_ids[None, :], factor[None, :], 0.0), axis=1
    )
    d_output = cotangent.astype(jnp.float32) * row_factor[:, None]
    d_returned = (gate_value[:, None] * d_output).astype(jnp.bfloat16)
    d_gate = jnp.sum(d_output * returned, axis=1) * gate_value * (1.0 - gate_value)
    d_logits = jnp.where(picked, d_gate[:, None], 0.0).astype(jnp.bfloat16)
    grad_router = jnp.einsum(
        "td,te->de", normed_two_low, d_logits, preferred_element_type=jnp.float32
    )
    d_norm_router = jnp.einsum("te,de->td", d_logits, w_router, preferred_element_type=jnp.float32)
    d_send = (
        jnp.zeros((experts_all * capacity, model_width), jnp.bfloat16).at[own_slots].set(d_returned)
    )
    d_expert_rows = to_experts(d_send.reshape(experts_all, 1, capacity, model_width))
    d_flat = d_expert_rows.reshape(-1, model_width)
    d_activity = jnp.einsum("rd,fd->rf", d_flat, full_out, preferred_element_type=jnp.float32)
    grad_w_out = jnp.einsum("rf,rd->fd", activity, d_flat, preferred_element_type=jnp.float32)
    gelu_pull = jax.vjp(lambda pre_vals: jax.nn.gelu(pre_vals, approximate=True), pre_act)[1]
    d_pre = gelu_pull(d_activity)[0].astype(jnp.bfloat16)
    grad_w_in = jnp.einsum("rd,rf->df", flat_rows, d_pre, preferred_element_type=jnp.float32)
    d_rows_part = jnp.einsum(
        "rf,df->rd", d_pre, full_in, preferred_element_type=jnp.float32
    ).reshape(expert_rows.shape)
    came_grad = from_experts(d_rows_part)
    d_norm_expert = jnp.take(
        came_grad.reshape(experts_all * capacity, model_width), own_slots, axis=0
    ).astype(jnp.float32)
    grad_w_in, grad_w_out = (
        lax.psum_scatter(
            grad_w_in.astype(jnp.bfloat16), "mp", scatter_dimension=1, tiled=True
        ).astype(jnp.float32),
        lax.psum_scatter(
            grad_w_out.astype(jnp.bfloat16), "mp", scatter_dimension=0, tiled=True
        ).astype(jnp.float32),
    )
    d_norm_two = d_norm_expert + d_norm_router
    d_back_two, grad_gain_two, grad_shift_two = norm_backward(
        d_norm_two, scaled_two, inverse_two, gain_two
    )
    d_hidden = d_output + d_back_two
    d_branch = lax.all_gather(d_hidden.astype(jnp.bfloat16), "mp", axis=0, tiled=True)
    grad_w_proj = jnp.einsum("tf,td->fd", attended, d_branch, preferred_element_type=jnp.float32)
    d_attended = jnp.einsum(
        "td,fd->tf", d_branch, w_proj, preferred_element_type=jnp.float32
    ).astype(jnp.bfloat16)
    d_packed = lax.map(
        attend_backward,
        (packed, d_attended.reshape(seq_count, LEN, local_heads, HEAD_DIM), log_total),
    )
    d_projected = d_packed.reshape(group_rows, 3, local_heads * HEAD_DIM)
    grad_w_qkv = jnp.einsum(
        "td,tcf->dcf", gathered, d_projected, preferred_element_type=jnp.float32
    )
    d_norm_one = lax.psum_scatter(
        jnp.einsum("tcf,dcf->td", d_projected, w_qkv, preferred_element_type=jnp.float32),
        "mp",
        scatter_dimension=0,
        tiled=True,
    )
    d_back_one, grad_gain_one, grad_shift_one = norm_backward(
        d_norm_one, scaled_one, inverse_one, gain_one
    )
    input_grad = d_hidden + d_back_one
    grad_w_qkv, grad_w_proj = lax.psum((grad_w_qkv, grad_w_proj), "dp")
    grad_gain_one, grad_shift_one, grad_gain_two, grad_shift_two, grad_router = lax.psum(
        (grad_gain_one, grad_shift_one, grad_gain_two, grad_shift_two, grad_router), ("dp", "mp")
    )
    return (
        output.astype(jnp.bfloat16),
        input_grad.astype(jnp.bfloat16),
        grad_gain_one,
        grad_shift_one,
        grad_w_qkv,
        grad_w_proj,
        grad_gain_two,
        grad_shift_two,
        grad_router,
        grad_w_in[None],
        grad_w_out[None],
    )


def solution(mesh):
    return jax.shard_map(
        shards,
        mesh=mesh,
        in_specs=(
            P(("dp", "mp"), None),
            P(("dp", "mp"), None),
            P("dp", None),
            P("dp"),
            P(),
            P(),
            P("dp"),
            P(),
            P(),
            P(None, None, "mp"),
            P("mp", None),
            P(),
            P(),
            P(),
            P("dp", None, "mp"),
            P("dp", "mp", None),
        ),
        out_specs=(
            P(("dp", "mp"), None),
            P(("dp", "mp"), None),
            P(),
            P(),
            P(None, None, "mp"),
            P("mp", None),
            P(),
            P(),
            P(),
            P("dp", None, "mp"),
            P("dp", "mp", None),
        ),
        check_vma=False,
    )
```

profile of v0, /device:TPU:12, one launch (start us, length us, event | category | flops | bytes accessed | tf_op | source)
XLA Modules:
  0.0 766.5 jit_solution(17716853276737096383)
XLA Ops:
  12.9 37.7 %all-gather.7.cloned.1.call-done = bf16[3072,768]{1,0:T(8,128)(2,1)} async-done(((bf16[768,768]{1,0:T(8,128)(2,1)}), bf16[3072,768]{1,0:T(8,128)(2,1)}) %all-gather.7.cloned.1.call-update) | async-done | bytes 4718608 | tf_op jit(solution)/shard_map/all_gather | solution.py:126
  57.8 10.5 %reshape.401 = bf16[3,1024,3,3,64]{1,0,4,3,2:T(4,128)(2,1)} reshape(bf16[3072,3,192]{0,2,1:T(8,128)(2,1)} %convert_element_type.121) | data formatting | bytes 7077888 | tf_op jit(solution)/shard_map/reshape | solution.py:130
  73.8 67.4 %while.22 = (s32[]{:T(128)}, bf16[3,1024,3,64]{1,3,2,0:T(8,128)(2,1)S(1)}, f32[3,3,1024,1]{2,1,3,0:T(4,128)}, bf16[3,1024,3,3,64]{1,4,3,2,0:T(8,128)(2,1)}, s32[]{:T(128)}) while((s32[]{:T(128)}, bf16[3,1024,3,64]{1,3,2,0:T(8,128)(2,1)S(1)}, f32[3,3,1024,1]{2,1,3,0:T(4,128)}, bf16[3,1024,3,3,64]{1,4,3,2,0:T(8,128)(2,1)}, s32[]{:T(128)}) %tuple.62), condition=%wide.region_5.6_spmd, body=%wide.region_2.5_spmd.sunk | while | flops 844297216 | bytes 45985872 | solution.py:131
  103.9 7.3 fusion.140
  152.5 75.1 %reduce-scatter.5.cloned.1.call-done = f32[768,768]{1,0:T(8,128)} async-done(((f32[3072,768]{1,0:T(8,128)}), f32[768,768]{1,0:T(8,128)}) %reduce-scatter.5.cloned.1.call-update) | async-done | bytes 2359312 | tf_op jit(solution)/shard_map/reduce_scatter | solution.py:133
  230.6 7.5 scatter_custom_fusion
  247.1 8.0 %scatter_custom_fusion.1 = bf16[960,768]{1,0:T(8,128)(2,1)} fusion(s32[768]{0:T(1024)S(1)} %fusion.93, bf16[768,768]{1,0:T(8,128)(2,1)} %param.23, f32[768]{0:T(1024)S(1)} %select_reduce_fusion, f32[768]{0:T(1024)S(1)} %add_divide_fusion, bf16[]{:T(256)} %constant.67.clone.1), kind=kCustom, calls=%fused_computation.112 | custom fusion | flops 2359296 | bytes 2662402 | tf_op jit(solution)/shard_map/scatter | solution.py:191
  255.1 21.4 %all-to-all-done = bf16[8,1,120,768]{3,2,1,0:T(8,128)(2,1)} async-done(((bf16[8,1,120,768]{3,2,1,0:T(8,128)(2,1)}), bf16[8,1,120,768]{3,2,1,0:T(8,128)(2,1)}, u32[]{:S(2)}, u32[]{:S(2)}) %all-to-all-start) | async-done | bytes 1474592 | tf_op jit(solution)/shard_map/all_to_all | solution.py:88
  283.2 11.9 %fusion.46 = f32[960,3072]{1,0:T(8,128)} fusion(bf16[960,768]{1,0:T(8,128)(2,1)} %bitcast.29, bf16[1,768,3072]{2,1,0:T(8,128)(2,1)} %all-gather.11.cloned.1.call-done), kind=kOutput, calls=%fused_computation.72 | convolution fusion | flops 4529848320 | bytes 17989632 | tf_op jit(solution)/shard_map/dot_general | solution.py:160
  295.1 10.4 %all-gather.13.cloned.1.call-done = bf16[1,3072,768]{2,1,0:T(8,128)(2,1)} async-done(((bf16[1,768,768]{2,1,0:T(8,128)(2,1)}), bf16[1,3072,768]{2,1,0:T(8,128)(2,1)}) %all-gather.13.cloned.1.call-update) | async-done | bytes 4718608 | tf_op jit(solution)/shard_map/all_gather | solution.py:157
  305.5 12.0 %fusion.72 = bf16[960,768]{1,0:T(8,128)(2,1)} fusion(bf16[1,3072,768]{2,1,0:T(8,128)(2,1)} %all-gather.13.cloned.1.call-done, f32[960,3072]{1,0:T(8,128)} %fusion.46), kind=kOutput, calls=%fused_computation.111 | convolution fusion | flops 4557127680 | bytes 17989632 | tf_op jit(solution)/shard_map/dot_general | solution.py:162
  325.1 14.5 %fusion.39 = bf16[960,3072]{1,0:T(8,128)(2,1)S(1)} fusion(f32[960,3072]{1,0:T(8,128)} %fusion.46, bf16[960,768]{1,0:T(8,128)(2,1)} %bitcast.211, bf16[1,3072,768]{2,1,0:T(8,128)(2,1)} %all-gather.13.cloned.1.call-done), kind=kOutput, calls=%fused_computation.61 | convolution fusion | flops 4588830720 | bytes 23887872 | tf_op jit(solution)/shard_map/rd,fd->rf/dot_general | solution.py:195
  342.1 8.3 %fusion.69 = bf16[960,768]{1,0:T(8,128)(2,1)} fusion(bf16[960,3072]{1,0:T(8,128)(2,1)S(1)} %fusion.39, bf16[1,768,3072]{2,1,0:T(8,128)(2,1)} %all-gather.11.cloned.1.call-done), kind=kOutput, calls=%fused_computation.110 | convolution fusion | flops 4530585600 | bytes 12091392 | tf_op jit(solution)/shard_map/rf,df->rd/dot_general | solution.py:200
  350.4 7.4 all-to-all-done.1
  371.6 24.1 %all-to-all-done.3 = bf16[8,1,120,768]{3,2,1,0:T(8,128)(2,1)} async-done(((bf16[8,1,120,768]{3,2,1,0:T(8,128)(2,1)}), bf16[8,1,120,768]{3,2,1,0:T(8,128)(2,1)}, u32[]{:S(2)}, u32[]{:S(2)}) %all-to-all-start.3) | async-done | bytes 1474592 | tf_op jit(solution)/shard_map/all_to_all | solution.py:93
  408.6 12.0 %convolution_convert_fusion = bf16[3072,768]{1,0:T(8,128)(2,1)} fusion(bf16[960,768]{1,0:T(8,128)(2,1)} %bitcast.212, f32[960,3072]{1,0:T(8,128)} %fusion.46), kind=kOutput, calls=%fused_computation.64 | convolution fusion | flops 4558749696 | bytes 17989632 | tf_op jit(solution)/shard_map/rf,rd->fd/dot_general | solution.py:196
  420.7 9.1 %convolution_convert_fusion.1 = bf16[768,3072]{1,0:T(8,128)(2,1)} fusion(bf16[960,768]{1,0:T(8,128)(2,1)} %bitcast.29, bf16[960,3072]{1,0:T(8,128)(2,1)} %copy-done.44), kind=kOutput, calls=%fused_computation.65 | convolution fusion | flops 4532207616 | bytes 12091392 | tf_op jit(solution)/shard_map/rd,rf->df/dot_general | solution.py:199
  429.9 17.3 %all-gather.9.cloned.1.call-done = bf16[3072,768]{1,0:T(8,128)(2,1)} async-done(((bf16[768,768]{1,0:T(8,128)(2,1)}), bf16[3072,768]{1,0:T(8,128)(2,1)}) %all-gather.9.cloned.1.call-update) | async-done | bytes 4718608 | tf_op jit(solution)/shard_map/all_gather | solution.py:220
  456.1 80.3 %while.23 = (s32[]{:T(128)}, bf16[3,1024,3,3,64]{1,4,3,2,0:T(8,128)(2,1)}, bf16[3,1024,3,3,64]{1,4,3,2,0:T(8,128)(2,1)}, f32[3,3,1024,1]{2,1,3,0:T(4,128)}, bf16[3,1024,3,64]{1,3,2,0:T(8,128)(2,1)S(1)}, /*index=5*/s32[]{:T(128)}) while((s32[]{:T(128)}, bf16[3,1024,3,3,64]{1,4,3,2,0:T(8,128)(2,1)}, bf16[3,1024,3,3,64]{1,4,3,2,0:T(8,128)(2,1)}, ...), condition=%wide.region_23.25_spmd, body=%wide.region_21.24_spmd.sunk | while | flops 2066019328 | bytes 107311192 | solution.py:225
  543.7 10.4 %reshape.415 = bf16[3072,3,192]{0,2,1:T(8,128)(2,1)} reshape(bf16[3,1024,3,3,64]{1,0,4,3,2:T(4,128)(2,1)} %copy.72) | data formatting | bytes 7077888 | tf_op jit(solution)/shard_map/reshape | solution.py:229
  554.2 8.3 %convolution_bitcast_fusion = f32[3072,768]{1,0:T(8,128)} fusion(bf16[3072,3,192]{0,2,1:T(8,128)(2,1)} %reshape.415, bf16[768,3,192]{0,2,1:T(8,128)(2,1)S(1)} %copy-done), kind=kOutput, calls=%fused_computation.63 | convolution fusion | flops 2717908992 | bytes 13860864 | tf_op jit(solution)/shard_map/tcf,dcf->td/dot_general | solution.py:234
  583.9 57.5 %reduce-scatter.7.cloned.1.call-done = f32[768,768]{1,0:T(8,128)} async-done(((f32[3072,768]{1,0:T(8,128)}), f32[768,768]{1,0:T(8,128)}) %reduce-scatter.7.cloned.1.call-update) | async-done | bytes 2359312 | tf_op jit(solution)/shard_map/reduce_scatter | solution.py:233
  644.2 45.9 %all-reduce = (f32[768]{0:T(1024)}, f32[768]{0:T(1024)}, f32[768]{0:T(1024)}, f32[768]{0:T(1024)}, f32[768,8]{0,1:T(8,128)}) all-reduce(f32[768]{0:T(1024)S(1)} %get-tuple-element.103, f32[768]{0:T(1024)S(1)} %get-tuple-element.108, f32[768]{0:T(1024)S(1)} %copy-done.37, ...), channel_id=1, replica_groups=mesh['dp'=8,'mp'=4] {'dp','mp'}, use_global_device_ids=true, to_apply=%region_28.30 | all-reduce | flops 9216 | bytes 73728 | tf_op jit(solution)/shard_map/psum | solution.py:244
  693.8 62.1 %all-reduce.4.cloned.1.call-done = (f32[768,3,192]{0,2,1:T(8,128)}, f32[192,768]{1,0:T(8,128)}) async-done(((f32[768,3,192]{0,2,1:T(8,128)}, f32[192,768]{1,0:T(8,128)}), (f32[768,3,192]{0,2,1:T(8,128)}, f32[192,768]{1,0:T(8,128)})) %all-reduce.4.cloned.1.call-update) | async-done | bytes 2359312 | tf_op jit(solution)/shard_map/psum | solution.py:243
  (230 shorter events, 271.9 us)
Async XLA Ops:
  7.2 43.5 %copy-start = (bf16[768,3,192]{0,2,1:T(8,128)(2,1)S(1)}, bf16[768,3,192]{0,2,1:T(8,128)(2,1)}, u32[]{:S(2)}) copy-start(bf16[768,3,192]{0,2,1:T(8,128)(2,1)} %param.31) | copy-start | bytes 2654212
  7.2 43.4 %all-gather.7.cloned.1.call-start = ((), (), s32[]{:S(2)}) async-start(), calls=%async_computation.8 | async-start | bytes 5898240 | tf_op jit(solution)/shard_map/all_gather | solution.py:126
  12.8 214.7 %reduce-scatter.5.cloned.1.call-start = ((), (), s32[]{:S(2)}) async-start(), calls=%async_computation.9 | async-start | bytes 11796480 | tf_op jit(solution)/shard_map/reduce_scatter | solution.py:133
  149.0 134.2 %all-gather.11.cloned.1.call-start = ((), (), s32[]{:S(2)}) async-start(), calls=%async_computation.14 | async-start | bytes 5898240 | tf_op jit(solution)/shard_map/all_gather | solution.py:156
  149.7 155.8 %all-gather.13.cloned.1.call-start = ((), (), s32[]{:S(2)}) async-start(), calls=%async_computation.15 | async-start | bytes 5898240 | tf_op jit(solution)/shard_map/all_gather | solution.py:157
  150.3 251.2 %copy-start.16 = (s32[768]{0:T(1024)}, s32[768]{0:T(1024)S(1)}, u32[]{:S(2)}) copy-start(s32[768]{0:T(1024)S(1)} %dynamic-slice_reduce_fusion) | copy-start | bytes 9220
  238.1 38.4 %all-to-all-start = ((bf16[8,1,120,768]{3,2,1,0:T(8,128)(2,1)}), bf16[8,1,120,768]{3,2,1,0:T(8,128)(2,1)}, u32[]{:S(2)}, u32[]{:S(2)}) async-start(bf16[8,1,120,768]{3,2,1,0:T(8,128)(2,1)} %bitcast.208), calls=%async_computation.1 | async-start | bytes 2949120 | tf_op jit(solution)/shard_map/all_to_all | solution.py:88
  247.0 29.5 %copy-start.26 = (f32[768]{0:T(1024)}, f32[768]{0:T(1024)S(1)}, u32[]{:S(2)}) copy-start(f32[768]{0:T(1024)S(1)} %fusion.78) | copy-start | bytes 9220
  247.1 29.5 %copy-start.22 = (f32[768]{0:T(1024)}, f32[768]{0:T(1024)S(1)}, u32[]{:S(2)}) copy-start(f32[768]{0:T(1024)S(1)} %add_divide_fusion) | copy-start | bytes 9220
  276.5 40.9 %all-to-all-start.2 = ((bf16[8,1,120,768]{3,2,1,0:T(8,128)(2,1)}), bf16[8,1,120,768]{3,2,1,0:T(8,128)(2,1)S(1)}, u32[]{:S(2)}, u32[]{:S(2)}) async-start(bf16[8,1,120,768]{3,2,1,0:T(8,128)(2,1)} %bitcast.35), calls=%async_computation.3 | async-start | bytes 2949120 | tf_op jit(solution)/shard_map/all_to_all | solution.py:88
  318.6 39.3 %all-to-all-start.1 = ((bf16[8,1,120,768]{3,2,1,0:T(8,128)(2,1)}), bf16[8,1,120,768]{3,2,1,0:T(8,128)(2,1)S(1)}, u32[]{:S(2)}, u32[]{:S(2)}) async-start(bf16[8,1,120,768]{3,2,1,0:T(8,128)(2,1)} %bitcast.214), calls=%async_computation.2 | async-start | bytes 2949120 | tf_op jit(solution)/shard_map/all_to_all | solution.py:93
  357.9 37.8 %all-to-all-start.3 = ((bf16[8,1,120,768]{3,2,1,0:T(8,128)(2,1)}), bf16[8,1,120,768]{3,2,1,0:T(8,128)(2,1)}, u32[]{:S(2)}, u32[]{:S(2)}) async-start(bf16[8,1,120,768]{3,2,1,0:T(8,128)(2,1)} %bitcast.213), calls=%async_computation.4 | async-start | bytes 2949120 | tf_op jit(solution)/shard_map/all_to_all | solution.py:93
  364.5 82.8 %all-gather.9.cloned.1.call-start = ((), (), s32[]{:S(2)}) async-start(), calls=%async_computation.10 | async-start | bytes 5898240 | tf_op jit(solution)/shard_map/all_gather | solution.py:220
  368.6 27.1 %copy-start.7 = (bf16[768,768]{1,0:T(8,128)(2,1)}, bf16[768,768]{1,0:T(8,128)(2,1)S(1)}, u32[]{:S(2)}) copy-start(bf16[768,768]{1,0:T(8,128)(2,1)S(1)} %gather_fusion) | copy-start | bytes 3538948
  408.6 169.2 %reduce-scatter.11.cloned.1.call-start = ((), (), s32[]{:S(2)}) async-start(), calls=%async_computation.13 | async-start | bytes 5898240 | tf_op jit(solution)/shard_map/reduce_scatter | solution.py:211
  420.6 160.3 %reduce-scatter.9.cloned.1.call-start = ((), (), s32[]{:S(2)}) async-start(), calls=%async_computation.12 | async-start | bytes 5898240 | tf_op jit(solution)/shard_map/reduce_scatter | solution.py:208
  429.9 211.6 %reduce-scatter.7.cloned.1.call-start = ((), (), s32[]{:S(2)}) async-start(), calls=%async_computation.11 | async-start | bytes 11796480 | tf_op jit(solution)/shard_map/reduce_scatter | solution.py:233
  562.5 193.3 %all-reduce.4.cloned.1.call-start = ((), (), s32[]{:S(2)}) async-start(), calls=%async_computation.16 | async-start | bytes 4718592 | tf_op jit(solution)/shard_map/psum | solution.py:243
  580.9 60.6 %copy-start.4 = (bf16[768,768]{1,0:T(8,128)(2,1)S(1)}, bf16[768,768]{1,0:T(8,128)(2,1)}, u32[]{:S(2)}) copy-start(bf16[768,768]{1,0:T(8,128)(2,1)} %param.22) | copy-start | bytes 3538948
  580.9 60.6 %copy-start.19 = (f32[768]{0:T(1024)S(1)}, f32[768]{0:T(1024)}, u32[]{:S(2)}) copy-start(f32[768]{0:T(1024)} %copy-done.18) | copy-start | bytes 9220
  580.9 60.6 %copy-start.21 = (f32[768]{0:T(1024)S(1)}, f32[768]{0:T(1024)}, u32[]{:S(2)}) copy-start(f32[768]{0:T(1024)} %copy-done.20) | copy-start | bytes 9220
  580.9 60.6 %copy-start.29 = (f32[768]{0:T(1024)S(1)}, f32[768]{0:T(1024)}, u32[]{:S(2)}) copy-start(f32[768]{0:T(1024)} %param.29) | copy-start | bytes 9220
  583.9 60.3 %copy-start.37 = (f32[768]{0:T(1024)S(1)}, f32[768]{0:T(1024)}, u32[]{:S(2)}) copy-start(f32[768]{0:T(1024)} %get-tuple-element.101) | copy-start | bytes 9220
  583.9 60.3 %copy-start.38 = (f32[768]{0:T(1024)S(1)}, f32[768]{0:T(1024)}, u32[]{:S(2)}) copy-start(f32[768]{0:T(1024)} %get-tuple-element.107) | copy-start | bytes 9220
  (36 other events, 160.6 us)
Sparse Core Ops, SparseCore 0:
  13.0 37.6 all-gather.6
  149.1 78.4 reduce-scatter.4
  229.1 37.4 all-gather.10
  268.0 37.4 all-gather.12
  408.7 38.5 all-gather.8
  449.6 47.8 reduce-scatter.10
  500.2 47.8 reduce-scatter.8
  562.6 78.7 reduce-scatter.6
  645.6 110.1 all-reduce.3
where the time goes:
time: 779 us; the launch traced here: 767 us
  waiting for transfers between devices  314 us (40%)
  matrix products  189 us (24%)
  other arithmetic  98.2 us (13%)
  local copies, waits for them, and re-layouts  76.6 us (10%)
  blocking collectives  45.9 us (6%)
  starting transfers between devices  26.5 us (3%)
  between operations  15 us (2%)
    reduce_scatter x1, waiting for transfers between devices, shards(): lax.psum_scatter(jnp.dot(attended, w_proj, preferred_element_type=jnp.flo...  75.1 us
    psum x1, waiting for transfers between devices, shards(): grad_w_qkv, grad_w_proj = lax.psum((grad_w_qkv, grad_w_proj), 'dp')  62.1 us
    reduce_scatter x1, waiting for transfers between devices, shards(): lax.psum_scatter(jnp.einsum('tcf,dcf->td', d_projected, w_qkv, preferred_...  57.5 us
    psum x1, blocking collectives, shards(): lax.psum((grad_gain_one, grad_shift_one, grad_gain_two, grad_shift_two, g...  45.9 us
    all_gather x1, waiting for transfers between devices, shards(): lax.all_gather(normed_one.astype(jnp.bfloat16), 'mp', axis=0, tiled=True)  37.7 us
    all_to_all x2, waiting for transfers between devices, from_experts(): lax.all_to_all(expert_result.astype(jnp.bfloat16), 'dp', split_axis=0, co...  31.5 us
    dot_general x6, matrix products, causal_scores(): jnp.einsum('qhd,khd->hqk', queries, keys_all, preferred_element_type=jnp....  23.4 us
    reduce_sum x3, other arithmetic, attend_forward(): totals = jnp.sum(expo_vals, axis=-1, keepdims=True)  21.9 us
  transfers between devices with their start and end apart: 13, of which 9 were waited for; matrix products, arithmetic and copies ran while one was open for 31% of the time, Pallas kernels for 0%

commit v1 on v0

v1 whole, which is shorter than its diff:
```python
import jax
import jax.numpy as jnp
from jax import lax
from jax.experimental import pallas as pl
from jax.experimental.pallas import tpu as pltpu
from jax.sharding import PartitionSpec as P

HEAD_DIM = 64
LEN = 1024
BLOCK = 256
HALF = LEN // 2

norm_epsilon = 1e-05
count_scale = 10.0
masked_score = -1e30

f32 = jnp.float32
bf16 = jnp.bfloat16
NT = (((1,), (1,)), ((), ()))
NN = (((1,), (0,)), ((), ()))
TN = (((0,), (0,)), ((), ()))

ACROSS = [(0, 2), (2, 0), (1, 3), (3, 1)]
BESIDE = [(0, 1), (1, 0), (2, 3), (3, 2)]
LATER = [(0, 2), (1, 3)]
EARLIER = [(2, 0), (3, 1)]


def dot(left, right, dims=NN):
    return lax.dot_general(left, right, dims, preferred_element_type=f32)


def norm_forward(features, gain_vec, shift_vec):
    centre = features - jnp.mean(features, axis=-1, keepdims=True)
    inverse = lax.rsqrt(jnp.mean(centre * centre, axis=-1, keepdims=True) + norm_epsilon)
    scaled = centre * inverse
    return (scaled * gain_vec + shift_vec, scaled, inverse)


def norm_backward(d_normed, scaled, inverse, gain_vec):
    d_scaled = d_normed * gain_vec
    correction = jnp.mean(d_scaled, axis=-1, keepdims=True) + scaled * jnp.mean(
        d_scaled * scaled, axis=-1, keepdims=True
    )
    return (
        inverse * (d_scaled - correction),
        jnp.sum(d_normed * scaled, axis=0),
        jnp.sum(d_normed, axis=0),
    )


def plan(chip, run):
    second = chip == 1
    for whole, (here, there) in enumerate([(0, 2), (1, 3), (2, 0), (3, 1)]):
        run(pl.multiple_of(jnp.where(second, there, here) * BLOCK, BLOCK), whole)

    @pl.when(chip == 0)
    def _():
        run(4 * BLOCK, 0)
        run(5 * BLOCK, 1)

    @pl.when(chip == 1)
    def _():
        run(4 * BLOCK, 2)
        run(5 * BLOCK, 3)


def mask_diagonal(scores, whole):
    first = lax.broadcasted_iota(jnp.int32, (BLOCK, BLOCK), 0)
    second = lax.broadcasted_iota(jnp.int32, (BLOCK, BLOCK), 1)
    last = jnp.where(first <= second, scores[whole * BLOCK :], masked_score)
    if not whole:
        return last
    return jnp.concatenate([scores[: whole * BLOCK], last], axis=0)


def attend_kernel(chip_ref, q_ref, k_ref, v_ref, ke_ref, ve_ref, o_ref, l_ref, keys, values):
    chip = chip_ref[0]
    lane = lax.broadcasted_iota(jnp.int32, (1, 128), 1)
    row = lax.broadcasted_iota(jnp.int32, (128, 1), 0)
    keys[0:HALF] = ke_ref[...]
    keys[HALF:] = k_ref[...]
    values[:, 0:HALF] = ve_ref[...].T
    values[:, HALF:] = v_ref[...].T

    def run(first, whole):
        span = (whole + 1) * BLOCK
        start = pl.multiple_of(first + HALF - whole * BLOCK, BLOCK)
        queries = q_ref[pl.ds(first, BLOCK)] * bf16(0.125)
        near = keys[pl.ds(start, span)]
        mixed = values[:, pl.ds(start, span)]
        parts = []
        for head in range(2):
            own = jnp.where((lane // HEAD_DIM) == head, queries, bf16(0))
            scores = mask_diagonal(dot(near, own, NT), whole)
            largest = jnp.max(scores, axis=0, keepdims=True)
            expo = jnp.exp(scores - largest)
            total = jnp.sum(expo, axis=0, keepdims=True)
            parts.append(dot(mixed, expo.astype(bf16)) / total)
            l_ref[head : head + 1, pl.ds(first, BLOCK)] = largest + jnp.log(total)
        joined = jnp.where(row < HEAD_DIM, parts[0], parts[1])
        o_ref[pl.ds(first, BLOCK)] = joined.T.astype(bf16)

    plan(chip, run)


def column_block(rows, offset):
    return pl.BlockSpec((rows, 128), lambda pair: (0, offset + pair))


def attend(chip, qkv, ext):
    rows = qkv.shape[0]
    pairs = qkv.shape[1] // 384
    return pl.pallas_call(
        attend_kernel,
        grid=(pairs,),
        in_specs=[
            pl.BlockSpec(memory_space=pltpu.SMEM),
            column_block(rows, 0),
            column_block(rows, pairs),
            column_block(rows, 2 * pairs),
            column_block(HALF, 0),
            column_block(HALF, pairs),
        ],
        out_specs=[
            column_block(rows, 0),
            pl.BlockSpec((None, 8, rows), lambda pair: (pair, 0, 0)),
        ],
        out_shape=[
            jax.ShapeDtypeStruct((rows, pairs * 128), bf16),
            jax.ShapeDtypeStruct((pairs, 8, rows), f32),
        ],
        scratch_shapes=[
            pltpu.VMEM((HALF + rows, 128), bf16),
            pltpu.VMEM((128, HALF + rows), bf16),
        ],
        compiler_params=pltpu.CompilerParams(vmem_limit_bytes=48 * 2**20),
        cost_estimate=pl.CostEstimate(flops=16 * 10**9, bytes_accessed=8 * 10**6, transcendentals=8 * 10**6),
        name="attend",
    )(chip, qkv, qkv, qkv, ext, ext)


def attend_back_kernel(
    chip_ref, q_ref, k_ref, v_ref, ke_ref, ve_ref, d_ref, o_ref, l_ref,
    dq_ref, dk_ref, dv_ref, dke_ref, dve_ref, keys, values, d_keys, d_values,
):
    chip = chip_ref[0]
    lane = lax.broadcasted_iota(jnp.int32, (1, 128), 1)
    keys[0:HALF] = ke_ref[...]
    keys[HALF:] = k_ref[...]
    values[0:HALF] = ve_ref[...]
    values[HALF:] = v_ref[...]
    d_keys[...] = jnp.zeros_like(d_keys)
    d_values[...] = jnp.zeros_like(d_values)

    def run(first, whole):
        span = (whole + 1) * BLOCK
        start = pl.multiple_of(first + HALF - whole * BLOCK, BLOCK)
        queries = q_ref[pl.ds(first, BLOCK)] * bf16(0.125)
        d_mixed = d_ref[pl.ds(first, BLOCK)]
        near = keys[pl.ds(start, span)]
        near_values = values[pl.ds(start, span)]
        product = (d_mixed.astype(f32) * o_ref[pl.ds(first, BLOCK)].astype(f32)).T
        dq = dk = dv = 0.0
        for head in range(2):
            here = (lane // HEAD_DIM) == head
            own = jnp.where(here, queries, bf16(0))
            d_own = jnp.where(here, d_mixed, bf16(0))
            delta = jnp.sum(product[HEAD_DIM * head : HEAD_DIM * (head + 1)], axis=0, keepdims=True)
            scores = mask_diagonal(dot(near, own, NT), whole)
            probs = jnp.exp(scores - l_ref[head : head + 1, pl.ds(first, BLOCK)])
            d_probs = dot(near_values, d_own, NT)
            d_scores = (probs * (d_probs - delta)).astype(bf16)
            dv = dv + dot(probs.astype(bf16), d_own)
            dk = dk + dot(d_scores, own)
            dq = dq + dot(d_scores, jnp.where(here, near, bf16(0)), TN)
        dq_ref[pl.ds(first, BLOCK)] = (dq * 0.125).astype(bf16)
        d_keys[pl.ds(start, span)] += dk
        d_values[pl.ds(start, span)] += dv

    plan(chip, run)
    dk_ref[...] = d_keys[HALF:]
    dv_ref[...] = d_values[HALF:]
    dke_ref[...] = d_keys[:HALF].astype(bf16)
    dve_ref[...] = d_values[:HALF].astype(bf16)


def attend_back(chip, qkv, ext, d_mixed, mixed, log_total):
    rows = qkv.shape[0]
    pairs = qkv.shape[1] // 384
    return pl.pallas_call(
        attend_back_kernel,
        grid=(pairs,),
        in_specs=[
            pl.BlockSpec(memory_space=pltpu.SMEM),
            column_block(rows, 0),
            column_block(rows, pairs),
            column_block(rows, 2 * pairs),
            column_block(HALF, 0),
            column_block(HALF, pairs),
            column_block(rows, 0),
            column_block(rows, 0),
            pl.BlockSpec((None, 8, rows), lambda pair: (pair, 0, 0)),
        ],
        out_specs=[column_block(rows, 0)] * 3 + [column_block(HALF, 0)] * 2,
        out_shape=[
            jax.ShapeDtypeStruct((rows, pairs * 128), bf16),
            jax.ShapeDtypeStruct((rows, pairs * 128), f32),
            jax.ShapeDtypeStruct((rows, pairs * 128), f32),
            jax.ShapeDtypeStruct((HALF, pairs * 128), bf16),
            jax.ShapeDtypeStruct((HALF, pairs * 128), bf16),
        ],
        scratch_shapes=[
            pltpu.VMEM((HALF + rows, 128), bf16),
            pltpu.VMEM((HALF + rows, 128), bf16),
            pltpu.VMEM((HALF + rows, 128), f32),
            pltpu.VMEM((HALF + rows, 128), f32),
        ],
        compiler_params=pltpu.CompilerParams(vmem_limit_bytes=56 * 2**20),
        cost_estimate=pl.CostEstimate(flops=20 * 10**9, bytes_accessed=12 * 10**6, transcendentals=8 * 10**6),
        name="attend_back",
    )(chip, qkv, qkv, qkv, ext, ext, d_mixed, mixed, log_total)


def across(value):
    return lax.ppermute(value, "mp", ACROSS)


def beside(value):
    return lax.ppermute(value, "mp", BESIDE)


def in_order(first, own, other):
    return jnp.where(first, own, other), jnp.where(first, other, own)


def exchange(rows):
    return lax.all_to_all(rows, "dp", split_axis=0, concat_axis=0, tiled=True)


def gelu_parts(pre):
    scale = 0.7978845608028654
    inner = jnp.tanh(scale * (pre + 0.044715 * pre * pre * pre))
    value = 0.5 * pre * (1.0 + inner)
    slope = 0.5 * (1.0 + inner) + 0.5 * pre * (1.0 - inner * inner) * scale * (
        1.0 + 3.0 * 0.044715 * pre * pre
    )
    return value, slope


def shards(
    inputs, cotangent, routes, domains, domain_counts, domain_weights, keep_mask, gain_one, shift_one,
    w_qkv, w_proj, gain_two, shift_two, w_router, w_in, w_out,
):
    tok, width = inputs.shape
    experts = w_router.shape[1]
    cap = max(2, tok * 5 // (4 * experts))
    slots = (cap + 16) // 16 * 16
    mp_index = lax.axis_index("mp")
    chip, core = mp_index // 2, mp_index % 2
    on_first_chip, on_first_core = chip == 0, core == 0
    expert = lax.axis_index("dp")
    seq_count = routes.shape[0] // LEN

    own_routes = lax.dynamic_slice_in_dim(routes[:, 0], mp_index * tok, tok, 0)
    expert_ids = jnp.arange(experts, dtype=jnp.int32)
    picked = own_routes[:, None] == expert_ids[None, :]
    places = jnp.arange(tok, dtype=jnp.int32)
    earlier = (places[:, None] > places[None, :]).astype(bf16)
    counts = dot(earlier, picked.astype(bf16))
    rank = jnp.sum(jnp.where(picked, counts, 0.0), axis=1).astype(jnp.int32)
    own_slots = own_routes * slots + rank
    slot_ids = jnp.arange(experts * slots, dtype=jnp.int32)
    placed = own_slots[None, :] == slot_ids[:, None]
    placing = placed.astype(bf16)

    seq_ids = jnp.arange(seq_count, dtype=jnp.int32)
    domain_ids = jnp.arange(domain_weights.shape[0], dtype=jnp.int32)
    same_domain = domains[:, None] == domain_ids[None, :]
    seq_weight = jnp.sum(jnp.where(same_domain, domain_weights[None, :], 0.0), axis=1)
    seq_counts = jnp.sum(jnp.where(same_domain, domain_counts[None, :], 0), axis=1).astype(f32)
    factor = keep_mask.astype(f32) * seq_weight * count_scale / seq_counts
    row_seq = (mp_index * tok + places) // LEN
    row_factor = jnp.sum(jnp.where(row_seq[:, None] == seq_ids[None, :], factor[None, :], 0.0), axis=1)
    slot_factor = jnp.sum(jnp.where(placed, row_factor[None, :], 0.0), axis=1).reshape(experts, slots)
    high = slot_factor.astype(bf16)
    low = (slot_factor - high.astype(f32)).astype(bf16)
    cot_rows = dot(placing, cotangent).astype(bf16).reshape(experts, slots, width)
    cot_rows = cot_rows.at[:, cap, :slots].set(high).at[:, cap, width // 2 : width // 2 + slots].set(low)
    cot_rows = exchange(cot_rows)

    inputs_wide = inputs.astype(f32)
    normed_one, scaled_one, inverse_one = norm_forward(inputs_wide, gain_one, shift_one)
    normed_one = normed_one.astype(bf16)
    normed_chip = jnp.concatenate(in_order(on_first_core, normed_one, beside(normed_one)))
    w_own = jnp.transpose(w_qkv, (1, 2, 0))
    features = 2 * w_own.shape[1]
    w_heads = jnp.concatenate(in_order(on_first_chip, w_own, across(w_own)), axis=1)
    w_heads = w_heads.reshape(3 * features, width)
    qkv = dot(normed_chip, w_heads, NT).astype(bf16)
    ext = lax.ppermute(qkv[-HALF:, features:], "mp", LATER)
    chip_scalar = chip.astype(jnp.int32).reshape(1)
    mixed, log_total = attend(chip_scalar, qkv, ext)

    proj_own = jnp.concatenate(in_order(on_first_chip, w_proj, across(w_proj)))
    proj_other = beside(proj_own)
    mixed_own = lax.dynamic_slice_in_dim(mixed, core * tok, tok, 0)
    mixed_other = beside(lax.dynamic_slice_in_dim(mixed, (1 - core) * tok, tok, 0))
    hidden = inputs_wide + dot(mixed_own, proj_own) + dot(mixed_other, proj_other)
    normed_two, scaled_two, inverse_two = norm_forward(hidden, gain_two, shift_two)
    normed_two = normed_two.astype(bf16)
    expert_in = exchange(dot(placing, normed_two).astype(bf16).reshape(experts, slots, width))
    expert_in = expert_in.reshape(experts * slots, width)

    in_across, out_across = across(w_in[0]), across(w_out[0])
    weights_in = [w_in[0], in_across, beside(w_in[0]), beside(in_across)]
    weights_out = [w_out[0], out_across, beside(w_out[0]), beside(out_across)]

    cot_factor = cot_rows[:, cap, :slots].astype(f32) + cot_rows[
        :, cap, width // 2 : width // 2 + slots
    ].astype(f32)
    cot_factor = jnp.where(jnp.arange(slots)[None, :] < cap, cot_factor, 0.0).reshape(-1, 1)
    d_result = cot_rows.reshape(experts * slots, width).astype(f32) * cot_factor
    router_row = lax.dynamic_slice_in_dim(w_router.T, expert, 1, 0).astype(f32)
    gate = jax.nn.sigmoid(jnp.sum(expert_in.astype(f32) * router_row, axis=1, keepdims=True))
    d_out = (gate * d_result).astype(bf16)
    parts = [gelu_parts(dot(expert_in, w)) for w in weights_in]
    acts = [value.astype(bf16) for value, _ in parts]
    result = sum(dot(act, w) for act, w in zip(acts, weights_out))
    d_pres = [
        (dot(d_out, w, NT) * slope).astype(bf16) for (_, slope), w in zip(parts, weights_out)
    ]
    d_gate = jnp.sum(d_result * result, axis=1, keepdims=True)
    d_logit = (d_gate * gate * (1.0 - gate)).astype(bf16).astype(f32)
    d_expert_in = sum(dot(d_pre, w, NT) for d_pre, w in zip(d_pres, weights_in)) + d_logit * router_row
    returned = exchange((gate * result).astype(bf16).reshape(experts, slots, width))
    d_returned = exchange(d_expert_in.astype(bf16).reshape(experts, slots, width))
    grads_in = [dot(expert_in, d_pre, TN) for d_pre in d_pres]
    grads_out = [dot(act, d_out, TN) for act in acts]
    router_grad = jnp.sum(expert_in.astype(f32) * d_logit, axis=0)

    def collect(grads):
        here = grads[0] + beside(grads[2].astype(bf16)).astype(f32)
        there = grads[1] + beside(grads[3].astype(bf16)).astype(f32)
        return here + across(there.astype(bf16)).astype(f32)

    grad_w_in, grad_w_out = collect(grads_in), collect(grads_out)

    output = hidden + dot(placing, returned.reshape(experts * slots, width), TN)
    d_output = cotangent.astype(f32) * row_factor[:, None]
    d_norm_two = dot(placing, d_returned.reshape(experts * slots, width), TN)
    d_back_two, grad_gain_two, grad_shift_two = norm_backward(
        d_norm_two, scaled_two, inverse_two, gain_two
    )
    d_hidden = d_output + d_back_two

    d_branch = d_hidden.astype(bf16)
    d_branch = jnp.concatenate(in_order(on_first_core, d_branch, beside(d_branch)))
    grad_proj = dot(mixed, d_branch, TN)
    d_mixed = dot(d_branch, proj_own, NT).astype(bf16)
    dq, dk, dv, dk_ext, dv_ext = attend_back(chip_scalar, qkv, ext, d_mixed, mixed, log_total)
    ext_back = lax.ppermute(jnp.concatenate([dk_ext, dv_ext], axis=1), "mp", EARLIER).astype(f32)
    d_kv = jnp.concatenate([dk, dv], axis=1)
    d_kv = jnp.concatenate([d_kv[:-HALF], d_kv[-HALF:] + ext_back])
    d_qkv = jnp.concatenate([dq, d_kv.astype(bf16)], axis=1)
    grad_heads = dot(d_qkv, normed_chip, TN).reshape(3, features, width)
    d_norm_chip = dot(d_qkv, w_heads)
    d_norm_own = lax.dynamic_slice_in_dim(d_norm_chip, core * tok, tok, 0)
    d_norm_other = lax.dynamic_slice_in_dim(d_norm_chip, (1 - core) * tok, tok, 0).astype(bf16)
    d_norm_one = d_norm_own + beside(d_norm_other).astype(f32)
    d_back_one, grad_gain_one, grad_shift_one = norm_backward(
        d_norm_one, scaled_one, inverse_one, gain_one
    )
    input_grad = d_hidden + d_back_one

    def own_and_other(grads, axis):
        first, second = jnp.split(grads, 2, axis=axis)
        return in_order(on_first_chip, first, second)

    heads_own, heads_other = own_and_other(grad_heads, 1)
    proj_grad_own, proj_grad_other = own_and_other(grad_proj, 0)
    heads_sum = heads_own + across(heads_other.astype(bf16)).astype(f32)
    proj_sum = proj_grad_own + across(proj_grad_other.astype(bf16)).astype(f32)
    sums = jnp.concatenate([heads_sum.reshape(-1, width), proj_sum]).astype(bf16)
    groups = experts
    pieces = exchange(sums.reshape(groups, -1, width))
    piece = jnp.sum(pieces.astype(f32), axis=0).astype(bf16)
    sums = lax.all_gather(piece, "dp", axis=0, tiled=True).astype(f32)
    grad_w_qkv = jnp.transpose(sums[: -w_proj.shape[0]].reshape(w_own.shape), (2, 0, 1))
    grad_w_proj = sums[-w_proj.shape[0] :]
    own_expert = (expert_ids == expert)[:, None]
    small = jnp.concatenate(
        [
            jnp.stack([grad_gain_one, grad_shift_one, grad_gain_two, grad_shift_two]),
            jnp.where(own_expert, router_grad[None, :], 0.0),
        ]
    )
    small = lax.psum(small, ("dp", "mp"))
    return (
        output.astype(bf16),
        input_grad.astype(bf16),
        small[0],
        small[1],
        grad_w_qkv,
        grad_w_proj,
        small[2],
        small[3],
        small[4:].T,
        grad_w_in[None],
        grad_w_out[None],
    )


def solution(mesh):
    tokens, group = P(("dp", "mp"), None), P("dp")
    return jax.shard_map(
        shards,
        mesh=mesh,
        in_specs=(
            tokens, tokens, P("dp", None), group, P(), P(), group, P(), P(),
            P(None, None, "mp"), P("mp", None), P(), P(), P(),
            P("dp", None, "mp"), P("dp", "mp", None),
        ),
        out_specs=(
            tokens, tokens, P(), P(), P(None, None, "mp"), P("mp", None), P(), P(), P(),
            P("dp", None, "mp"), P("dp", "mp", None),
        ),
        check_vma=False,
    )
```

time: 779 us -> 528 us (0.68)
  waiting for transfers between devices: 314 us -> 182 us
  matrix products: 189 us -> 115 us
  other arithmetic: 98.2 us -> 37 us
  Pallas kernels: 0 us -> 43.7 us
  local copies, waits for them, and re-layouts: 76.6 us -> 37 us
  starting transfers between devices: 26.5 us -> 47 us
    ppermute x0 -> x23, waiting for transfers between devices: none -> 138 us  [the longest x8 120 us: across(): return lax.ppermute(value, 'mp', ACROSS)]
    reduce_scatter x4 -> x0, waiting for transfers between devices: 133 us -> none  [the longest x1 75.1 us: shards(): lax.psum_scatter(jnp.dot(attended, w_proj, preferred_element_type=jnp.flo...]
    all_gather x4 -> x1, waiting for transfers between devices: 65.5 us -> 0.01 us  [shards(): sums = lax.all_gather(piece, 'dp', axis=0, tiled=True).astype(f32)]
    dot_general x34 -> x36, matrix products: 180 us -> 115 us  [dot(): return lax.dot_general(left, right, dims, preferred_element_type=f32)]
    psum x1 -> x0, waiting for transfers between devices: 62.1 us -> none  [shards(): grad_w_qkv, grad_w_proj = lax.psum((grad_w_qkv, grad_w_proj), 'dp')]
    pallas_call x0 -> x2, Pallas kernels: none -> 43.7 us  [the longest x1 23 us: attend_back(): pl.pallas_call(attend_back_kernel, grid=(pairs,), in_specs=[pl.BlockSpec(...]
    reshape x3 -> x0, local copies, waits for them, and re-layouts: 24 us -> none  [the longest x1 10.5 us: shards(): packed = projected.reshape(seq_count, LEN, 3, local_heads, HEAD_DIM)]
    convert_element_type x8 -> x11, other arithmetic: 32.1 us -> 8.61 us  [the longest x1 2.84 us: shards(): input_grad.astype(bf16)]
  transfers between devices with their start and end apart: 13 -> 29, of which waited for: 9 -> 11; matrix products, arithmetic and copies ran while one was open for 31% -> 24% of each run, Pallas kernels for 0% -> 8%
where the time goes in v1:
time: 528 us; the launch traced here: 520 us
  waiting for transfers between devices  182 us (34%)
  matrix products  115 us (22%)
  starting transfers between devices  47 us (9%)
  Pallas kernels  43.7 us (8%)
  blocking collectives  41.6 us (8%)
  local copies, waits for them, and re-layouts  37 us (7%)
  other arithmetic  37 us (7%)
  between operations  16.1 us (3%)
    ppermute x8, waiting for transfers between devices, across(): return lax.ppermute(value, 'mp', ACROSS)  120 us
    dot_general x36, matrix products, dot(): return lax.dot_general(left, right, dims, preferred_element_type=f32)  115 us
    all_to_all x5, waiting for transfers between devices, exchange(): return lax.all_to_all(rows, 'dp', split_axis=0, concat_axis=0, tiled=True)  43.4 us
    psum x1, blocking collectives, shards(): small = lax.psum(small, ('dp', 'mp'))  41.6 us
    all_to_all x5, starting transfers between devices, exchange(): return lax.all_to_all(rows, 'dp', split_axis=0, concat_axis=0, tiled=True)  33.3 us
    pallas_call x1, Pallas kernels, attend_back(): pl.pallas_call(attend_back_kernel, grid=(pairs,), in_specs=[pl.BlockSpec(...  23 us
    unnamed x191, local copies, waits for them, and re-layouts  21.2 us
    pallas_call x1, Pallas kernels, attend(): pl.pallas_call(attend_kernel, grid=(pairs,), in_specs=[pl.BlockSpec(memor...  20.6 us
  transfers between devices with their start and end apart: 29, of which 11 were waited for; matrix products, arithmetic and copies ran while one was open for 24% of the time, Pallas kernels for 8%

profile of v1, /device:TPU:12, one launch (start us, length us, event | category | flops | bytes accessed | tf_op | source)
XLA Modules:
  0.0 519.6 jit_solution(5169194856980033225)
XLA Ops:
  20.8 9.4 %collective-permute-done.1 = bf16[3,192,768]{2,1,0:T(8,128)(2,1)} collective-permute-done((bf16[3,192,768]{2,1,0:T(8,128)(2,1)}, bf16[3,192,768]{2,1,0:T(8,128)(2,1)}, u32[]{:S(2)}, u32[]{:S(2)}) %collective-permute-start.1) | collective-permute-done | bytes 884768 | tf_op jit(solution)/shard_map/ppermute | solution.py:226
  43.3 6.8 %all-to-all-start.2 = ((bf16[8,128,768]{2,1,0:T(8,128)(2,1)}), bf16[8,128,768]{2,1,0:T(8,128)(2,1)}, u32[]{:S(2)}, u32[]{:S(2)}) async-start(bf16[8,128,768]{2,1,0:T(8,128)(2,1)} %scatter.9), calls=%async_computation.2 | async-start | bytes 3145728 | tf_op jit(solution)/shard_map/all_to_all | solution.py:238
  52.2 5.6 %collective-permute-done.2.ke_ref.ve_ref = bf16[512,768]{1,0:T(8,128)(2,1)S(1)} collective-permute-done((bf16[512,768]{1,0:T(8,128)(2,1)S(1)}, bf16[512,768]{1,0:T(8,128)(2,1)S(1)}, u32[]{:S(2)}, u32[]{:S(2)}) %collective-permute-start.2) | collective-permute-done | bytes 786464 | tf_op jit(solution)/shard_map/ppermute | solution.py:301
  60.1 20.6 %attend.1 = (bf16[1536,384]{1,0:T(8,128)(2,1)S(1)}, f32[3,8,1536]{2,1,0:T(8,128)S(1)}) custom-call(s32[1]{0:T(128)} %bitcast.chip_ref, bf16[1536,1152]{1,0:T(8,128)(2,1)S(1)} %copy-done.5, bf16[1536,1152]{1,0:T(8,128)(2,1)S(1)} %copy-done.5, bf16[1536,1152]{1,0:T(8,128)(2,1)S(1)} %copy-done.5, bf16[512,768]{1,0:T(8,128)(2,1)S(1)} %collective-permute-done.2.ke_ref.ve_ref, ...), custom_call_target="tpu_custom_call" | custom-call | flops 16000000000 | bytes 8000000 | tf_op jit(solution)/shard_map/attend/pallas_call | solution.py:114
  90.9 6.5 %all-to-all-start = ((bf16[8,128,768]{2,1,0:T(8,128)(2,1)}), bf16[8,128,768]{2,1,0:T(8,128)(2,1)S(1)}, u32[]{:S(2)}, u32[]{:S(2)}) async-start(bf16[8,128,768]{2,1,0:T(8,128)(2,1)} %bitcast.3), calls=%async_computation | async-start | bytes 3145728 | tf_op jit(solution)/shard_map/all_to_all | solution.py:238
  100.7 25.9 %collective-permute-done.6 = bf16[768,768]{1,0:T(8,128)(2,1)} collective-permute-done((bf16[768,768]{1,0:T(8,128)(2,1)}, bf16[768,768]{1,0:T(8,128)(2,1)}, u32[]{:S(2)}, u32[]{:S(2)}) %collective-permute-start.6) | collective-permute-done | bytes 1179680 | tf_op jit(solution)/shard_map/ppermute | solution.py:226
  126.6 23.8 %collective-permute-done.7 = bf16[768,768]{1,0:T(8,128)(2,1)} collective-permute-done((bf16[768,768]{1,0:T(8,128)(2,1)}, bf16[768,768]{1,0:T(8,128)(2,1)}, u32[]{:S(2)}, u32[]{:S(2)}) %collective-permute-start.7) | collective-permute-done | bytes 1179680 | tf_op jit(solution)/shard_map/ppermute | solution.py:226
  174.0 5.5 %multiply_reduce_fusion = (f32[1024]{0:T(1024)S(1)}, bf16[1024,768]{1,0:T(8,128)(2,1)}, bf16[1024,768]{1,0:T(8,128)(2,1)S(1)}) fusion(bf16[8,128,768]{2,1,0:T(8,128)(2,1)} %all-to-all-done.2, f32[1024]{0:T(1024)S(1)} %bitcast_select_fusion, f32[1024]{0:T(1024)S(1)} %fusion.92, bf16[768,768]{1,0:T(8,128)(2,1)} %collective-permute-done.11, ...), kind=kOutput, calls=%fused_computation.48 | convolution fusion | flops 1223687168 | bytes 18493440 | tf_op jit(solution)/shard_map/dot_general | solution.py:30
  189.4 4.1 fusion.29
  193.6 4.7 fusion.19
  198.3 4.7 fusion.24
  211.8 6.6 %all-to-all-start.3 = ((bf16[8,128,768]{2,1,0:T(8,128)(2,1)}), bf16[8,128,768]{2,1,0:T(8,128)(2,1)S(1)}, u32[]{:S(2)}, u32[]{:S(2)}) async-start(bf16[8,128,768]{2,1,0:T(8,128)(2,1)} %bitcast.17), calls=%async_computation.3 | async-start | bytes 3145728 | tf_op jit(solution)/shard_map/all_to_all | solution.py:238
  219.9 33.6 %all-to-all-done.3 = bf16[8,128,768]{2,1,0:T(8,128)(2,1)S(1)} async-done(((bf16[8,128,768]{2,1,0:T(8,128)(2,1)}), bf16[8,128,768]{2,1,0:T(8,128)(2,1)S(1)}, u32[]{:S(2)}, u32[]{:S(2)}) %all-to-all-start.3) | async-done | bytes 1572896 | tf_op jit(solution)/shard_map/all_to_all | solution.py:238
  272.5 23.0 %attend_back.1 = (bf16[1536,384]{1,0:T(8,128)(2,1)}, f32[1536,384]{1,0:T(8,128)}, f32[1536,384]{1,0:T(8,128)}, bf16[512,384]{1,0:T(8,128)(2,1)}, bf16[512,384]{1,0:T(8,128)(2,1)}) custom-call(s32[1]{0:T(128)} %bitcast.chip_ref, bf16[1536,1152]{1,0:T(8,128)(2,1)} %copy-done.4, bf16[1536,1152]{1,0:T(8,128)(2,1)} %copy-done.4, bf16[1536,1152]{1,0:T(8,128)(2,1)} %copy-done.4, ...), custom_call_target="tpu_custom_call" | custom-call | flops 20000000000 | bytes 12000000 | tf_op jit(solution)/shard_map/attend_back/pallas_call | solution.py:191
  303.3 12.0 %collective-permute-done.13 = bf16[512,768]{1,0:T(8,128)(2,1)S(1)} collective-permute-done((bf16[512,768]{1,0:T(8,128)(2,1)S(1)}, bf16[512,768]{1,0:T(8,128)(2,1)S(1)}, u32[]{:S(2)}, u32[]{:S(2)}) %collective-permute-start.13) | collective-permute-done | bytes 786464 | tf_op jit(solution)/shard_map/ppermute | solution.py:362
  324.0 23.0 %collective-permute-done.16 = bf16[192,768]{1,0:T(8,128)(2,1)S(1)} collective-permute-done((bf16[192,768]{1,0:T(8,128)(2,1)S(1)}, bf16[192,768]{1,0:T(8,128)(2,1)S(1)}, u32[]{:S(2)}, u32[]{:S(2)}) %collective-permute-start.16) | collective-permute-done | bytes 294944 | tf_op jit(solution)/shard_map/ppermute | solution.py:226
  348.5 6.4 %all-to-all-start.4 = ((bf16[8,96,768]{2,1,0:T(8,128)(2,1)}), bf16[8,96,768]{2,1,0:T(8,128)(2,1)S(1)}, u32[]{:S(2)}, u32[]{:S(2)}) async-start(bf16[8,96,768]{2,1,0:T(8,128)(2,1)} %bitcast.111), calls=%async_computation.4 | async-start | bytes 2359296 | tf_op jit(solution)/shard_map/all_to_all | solution.py:238
  354.9 5.4 %convolution_convert_fusion.3 = bf16[768,768]{1,0:T(8,128)(2,1)} fusion(bf16[1024,768]{1,0:T(8,128)(2,1)} %copy-done.78, f32[1024,768]{1,0:T(8,128)} %copy-done.84), kind=kOutput, calls=%fused_computation.112 | convolution fusion | flops 1215627264 | bytes 5898240 | tf_op jit(solution)/shard_map/dot_general | solution.py:30
  370.0 9.8 %all-to-all-done.4 = bf16[8,96,768]{2,1,0:T(8,128)(2,1)S(1)} async-done(((bf16[8,96,768]{2,1,0:T(8,128)(2,1)}), bf16[8,96,768]{2,1,0:T(8,128)(2,1)S(1)}, u32[]{:S(2)}, u32[]{:S(2)}) %all-to-all-start.4) | async-done | bytes 1179680 | tf_op jit(solution)/shard_map/all_to_all | solution.py:238
  379.8 7.1 %all-to-all-start.1 = ((bf16[8,128,768]{2,1,0:T(8,128)(2,1)}), bf16[8,128,768]{2,1,0:T(8,128)(2,1)}, u32[]{:S(2)}, u32[]{:S(2)}) async-start(bf16[8,128,768]{2,1,0:T(8,128)(2,1)} %bitcast.116), calls=%async_computation.1 | async-start | bytes 3145728 | tf_op jit(solution)/shard_map/all_to_all | solution.py:238
  387.2 4.7 add_convert_fusion.1
  402.5 18.5 %collective-permute-done.22 = bf16[768,768]{1,0:T(8,128)(2,1)S(1)} collective-permute-done((bf16[768,768]{1,0:T(8,128)(2,1)S(1)}, bf16[768,768]{1,0:T(8,128)(2,1)S(1)}, u32[]{:S(2)}, u32[]{:S(2)}) %collective-permute-start.22) | collective-permute-done | bytes 1179680 | tf_op jit(solution)/shard_map/ppermute | solution.py:226
  424.0 19.8 %collective-permute-done.19 = bf16[768,768]{1,0:T(8,128)(2,1)S(1)} collective-permute-done((bf16[768,768]{1,0:T(8,128)(2,1)S(1)}, bf16[768,768]{1,0:T(8,128)(2,1)S(1)}, u32[]{:S(2)}, u32[]{:S(2)}) %collective-permute-start.19) | collective-permute-done | bytes 1179680 | tf_op jit(solution)/shard_map/ppermute | solution.py:226
  465.9 41.6 %psum.7 = f32[12,768]{1,0:T(8,128)S(1)} all-reduce(f32[12,768]{1,0:T(8,128)S(1)} %concatenate.46), channel_id=1, replica_groups=mesh['dp'=8,'mp'=4] {'dp','mp'}, use_global_device_ids=true, to_apply=%region_20.21 | all-reduce | flops 9216 | bytes 73728 | tf_op jit(solution)/shard_map/psum | solution.py:398
  (336 shorter events, 174.5 us)
Async XLA Ops:
  7.2 22.9 %collective-permute-start.1 = (bf16[3,192,768]{2,1,0:T(8,128)(2,1)}, bf16[3,192,768]{2,1,0:T(8,128)(2,1)}, u32[]{:S(2)}, u32[]{:S(2)}) collective-permute-start(bf16[3,192,768]{2,1,0:T(8,128)(2,1)} %bitcast.119), channel_id=1, source_target_pairs={{0,2},{2,0},{1,3},{3,1},{4,6},{6,4},{5,7},{7,5},{8,10},{10,8},{9,1... | collective-permute-start | bytes 2654216 | tf_op jit(solution)/shard_map/ppermute | solution.py:226
  12.1 38.1 %collective-permute-start.3 = (bf16[192,768]{1,0:T(8,128)(2,1)}, bf16[192,768]{1,0:T(8,128)(2,1)}, u32[]{:S(2)}, u32[]{:S(2)}) collective-permute-start(bf16[192,768]{1,0:T(8,128)(2,1)} %param.30), channel_id=1, source_target_pairs={{0,2},{2,0},{1,3},{3,1},{4,6},{6,4},{5,7},{7,5},{8,10},{10,8},{9,1... | collective-permute-start | bytes 884744 | tf_op jit(solution)/shard_map/ppermute | solution.py:226
  43.3 47.6 %all-to-all-start.2 = ((bf16[8,128,768]{2,1,0:T(8,128)(2,1)}), bf16[8,128,768]{2,1,0:T(8,128)(2,1)}, u32[]{:S(2)}, u32[]{:S(2)}) async-start(bf16[8,128,768]{2,1,0:T(8,128)(2,1)} %scatter.9), calls=%async_computation.2 | async-start | bytes 3145728 | tf_op jit(solution)/shard_map/all_to_all | solution.py:238
  52.2 32.0 %collective-permute-start.5 = (bf16[384,768]{1,0:T(8,128)(2,1)}, bf16[384,768]{1,0:T(8,128)(2,1)}, u32[]{:S(2)}, u32[]{:S(2)}) collective-permute-start(bf16[384,768]{1,0:T(8,128)(2,1)} %pad_maximum_fusion.9), channel_id=1, source_target_pairs={{0,1},{1,0},{2,3},{3,2},{4,5},{5,4},{6,7},{7,6},{8,9},{9,8},{10,11... | collective-permute-start | bytes 1769480 | tf_op jit(solution)/shard_map/ppermute | solution.py:230
  90.9 60.4 %all-to-all-start = ((bf16[8,128,768]{2,1,0:T(8,128)(2,1)}), bf16[8,128,768]{2,1,0:T(8,128)(2,1)S(1)}, u32[]{:S(2)}, u32[]{:S(2)}) async-start(bf16[8,128,768]{2,1,0:T(8,128)(2,1)} %bitcast.3), calls=%async_computation | async-start | bytes 3145728 | tf_op jit(solution)/shard_map/all_to_all | solution.py:238
  97.3 29.3 %collective-permute-start.6 = (bf16[768,768]{1,0:T(8,128)(2,1)}, bf16[768,768]{1,0:T(8,128)(2,1)}, u32[]{:S(2)}, u32[]{:S(2)}) collective-permute-start(bf16[768,768]{1,0:T(8,128)(2,1)} %bitcast.6), channel_id=1, source_target_pairs={{0,2},{2,0},{1,3},{3,1},{4,6},{6,4},{5,7},{7,5},{8,10},{10,8},{9,1... | collective-permute-start | bytes 3538952 | tf_op jit(solution)/shard_map/ppermute | solution.py:226
  97.4 53.0 %collective-permute-start.7 = (bf16[768,768]{1,0:T(8,128)(2,1)}, bf16[768,768]{1,0:T(8,128)(2,1)}, u32[]{:S(2)}, u32[]{:S(2)}) collective-permute-start(bf16[768,768]{1,0:T(8,128)(2,1)} %bitcast.7), channel_id=1, source_target_pairs={{0,2},{2,0},{1,3},{3,1},{4,6},{6,4},{5,7},{7,5},{8,10},{10,8},{9,1... | collective-permute-start | bytes 3538952 | tf_op jit(solution)/shard_map/ppermute | solution.py:226
  99.4 58.6 %collective-permute-start.8 = (bf16[768,768]{1,0:T(8,128)(2,1)}, bf16[768,768]{1,0:T(8,128)(2,1)}, u32[]{:S(2)}, u32[]{:S(2)}) collective-permute-start(bf16[768,768]{1,0:T(8,128)(2,1)} %bitcast.6), channel_id=1, source_target_pairs={{0,1},{1,0},{2,3},{3,2},{4,5},{5,4},{6,7},{7,6},{8,9},{9,8},{10,11... | collective-permute-start | bytes 3538952 | tf_op jit(solution)/shard_map/ppermute | solution.py:230
  99.4 71.3 %collective-permute-start.9 = (bf16[768,768]{1,0:T(8,128)(2,1)}, bf16[768,768]{1,0:T(8,128)(2,1)}, u32[]{:S(2)}, u32[]{:S(2)}) collective-permute-start(bf16[768,768]{1,0:T(8,128)(2,1)} %bitcast.7), channel_id=1, source_target_pairs={{0,1},{1,0},{2,3},{3,2},{4,5},{5,4},{6,7},{7,6},{8,9},{9,8},{10,11... | collective-permute-start | bytes 3538952 | tf_op jit(solution)/shard_map/ppermute | solution.py:230
  126.6 35.0 %collective-permute-start.10 = (bf16[768,768]{1,0:T(8,128)(2,1)}, bf16[768,768]{1,0:T(8,128)(2,1)S(1)}, u32[]{:S(2)}, u32[]{:S(2)}) collective-permute-start(bf16[768,768]{1,0:T(8,128)(2,1)} %collective-permute-done.6), channel_id=1, source_target_pairs={{0,1},{1,0},{2,3},{3,2},{4,5},{5,4},{6,7},{7,6},{8,9},{9,8},{10,11... | collective-permute-start | bytes 3538952 | tf_op jit(solution)/shard_map/ppermute | solution.py:230
  150.5 23.5 %collective-permute-start.11 = (bf16[768,768]{1,0:T(8,128)(2,1)}, bf16[768,768]{1,0:T(8,128)(2,1)}, u32[]{:S(2)}, u32[]{:S(2)}) collective-permute-start(bf16[768,768]{1,0:T(8,128)(2,1)} %collective-permute-done.7), channel_id=1, source_target_pairs={{0,1},{1,0},{2,3},{3,2},{4,5},{5,4},{6,7},{7,6},{8,9},{9,8},{10,11... | collective-permute-start | bytes 3538952 | tf_op jit(solution)/shard_map/ppermute | solution.py:230
  211.8 41.7 %all-to-all-start.3 = ((bf16[8,128,768]{2,1,0:T(8,128)(2,1)}), bf16[8,128,768]{2,1,0:T(8,128)(2,1)S(1)}, u32[]{:S(2)}, u32[]{:S(2)}) async-start(bf16[8,128,768]{2,1,0:T(8,128)(2,1)} %bitcast.17), calls=%async_computation.3 | async-start | bytes 3145728 | tf_op jit(solution)/shard_map/all_to_all | solution.py:238
  269.0 118.2 %collective-permute-start.21 = (bf16[768,768]{1,0:T(8,128)(2,1)}, bf16[768,768]{1,0:T(8,128)(2,1)}, u32[]{:S(2)}, u32[]{:S(2)}) collective-permute-start(bf16[768,768]{1,0:T(8,128)(2,1)} %convolution_convert_fusion.2), channel_id=1, source_target_pairs={{0,1},{1,0},{2,3},{3,2},{4,5},{5,4},{6,7},{7,6},{8,9},{9,8},{10,11... | collective-permute-start | bytes 3538952 | tf_op jit(solution)/shard_map/ppermute | solution.py:230
  318.8 28.3 %collective-permute-start.15 = (bf16[3,192,768]{2,1,0:T(8,128)(2,1)S(1)}, bf16[3,192,768]{2,1,0:T(8,128)(2,1)S(1)}, u32[]{:S(2)}, u32[]{:S(2)}) collective-permute-start(bf16[3,192,768]{2,1,0:T(8,128)(2,1)S(1)} %select_convert_fusion), channel_id=1, source_target_pairs={{0,2},{2,0},{1,3},{3,1},{4,6},{6,4},{5,7},{7,5},{8,10},{10,8},{9,1... | collective-permute-start | bytes 2654216 | tf_op jit(solution)/shard_map/ppermute | solution.py:226
  321.4 25.6 %collective-permute-start.16 = (bf16[192,768]{1,0:T(8,128)(2,1)S(1)}, bf16[192,768]{1,0:T(8,128)(2,1)S(1)}, u32[]{:S(2)}, u32[]{:S(2)}) collective-permute-start(bf16[192,768]{1,0:T(8,128)(2,1)S(1)} %select_convert_fusion.1), channel_id=1, source_target_pairs={{0,2},{2,0},{1,3},{3,1},{4,6},{6,4},{5,7},{7,5},{8,10},{10,8},{9,1... | collective-permute-start | bytes 884744 | tf_op jit(solution)/shard_map/ppermute | solution.py:226
  348.5 31.3 %all-to-all-start.4 = ((bf16[8,96,768]{2,1,0:T(8,128)(2,1)}), bf16[8,96,768]{2,1,0:T(8,128)(2,1)S(1)}, u32[]{:S(2)}, u32[]{:S(2)}) async-start(bf16[8,96,768]{2,1,0:T(8,128)(2,1)} %bitcast.111), calls=%async_computation.4 | async-start | bytes 2359296 | tf_op jit(solution)/shard_map/all_to_all | solution.py:238
  362.9 39.6 %collective-permute-start.20 = (bf16[768,768]{1,0:T(8,128)(2,1)}, bf16[768,768]{1,0:T(8,128)(2,1)}, u32[]{:S(2)}, u32[]{:S(2)}) collective-permute-start(bf16[768,768]{1,0:T(8,128)(2,1)} %convolution_convert_fusion.3), channel_id=1, source_target_pairs={{0,1},{1,0},{2,3},{3,2},{4,5},{5,4},{6,7},{7,6},{8,9},{9,8},{10,11... | collective-permute-start | bytes 3538952 | tf_op jit(solution)/shard_map/ppermute | solution.py:230
  362.9 30.6 %collective-permute-start.18 = (bf16[768,768]{1,0:T(8,128)(2,1)}, bf16[768,768]{1,0:T(8,128)(2,1)}, u32[]{:S(2)}, u32[]{:S(2)}) collective-permute-start(bf16[768,768]{1,0:T(8,128)(2,1)} %convolution_convert_fusion.4), channel_id=1, source_target_pairs={{0,1},{1,0},{2,3},{3,2},{4,5},{5,4},{6,7},{7,6},{8,9},{9,8},{10,11... | collective-permute-start | bytes 3538952 | tf_op jit(solution)/shard_map/ppermute | solution.py:230
  363.4 60.6 %collective-permute-start.17 = (bf16[768,768]{1,0:T(8,128)(2,1)}, bf16[768,768]{1,0:T(8,128)(2,1)}, u32[]{:S(2)}, u32[]{:S(2)}) collective-permute-start(bf16[768,768]{1,0:T(8,128)(2,1)} %convolution_convert_fusion.5), channel_id=1, source_target_pairs={{0,1},{1,0},{2,3},{3,2},{4,5},{5,4},{6,7},{7,6},{8,9},{9,8},{10,11... | collective-permute-start | bytes 3538952 | tf_op jit(solution)/shard_map/ppermute | solution.py:230
  379.8 69.1 %all-to-all-start.1 = ((bf16[8,128,768]{2,1,0:T(8,128)(2,1)}), bf16[8,128,768]{2,1,0:T(8,128)(2,1)}, u32[]{:S(2)}, u32[]{:S(2)}) async-start(bf16[8,128,768]{2,1,0:T(8,128)(2,1)} %bitcast.116), calls=%async_computation.1 | async-start | bytes 3145728 | tf_op jit(solution)/shard_map/all_to_all | solution.py:238
  386.9 121.8 %all-gather.2.cloned.1.call-start = ((), (), s32[]{:S(2)}) async-start(), calls=%async_computation.5 | async-start | bytes 1327104 | tf_op jit(solution)/shard_map/all_gather | solution.py:388
  392.0 29.0 %collective-permute-start.22 = (bf16[768,768]{1,0:T(8,128)(2,1)S(1)}, bf16[768,768]{1,0:T(8,128)(2,1)S(1)}, u32[]{:S(2)}, u32[]{:S(2)}) collective-permute-start(bf16[768,768]{1,0:T(8,128)(2,1)S(1)} %add_convert_fusion.1), channel_id=1, source_target_pairs={{0,2},{2,0},{1,3},{3,1},{4,6},{6,4},{5,7},{7,5},{8,10},{10,8},{9,1... | collective-permute-start | bytes 3538952 | tf_op jit(solution)/shard_map/ppermute | solution.py:226
  396.3 47.6 %collective-permute-start.19 = (bf16[768,768]{1,0:T(8,128)(2,1)S(1)}, bf16[768,768]{1,0:T(8,128)(2,1)S(1)}, u32[]{:S(2)}, u32[]{:S(2)}) collective-permute-start(bf16[768,768]{1,0:T(8,128)(2,1)S(1)} %add_convert_fusion.2), channel_id=1, source_target_pairs={{0,2},{2,0},{1,3},{3,1},{4,6},{6,4},{5,7},{7,5},{8,10},{10,8},{9,1... | collective-permute-start | bytes 3538952 | tf_op jit(solution)/shard_map/ppermute | solution.py:226
  402.5 53.3 %collective-permute-start.14 = (bf16[768,768]{0,1:T(8,128)(2,1)}, bf16[768,768]{0,1:T(8,128)(2,1)}, u32[]{:S(2)}, u32[]{:S(2)}) collective-permute-start(bf16[768,768]{0,1:T(8,128)(2,1)} %dynamic-slice_convert_fusion), channel_id=1, source_target_pairs={{0,1},{1,0},{2,3},{3,2},{4,5},{5,4},{6,7},{7,6},{8,9},{9,8},{10,11... | collective-permute-start | bytes 3538952 | tf_op jit(solution)/shard_map/ppermute | solution.py:230
  (98 other events, 1115.3 us)
Sparse Core Ops, SparseCore 0:
  449.1 41.9 all-gather.1

commit v2 on v1

--- a/solution.py
+++ b/solution.py
@@ -1,3 +1,5 @@
+import functools
+
 import jax
 import jax.numpy as jnp
 from jax import lax
@@ -16,6 +18,7 @@
 
 f32 = jnp.float32
 bf16 = jnp.bfloat16
+MESH = pl.DeviceIdType.MESH
 NT = (((1,), (1,)), ((), ()))
 NN = (((1,), (0,)), ((), ()))
 TN = (((0,), (0,)), ((), ()))
@@ -240,12 +243,238 @@
 
 def gelu_parts(pre):
     scale = 0.7978845608028654
-    inner = jnp.tanh(scale * (pre + 0.044715 * pre * pre * pre))
-    value = 0.5 * pre * (1.0 + inner)
-    slope = 0.5 * (1.0 + inner) + 0.5 * pre * (1.0 - inner * inner) * scale * (
-        1.0 + 3.0 * 0.044715 * pre * pre
-    )
-    return value, slope
+    square = pre * pre
+    inner = jnp.tanh(pre * (scale + (scale * 0.044715) * square))
+    half = 0.5 * (1.0 + inner)
+    slope = half + (0.5 * pre) * (1.0 - inner * inner) * (scale + (3.0 * scale * 0.044715) * square)
+    return pre * half, slope
+
+STAGES = 4
+
+def expert_kernel(
+    experts, slots, steps,
+    rows_ref, cot_ref, factor_ref, router_ref, w_in_ref, w_out_ref, w_in_far_ref,
+    back_ref, result_ref, router_grad_ref, here_in_ref, here_out_ref, there_in_ref, there_out_ref,
+    x, wi, wo, d_out, act, d_pre, total, d_x, give, g_send, g_recv,
+    row_send, row_recv, back_send, back_recv, w_send, w_recv, g_send_sem, g_recv_sem, local_sem,
+):
+    me = lax.axis_index("dp")
+    mp = lax.axis_index("mp")
+    beside = {"mp": mp + 1 - 2 * (mp % 2)}
+    across = {"mp": (mp + 2) % 4}
+    members = experts // STAGES
+    span = members * slots
+    own_group, own_member = me // members, me % members
+
+    def group_of(stage):
+        return 2 * ((own_group // 2 + stage // 2) % 2) + (own_group % 2 + stage % 2) % 2
+
+    def chunk(index):
+        return pl.ds(pl.multiple_of(index * slots, 16), slots)
+
+    def group_rows(group):
+        return pl.ds(pl.multiple_of(group * span, 16), span)
+
+    barrier = pltpu.get_barrier_semaphore()
+
+    def greet(step, carry):
+        pl.semaphore_signal(barrier, inc=1, device_id={"dp": (me + step) % experts}, device_id_type=MESH)
+        return carry
+
+    lax.fori_loop(1, experts, greet, 0)
+    pl.semaphore_signal(barrier, inc=1, device_id=beside, device_id_type=MESH)
+    pl.semaphore_signal(barrier, inc=1, device_id=across, device_id_type=MESH)
+    pl.semaphore_wait(barrier, experts + 1)
+
+    def remote(src, dst, send, recv, device):
+        return pltpu.make_async_remote_copy(
+            src_ref=src, dst_ref=dst, send_sem=send, recv_sem=recv, device_id=device, device_id_type=MESH
+        )
+
+    def row_copy(target, source):
+        return remote(rows_ref.at[chunk(target)], x.at[chunk(source)], row_send.at[target], row_recv.at[source], {"dp": target})
+
+    def back_copy(target, source):
+        return remote(give.at[chunk(target)], back_ref.at[chunk(source)], back_send.at[target], back_recv.at[source], {"dp": target})
+
+    def partners(stage):
+        group = group_of(stage)
+        if stage == 0:
+            return [group * members + (own_member + k) % members for k in range(1, members)]
+        return [group * members + (own_member + k) % members for k in range(members)]
+
+    for stage in reversed(range(STAGES)):
+        for other in partners(stage):
+            row_copy(other, me).start()
+    own_rows = pltpu.make_async_copy(rows_ref.at[chunk(me)], x.at[chunk(me)], local_sem.at[0])
+    own_in = pltpu.make_async_copy(w_in_ref, wi.at[0], local_sem.at[1])
+    own_out = pltpu.make_async_copy(w_out_ref, wo.at[0], local_sem.at[2])
+    far_in = pltpu.make_async_copy(w_in_far_ref, wi.at[2], local_sem.at[3])
+    near_in = remote(w_in_ref, wi.at[1], w_send.at[0], w_recv.at[0], beside)
+    near_out = remote(w_out_ref, wo.at[1], w_send.at[1], w_recv.at[1], beside)
+    far_near_in = remote(w_in_far_ref, wi.at[3], w_send.at[2], w_recv.at[2], beside)
+    far_out = remote(w_out_ref, wo.at[2], w_send.at[3], w_recv.at[3], across)
+    far_near_out = remote(wo.at[2], wo.at[3], w_send.at[4], w_recv.at[4], beside)
+    for copy in (own_rows, own_in, own_out, near_in, near_out, far_in, far_out, far_near_in):
+        copy.start()
+    router_grad_ref[...] = jnp.zeros_like(router_grad_ref)
+
+    def prepare(stage, rows):
+        features = x[rows].astype(f32)
+        gate = jax.nn.sigmoid(jnp.sum(features * router_ref[...], axis=1, keepdims=True))
+        d_out[rows] = (gate * (cot_ref[rows].astype(f32) * factor_ref[rows])).astype(bf16)
+        total[rows] = jnp.zeros((span, x.shape[1]), f32)
+        d_x[rows] = jnp.zeros((span, x.shape[1]), f32)
+
+    def finish(stage, rows):
+        features = x[rows].astype(f32)
+        gate = jax.nn.sigmoid(jnp.sum(features * router_ref[...], axis=1, keepdims=True))
+        value = total[rows]
+        d_gate = jnp.sum(cot_ref[rows].astype(f32) * factor_ref[rows] * value, axis=1, keepdims=True)
+        d_logit = (d_gate * gate * (1.0 - gate)).astype(bf16).astype(f32)
+        give[rows] = (d_x[rows] + d_logit * router_ref[...]).astype(bf16)
+        result_ref[rows] = (gate * value).astype(bf16)
+        router_grad_ref[...] += jnp.sum(features * d_logit, axis=0, keepdims=True)
+
+    def stage_of(step):
+        return jnp.where(step < 6, step // 2, jnp.where(step < 12, (step - 6) // 2, 3))
+
+    def step_body(step, carry):
+        stage = stage_of(step)
+        part = jnp.where(step < 6, step % 2, jnp.where(step < 12, 2 + step % 2, step - 12))
+        rows = group_rows(group_of(stage))
+
+        for static, at in enumerate((0, 2, 4, 12)):
+            @pl.when(step == at)
+            def _():
+                if static == 0:
+                    own_rows.wait()
+                for other in partners(static):
+                    row_copy(me, other).wait_recv()
+        @pl.when((step == 0) | (step == 2) | (step == 4) | (step == 12))
+        def _():
+            prepare(stage, rows)
+
+        @pl.when(step == 0)
+        def _():
+            own_in.wait()
+            own_out.wait()
+
+        @pl.when(step == 1)
+        def _():
+            near_in.wait_recv()
+            near_out.wait_recv()
+
+        @pl.when(step == 6)
+        def _():
+            far_in.wait()
+            far_out.wait_recv()
+            far_near_out.start()
+
+        @pl.when(step == 7)
+        def _():
+            far_near_in.wait_recv()
+            far_near_out.wait_recv()
+
+        pre = dot(x[rows], wi[part])
+        value, slope = gelu_parts(pre)
+        value = value.astype(bf16)
+        act[part, rows] = value
+        total[rows] += dot(value, wo[part])
+        d_value = (dot(d_out[rows], wo[part], NT) * slope).astype(bf16)
+        d_pre[part, rows] = d_value
+        d_x[rows] += dot(d_value, wi[part], NT)
+
+        @pl.when((step == 7) | (step == 9) | (step == 11) | (step == 15))
+        def _():
+            finish(stage, rows)
+
+        for static, at in enumerate((7, 9, 11, 15)):
+            @pl.when(step == at)
+            def _():
+                for other in partners(static):
+                    back_copy(other, me).start()
+        return carry
+
+    lax.fori_loop(0, 16, step_body, 0)
+    own_back = pltpu.make_async_copy(give.at[chunk(me)], back_ref.at[chunk(me)], local_sem.at[4])
+    own_back.start()
+
+    def grad_copy(index):
+        return remote(outgoing[index], g_recv.at[index], g_send_sem.at[index], g_recv_sem.at[index], beside)
+
+    kept = pl.ds(0, x.shape[1])
+    outgoing = [g_send, act.at[3, kept], d_pre.at[3, kept], act.at[1, kept]]
+    for index, part in enumerate((3, 1)):
+        outgoing[2 * index][...] = dot(act[part], d_out[...], TN).astype(bf16)
+        grad_copy(2 * index).start()
+        outgoing[2 * index + 1][...] = dot(x[...], d_pre[part], TN).astype(bf16)
+        grad_copy(2 * index + 1).start()
+    grad = dot(act[2], d_out[...], TN)
+    grad_copy(0).wait_recv()
+    there_out_ref[...] = (grad + g_recv[0].astype(f32)).astype(bf16)
+    grad = dot(x[...], d_pre[2], TN)
+    grad_copy(1).wait_recv()
+    there_in_ref[...] = (grad + g_recv[1].astype(f32)).astype(bf16)
+    grad = dot(act[0], d_out[...], TN)
+    grad_copy(2).wait_recv()
+    here_out_ref[...] = grad + g_recv[2].astype(f32)
+    grad = dot(x[...], d_pre[0], TN)
+    grad_copy(3).wait_recv()
+    here_in_ref[...] = grad + g_recv[3].astype(f32)
+
+    own_back.wait()
+    for stage in range(STAGES):
+        for other in partners(stage):
+            back_copy(me, other).wait_recv()
+            back_copy(other, me).wait_send()
+            row_copy(other, me).wait_send()
+    for copy in (near_in, near_out, far_near_in, far_out, far_near_out):
+        copy.wait_send()
+    for index in range(4):
+        grad_copy(index).wait_send()
+
+
+def run_expert(rows, cot_rows, factor, router_row, w_in, w_out, w_in_far, experts):
+    total, width = rows.shape
+    slots = total // experts
+    hidden = w_in.shape[1]
+    anyspace, vmem = pl.BlockSpec(memory_space=pl.ANY), pl.BlockSpec(memory_space=pltpu.VMEM)
+    dma = pltpu.SemaphoreType.DMA
+    return pl.pallas_call(
+        functools.partial(expert_kernel, experts, slots, 0),
+        in_specs=[anyspace, vmem, vmem, vmem, anyspace, anyspace, anyspace],
+        out_specs=[vmem] * 7,
+        out_shape=[
+            jax.ShapeDtypeStruct((total, width), bf16),
+            jax.ShapeDtypeStruct((total, width), bf16),
+            jax.ShapeDtypeStruct((1, width), f32),
+            jax.ShapeDtypeStruct((width, hidden), f32),
+            jax.ShapeDtypeStruct((hidden, width), f32),
+            jax.ShapeDtypeStruct((width, hidden), bf16),
+            jax.ShapeDtypeStruct((hidden, width), bf16),
+        ],
+        scratch_shapes=[
+            pltpu.VMEM((total, width), bf16),
+            pltpu.VMEM((4, width, hidden), bf16),
+            pltpu.VMEM((4, hidden, width), bf16),
+            pltpu.VMEM((total, width), bf16),
+            pltpu.VMEM((4, total, hidden), bf16),
+            pltpu.VMEM((4, total, hidden), bf16),
+            pltpu.VMEM((total, width), f32),
+            pltpu.VMEM((total, width), f32),
+            pltpu.VMEM((total, width), bf16),
+            pltpu.VMEM((width, width), bf16),
+            pltpu.VMEM((4, width, width), bf16),
+            dma((experts,)), dma((experts,)), dma((experts,)), dma((experts,)),
+            dma((5,)), dma((5,)), dma((4,)), dma((4,)), dma((5,)),
+        ],
+        compiler_params=pltpu.CompilerParams(
+            collective_id=1, has_side_effects=True, vmem_limit_bytes=60 * 2**20
+        ),
+        cost_estimate=pl.CostEstimate(flops=30 * 10**9, bytes_accessed=40 * 10**6, transcendentals=3 * 10**6),
+        name="expert",
+    )(rows, cot_rows, factor, router_row, w_in, w_out, w_in_far)
 
 
 def shards(
@@ -309,46 +538,25 @@
     hidden = inputs_wide + dot(mixed_own, proj_own) + dot(mixed_other, proj_other)
     normed_two, scaled_two, inverse_two = norm_forward(hidden, gain_two, shift_two)
     normed_two = normed_two.astype(bf16)
-    expert_in = exchange(dot(placing, normed_two).astype(bf16).reshape(experts, slots, width))
-    expert_in = expert_in.reshape(experts * slots, width)
-
-    in_across, out_across = across(w_in[0]), across(w_out[0])
-    weights_in = [w_in[0], in_across, beside(w_in[0]), beside(in_across)]
-    weights_out = [w_out[0], out_across, beside(w_out[0]), beside(out_across)]
+    rows = dot(placing, normed_two).astype(bf16)
 
     cot_factor = cot_rows[:, cap, :slots].astype(f32) + cot_rows[
         :, cap, width // 2 : width // 2 + slots
     ].astype(f32)
     cot_factor = jnp.where(jnp.arange(slots)[None, :] < cap, cot_factor, 0.0).reshape(-1, 1)
-    d_result = cot_rows.reshape(experts * slots, width).astype(f32) * cot_factor
     router_row = lax.dynamic_slice_in_dim(w_router.T, expert, 1, 0).astype(f32)
-    gate = jax.nn.sigmoid(jnp.sum(expert_in.astype(f32) * router_row, axis=1, keepdims=True))
-    d_out = (gate * d_result).astype(bf16)
-    parts = [gelu_parts(dot(expert_in, w)) for w in weights_in]
-    acts = [value.astype(bf16) for value, _ in parts]
-    result = sum(dot(act, w) for act, w in zip(acts, weights_out))
-    d_pres = [
-        (dot(d_out, w, NT) * slope).astype(bf16) for (_, slope), w in zip(parts, weights_out)
-    ]
-    d_gate = jnp.sum(d_result * result, axis=1, keepdims=True)
-    d_logit = (d_gate * gate * (1.0 - gate)).astype(bf16).astype(f32)
-    d_expert_in = sum(dot(d_pre, w, NT) for d_pre, w in zip(d_pres, weights_in)) + d_logit * router_row
-    returned = exchange((gate * result).astype(bf16).reshape(experts, slots, width))
-    d_returned = exchange(d_expert_in.astype(bf16).reshape(experts, slots, width))
-    grads_in = [dot(expert_in, d_pre, TN) for d_pre in d_pres]
-    grads_out = [dot(act, d_out, TN) for act in acts]
-    router_grad = jnp.sum(expert_in.astype(f32) * d_logit, axis=0)
-
-    def collect(grads):
-        here = grads[0] + beside(grads[2].astype(bf16)).astype(f32)
-        there = grads[1] + beside(grads[3].astype(bf16)).astype(f32)
-        return here + across(there.astype(bf16)).astype(f32)
-
-    grad_w_in, grad_w_out = collect(grads_in), collect(grads_out)
+    d_returned, result, router_grad, here_in, here_out, there_in, there_out = run_expert(
+        rows, cot_rows.reshape(experts * slots, width), cot_factor, router_row,
+        w_in[0], w_out[0], across(w_in[0]), experts,
+    )
+    router_grad = router_grad[0]
+    grad_w_out = here_out + across(there_out).astype(f32)
+    grad_w_in = here_in + across(there_in).astype(f32)
+    returned = exchange(result.reshape(experts, slots, width))
 
     output = hidden + dot(placing, returned.reshape(experts * slots, width), TN)
     d_output = cotangent.astype(f32) * row_factor[:, None]
-    d_norm_two = dot(placing, d_returned.reshape(experts * slots, width), TN)
+    d_norm_two = dot(placing, d_returned, TN)
     d_back_two, grad_gain_two, grad_shift_two = norm_backward(
         d_norm_two, scaled_two, inverse_two, gain_two
     )

time: 528 us -> 478 us (0.905)
  Pallas kernels: 43.7 us -> 140 us
  matrix products: 115 us -> 35.4 us
  waiting for transfers between devices: 182 us -> 106 us
  blocking collectives: 41.6 us -> 73.7 us
  starting transfers between devices: 47 us -> 23.2 us
    pallas_call x0 -> x1, Pallas kernels: none -> 96.5 us  [run_expert(): pl.pallas_call(functools.partial(expert_kernel, experts, slots, 0), in_sp...]
    dot_general x36 -> x12, matrix products: 115 us -> 35.4 us  [dot(): return lax.dot_general(left, right, dims, preferred_element_type=f32)]
    ppermute x8 -> x7, waiting for transfers between devices: 120 us -> 72 us  [across(): return lax.ppermute(value, 'mp', ACROSS)]
    all_to_all x5 -> x2, waiting for transfers between devices: 43.4 us -> 0.01 us  [exchange(): return lax.all_to_all(rows, 'dp', split_axis=0, concat_axis=0, tiled=True)]
    all_to_all x0 -> x1, blocking collectives: none -> 32 us  [exchange(): return lax.all_to_all(rows, 'dp', split_axis=0, concat_axis=0, tiled=True)]
    all_to_all x5 -> x2, starting transfers between devices: 33.3 us -> 11.8 us  [exchange(): return lax.all_to_all(rows, 'dp', split_axis=0, concat_axis=0, tiled=True)]
    ppermute x1, waiting for transfers between devices: 5.6 us -> 16.8 us  [shards(): ext = lax.ppermute(qkv[-HALF:, features:], 'mp', LATER)]
    unnamed x191 -> x126, local copies, waits for them, and re-layouts: 21.2 us -> 17.8 us
  transfers between devices with their start and end apart: 29 -> 17, of which waited for: 11 -> 7; matrix products, arithmetic and copies ran while one was open for 24% -> 17% of each run, Pallas kernels for 8% -> 4%
where the time goes in v2:
time: 478 us; the launch traced here: 470 us
  Pallas kernels  140 us (29%)
  waiting for transfers between devices  106 us (22%)
  blocking collectives  73.7 us (15%)
  other arithmetic  39 us (8%)
  local copies, waits for them, and re-layouts  37.2 us (8%)
  matrix products  35.4 us (7%)
  starting transfers between devices  23.2 us (5%)
  between operations  15.2 us (3%)
    pallas_call x1, Pallas kernels, run_expert(): pl.pallas_call(functools.partial(expert_kernel, experts, slots, 0), in_sp...  96.5 us
    ppermute x7, waiting for transfers between devices, across(): return lax.ppermute(value, 'mp', ACROSS)  72 us
    psum x1, blocking collectives, shards(): small = lax.psum(small, ('dp', 'mp'))  41.7 us
    dot_general x12, matrix products, dot(): return lax.dot_general(left, right, dims, preferred_element_type=f32)  35.4 us
    all_to_all x1, blocking collectives, exchange(): return lax.all_to_all(rows, 'dp', split_axis=0, concat_axis=0, tiled=True)  32 us
    pallas_call x1, Pallas kernels, attend_back(): pl.pallas_call(attend_back_kernel, grid=(pairs,), in_specs=[pl.BlockSpec(...  22.9 us
    pallas_call x1, Pallas kernels, attend(): pl.pallas_call(attend_kernel, grid=(pairs,), in_specs=[pl.BlockSpec(memor...  20.6 us
    unnamed x126, local copies, waits for them, and re-layouts  17.8 us
  transfers between devices with their start and end apart: 17, of which 7 were waited for; matrix products, arithmetic and copies ran while one was open for 17% of the time, Pallas kernels for 4%

profile of v2, /device:TPU:12, one launch (start us, length us, event | category | flops | bytes accessed | tf_op | source)
XLA Modules:
  0.0 469.5 jit_solution(8005963207390109555)
XLA Ops:
  21.2 15.2 %collective-permute-done.1 = bf16[3,192,768]{2,1,0:T(8,128)(2,1)} collective-permute-done((bf16[3,192,768]{2,1,0:T(8,128)(2,1)}, bf16[3,192,768]{2,1,0:T(8,128)(2,1)}, u32[]{:S(2)}, u32[]{:S(2)}) %collective-permute-start.1) | collective-permute-done | bytes 884768 | tf_op jit(solution)/shard_map/ppermute | solution.py:229
  39.3 3.8 convolution_convert_fusion.q_ref.k_ref.v_ref
  50.5 6.5 %all-to-all-start = ((bf16[8,128,768]{2,1,0:T(8,128)(2,1)}), bf16[8,128,768]{2,1,0:T(8,128)(2,1)}, u32[]{:S(2)}, u32[]{:S(2)}) async-start(bf16[8,128,768]{2,1,0:T(8,128)(2,1)} %scatter.9), calls=%async_computation | async-start | bytes 3145728 | tf_op jit(solution)/shard_map/all_to_all | solution.py:241
  60.5 16.8 %collective-permute-done.2.ke_ref.ve_ref = bf16[512,768]{1,0:T(8,128)(2,1)S(1)} collective-permute-done((bf16[512,768]{1,0:T(8,128)(2,1)}, bf16[512,768]{1,0:T(8,128)(2,1)S(1)}, u32[]{:S(2)}, u32[]{:S(2)}) %collective-permute-start.2) | collective-permute-done | bytes 786464 | tf_op jit(solution)/shard_map/ppermute | solution.py:530
  79.6 20.6 %attend.1 = (bf16[1536,384]{1,0:T(8,128)(2,1)S(1)}, f32[3,8,1536]{2,1,0:T(8,128)S(1)}) custom-call(s32[1]{0:T(128)} %bitcast.chip_ref, bf16[1536,1152]{1,0:T(8,128)(2,1)S(1)} %copy-done.5, bf16[1536,1152]{1,0:T(8,128)(2,1)S(1)} %copy-done.5, bf16[1536,1152]{1,0:T(8,128)(2,1)S(1)} %copy-done.5, bf16[512,768]{1,0:T(8,128)(2,1)S(1)} %collective-permute-done.2.ke_ref.ve_ref, ...), custom_call_target="tpu_custom_call" | custom-call | flops 16000000000 | bytes 8000000 | tf_op jit(solution)/shard_map/attend/pallas_call | solution.py:117
  108.3 2.9 fusion.22.rows_ref
  116.2 96.5 %expert.1 = (bf16[1024,768]{1,0:T(8,128)(2,1)}, bf16[1024,768]{1,0:T(8,128)(2,1)}, f32[1,768]{1,0:T(1,128)}, f32[768,768]{1,0:T(8,128)}, f32[768,768]{1,0:T(8,12...) custom-call(bf16[1024,768]{1,0:T(8,128)(2,1)} %fusion.22.rows_ref, bf16[1024,768]{1,0:T(8,128)(2,1)} %bitcast.5.cot_ref, ...), custom_call_target="tpu_custom_call" | custom-call | flops 30000001024 | bytes 40000000 | tf_op jit(solution)/shard_map/expert/pallas_call | solution.py:444
  212.7 5.1 %fusion.54 = (f32[768]{0:T(1024)}, f32[768,768]{1,0:T(8,128)}) fusion(bf16[1024,768]{1,0:T(8,128)(2,1)} %get-tuple-element.51, s32[768]{0:T(1024)S(1)} %copy-done.52), kind=kOutput, calls=%fused_computation.135 | convolution fusion | flops 1209335040 | bytes 3938304 | tf_op jit(solution)/shard_map/dot_general | solution.py:33
  217.8 3.2 copy.71
  221.1 3.2 multiply_reduce_fusion
  230.8 22.9 %attend_back.1 = (bf16[1536,384]{1,0:T(8,128)(2,1)}, f32[1536,384]{1,0:T(8,128)}, f32[1536,384]{1,0:T(8,128)}, bf16[512,384]{1,0:T(8,128)(2,1)}, bf16[512,384]{1,0:T(8,128)(2,1)}) custom-call(s32[1]{0:T(128)} %bitcast.chip_ref, bf16[1536,1152]{1,0:T(8,128)(2,1)} %copy-done.4, bf16[1536,1152]{1,0:T(8,128)(2,1)} %copy-done.4, bf16[1536,1152]{1,0:T(8,128)(2,1)} %copy-done.4, ...), custom_call_target="tpu_custom_call" | custom-call | flops 20000000000 | bytes 12000000 | tf_op jit(solution)/shard_map/attend_back/pallas_call | solution.py:194
  259.2 14.4 %collective-permute-done.8 = bf16[512,768]{1,0:T(8,128)(2,1)S(1)} collective-permute-done((bf16[512,768]{1,0:T(8,128)(2,1)S(1)}, bf16[512,768]{1,0:T(8,128)(2,1)S(1)}, u32[]{:S(2)}, u32[]{:S(2)}) %collective-permute-start.8) | collective-permute-done | bytes 786464 | tf_op jit(solution)/shard_map/ppermute | solution.py:570
  273.8 3.0 fusion.30
  281.9 23.5 %collective-permute-done.11 = bf16[192,768]{1,0:T(8,128)(2,1)S(1)} collective-permute-done((bf16[192,768]{1,0:T(8,128)(2,1)S(1)}, bf16[192,768]{1,0:T(8,128)(2,1)S(1)}, u32[]{:S(2)}, u32[]{:S(2)}) %collective-permute-start.11) | collective-permute-done | bytes 294944 | tf_op jit(solution)/shard_map/ppermute | solution.py:229
  306.0 32.0 %all_to_all.15 = bf16[8,96,768]{2,1,0:T(8,128)(2,1)} all-to-all(bf16[8,96,768]{2,1,0:T(8,128)(2,1)S(1)} %bitcast.46), channel_id=1, replica_groups=mesh['dp'=8,'mp'=4] {'dp'}, dimensions={0} | all-to-all | bytes 2359296 | tf_op jit(solution)/shard_map/all_to_all | solution.py:241
  338.0 5.3 %all-to-all-start.1 = ((bf16[8,128,768]{2,1,0:T(8,128)(2,1)}), bf16[8,128,768]{2,1,0:T(8,128)(2,1)}, u32[]{:S(2)}, u32[]{:S(2)}) async-start(bf16[8,128,768]{2,1,0:T(8,128)(2,1)} %bitcast.51), calls=%async_computation.1 | async-start | bytes 3145728 | tf_op jit(solution)/shard_map/all_to_all | solution.py:241
  351.0 6.0 %fusion.31 = f32[1536,768]{0,1:T(8,128)S(1)} fusion(bf16[1152,768]{1,0:T(8,128)(2,1)} %bitcast.49, bf16[512,768]{1,0:T(8,128)(2,1)} %copy-done.29, bf16[1024,768]{1,0:T(8,128)(2,1)} %copy-done.22, bf16[1536,384]{1,0:T(8,128)(2,1)} %get-tuple-element.53), kind=kOutput, calls=%fused_computation.60 | convolution fusion | flops 2728525824 | bytes 10027008 | tf_op jit(solution)/shard_map/dot_general | solution.py:33
  358.1 14.3 %collective-permute-done.12 = bf16[768,768]{1,0:T(8,128)(2,1)} collective-permute-done((bf16[768,768]{1,0:T(8,128)(2,1)}, bf16[768,768]{1,0:T(8,128)(2,1)}, u32[]{:S(2)}, u32[]{:S(2)}) %collective-permute-start.12) | collective-permute-done | bytes 1179680 | tf_op jit(solution)/shard_map/ppermute | solution.py:229
  372.5 3.1 add_bitcast_fusion.1
  375.6 19.0 %collective-permute-done.13 = bf16[768,768]{1,0:T(8,128)(2,1)} collective-permute-done((bf16[768,768]{1,0:T(8,128)(2,1)}, bf16[768,768]{1,0:T(8,128)(2,1)}, u32[]{:S(2)}, u32[]{:S(2)}) %collective-permute-start.13) | collective-permute-done | bytes 1179680 | tf_op jit(solution)/shard_map/ppermute | solution.py:229
  394.6 3.0 add_bitcast_fusion
  399.8 4.0 add_convert_fusion
  406.2 3.3 fusion.18
  416.2 41.7 %psum.7 = f32[12,768]{1,0:T(8,128)S(1)} all-reduce(f32[12,768]{1,0:T(8,128)S(1)} %concatenate.46), channel_id=1, replica_groups=mesh['dp'=8,'mp'=4] {'dp','mp'}, use_global_device_ids=true, to_apply=%region_17.18 | all-reduce | flops 9216 | bytes 73728 | tf_op jit(solution)/shard_map/psum | solution.py:606
  (221 shorter events, 85.0 us)
Async XLA Ops:
  7.2 51.3 %collective-permute-start.3 = (bf16[192,768]{1,0:T(8,128)(2,1)}, bf16[192,768]{1,0:T(8,128)(2,1)}, u32[]{:S(2)}, u32[]{:S(2)}) collective-permute-start(bf16[192,768]{1,0:T(8,128)(2,1)} %param.30), channel_id=1, source_target_pairs={{0,2},{2,0},{1,3},{3,1},{4,6},{6,4},{5,7},{7,5},{8,10},{10,8},{9,1... | collective-permute-start | bytes 884744 | tf_op jit(solution)/shard_map/ppermute | solution.py:229
  7.8 28.7 %collective-permute-start.1 = (bf16[3,192,768]{2,1,0:T(8,128)(2,1)}, bf16[3,192,768]{2,1,0:T(8,128)(2,1)}, u32[]{:S(2)}, u32[]{:S(2)}) collective-permute-start(bf16[3,192,768]{2,1,0:T(8,128)(2,1)} %bitcast.52), channel_id=1, source_target_pairs={{0,2},{2,0},{1,3},{3,1},{4,6},{6,4},{5,7},{7,5},{8,10},{10,8},{9,1... | collective-permute-start | bytes 2654216 | tf_op jit(solution)/shard_map/ppermute | solution.py:229
  13.5 24.5 %collective-permute-start = (bf16[768,768]{0,1:T(8,128)(2,1)}, bf16[768,768]{0,1:T(8,128)(2,1)S(1)}, u32[]{:S(2)}, u32[]{:S(2)}) collective-permute-start(bf16[768,768]{0,1:T(8,128)(2,1)} %fusion.11), channel_id=1, source_target_pairs={{0,1},{1,0},{2,3},{3,2},{4,5},{5,4},{6,7},{7,6},{8,9},{9,8},{10,11... | collective-permute-start | bytes 3538952 | tf_op jit(solution)/shard_map/ppermute | solution.py:233
  13.5 102.6 %collective-permute-start.6 = (bf16[768,768]{1,0:T(8,128)(2,1)}, bf16[768,768]{1,0:T(8,128)(2,1)}, u32[]{:S(2)}, u32[]{:S(2)}) collective-permute-start(bf16[768,768]{1,0:T(8,128)(2,1)} %bitcast.8.w_in_ref), channel_id=1, source_target_pairs={{0,2},{2,0},{1,3},{3,1},{4,6},{6,4},{5,7},{7,5},{8,10},{10,8},{9,1... | collective-permute-start | bytes 3538952 | tf_op jit(solution)/shard_map/ppermute | solution.py:229
  18.5 28.6 %copy-start.50 = (s32[768]{0:T(1024)}, s32[768]{0:T(1024)S(1)}, u32[]{:S(2)}) copy-start(s32[768]{0:T(1024)S(1)} %convert_add_fusion.3) | copy-start | bytes 9220
  18.6 17.9 %copy-start.28 = (bf16[768,3,192]{0,2,1:T(8,128)(2,1)S(1)}, bf16[768,3,192]{0,2,1:T(8,128)(2,1)}, u32[]{:S(2)}) copy-start(bf16[768,3,192]{0,2,1:T(8,128)(2,1)} %param.29) | copy-start | bytes 2654212
  45.8 31.5 %collective-permute-start.2 = (bf16[512,768]{1,0:T(8,128)(2,1)}, bf16[512,768]{1,0:T(8,128)(2,1)S(1)}, u32[]{:S(2)}, u32[]{:S(2)}) collective-permute-start(bf16[512,768]{1,0:T(8,128)(2,1)} %slice.101), channel_id=1, source_target_pairs={{0,2},{1,3},{4,6},{5,7},{8,10},{9,11},{12,14},{13,15},{16,18},{17,... | collective-permute-start | bytes 2359304 | tf_op jit(solution)/shard_map/ppermute | solution.py:530
  50.5 60.7 %all-to-all-start = ((bf16[8,128,768]{2,1,0:T(8,128)(2,1)}), bf16[8,128,768]{2,1,0:T(8,128)(2,1)}, u32[]{:S(2)}, u32[]{:S(2)}) async-start(bf16[8,128,768]{2,1,0:T(8,128)(2,1)} %scatter.9), calls=%async_computation | async-start | bytes 3145728 | tf_op jit(solution)/shard_map/all_to_all | solution.py:241
  59.6 43.7 %copy-start.14 = (bf16[192,768]{1,0:T(8,128)(2,1)}, bf16[192,768]{1,0:T(8,128)(2,1)S(1)}, u32[]{:S(2)}) copy-start(bf16[192,768]{1,0:T(8,128)(2,1)S(1)} %get-tuple-element.129) | copy-start | bytes 884740
  60.5 44.6 %collective-permute-start.5 = (bf16[384,768]{1,0:T(8,128)(2,1)}, bf16[384,768]{1,0:T(8,128)(2,1)}, u32[]{:S(2)}, u32[]{:S(2)}) collective-permute-start(bf16[384,768]{1,0:T(8,128)(2,1)} %pad_maximum_fusion.9), channel_id=1, source_target_pairs={{0,1},{1,0},{2,3},{3,2},{4,5},{5,4},{6,7},{7,6},{8,9},{9,8},{10,11... | collective-permute-start | bytes 1769480 | tf_op jit(solution)/shard_map/ppermute | solution.py:233
  77.3 22.9 %copy-start.6 = (bf16[512,768]{1,0:T(8,128)(2,1)}, bf16[512,768]{1,0:T(8,128)(2,1)S(1)}, u32[]{:S(2)}) copy-start(bf16[512,768]{1,0:T(8,128)(2,1)S(1)} %collective-permute-done.2.ke_ref.ve_ref) | copy-start | bytes 2359300
  101.0 4.1 collective-permute-start.4
  116.2 96.5 %copy-start.52 = (s32[768]{0:T(1024)S(1)}, s32[768]{0:T(1024)}, u32[]{:S(2)}) copy-start(s32[768]{0:T(1024)} %copy-done.50) | copy-start | bytes 9220
  225.3 2.9 collective-permute-start.7
  254.9 18.7 %collective-permute-start.8 = (bf16[512,768]{1,0:T(8,128)(2,1)S(1)}, bf16[512,768]{1,0:T(8,128)(2,1)S(1)}, u32[]{:S(2)}, u32[]{:S(2)}) collective-permute-start(bf16[512,768]{1,0:T(8,128)(2,1)S(1)} %pad_maximum_fusion.8), channel_id=1, source_target_pairs={{2,0},{3,1},{6,4},{7,5},{10,8},{11,9},{14,12},{15,13},{18,16},{19,... | collective-permute-start | bytes 2359304 | tf_op jit(solution)/shard_map/ppermute | solution.py:570
  277.0 28.4 %collective-permute-start.10 = (bf16[3,192,768]{2,1,0:T(8,128)(2,1)S(1)}, bf16[3,192,768]{2,1,0:T(8,128)(2,1)S(1)}, u32[]{:S(2)}, u32[]{:S(2)}) collective-permute-start(bf16[3,192,768]{2,1,0:T(8,128)(2,1)S(1)} %select_convert_fusion), channel_id=1, source_target_pairs={{0,2},{2,0},{1,3},{3,1},{4,6},{6,4},{5,7},{7,5},{8,10},{10,8},{9,1... | collective-permute-start | bytes 2654216 | tf_op jit(solution)/shard_map/ppermute | solution.py:229
  280.8 24.6 %collective-permute-start.11 = (bf16[192,768]{1,0:T(8,128)(2,1)S(1)}, bf16[192,768]{1,0:T(8,128)(2,1)S(1)}, u32[]{:S(2)}, u32[]{:S(2)}) collective-permute-start(bf16[192,768]{1,0:T(8,128)(2,1)S(1)} %select_convert_fusion.1), channel_id=1, source_target_pairs={{0,2},{2,0},{1,3},{3,1},{4,6},{6,4},{5,7},{7,5},{8,10},{10,8},{9,1... | collective-permute-start | bytes 884744 | tf_op jit(solution)/shard_map/ppermute | solution.py:229
  338.0 61.8 %all-to-all-start.1 = ((bf16[8,128,768]{2,1,0:T(8,128)(2,1)}), bf16[8,128,768]{2,1,0:T(8,128)(2,1)}, u32[]{:S(2)}, u32[]{:S(2)}) async-start(bf16[8,128,768]{2,1,0:T(8,128)(2,1)} %bitcast.51), calls=%async_computation.1 | async-start | bytes 3145728 | tf_op jit(solution)/shard_map/all_to_all | solution.py:241
  343.3 115.9 %all-gather.2.cloned.1.call-start = ((), (), s32[]{:S(2)}) async-start(), calls=%async_computation.3 | async-start | bytes 1327104 | tf_op jit(solution)/shard_map/all_gather | solution.py:596
  343.3 29.2 %collective-permute-start.12 = (bf16[768,768]{1,0:T(8,128)(2,1)}, bf16[768,768]{1,0:T(8,128)(2,1)}, u32[]{:S(2)}, u32[]{:S(2)}) collective-permute-start(bf16[768,768]{1,0:T(8,128)(2,1)} %get-tuple-element.60), channel_id=1, source_target_pairs={{0,2},{2,0},{1,3},{3,1},{4,6},{6,4},{5,7},{7,5},{8,10},{10,8},{9,1... | collective-permute-start | bytes 3538952 | tf_op jit(solution)/shard_map/ppermute | solution.py:229
  345.2 49.4 %collective-permute-start.13 = (bf16[768,768]{1,0:T(8,128)(2,1)}, bf16[768,768]{1,0:T(8,128)(2,1)}, u32[]{:S(2)}, u32[]{:S(2)}) collective-permute-start(bf16[768,768]{1,0:T(8,128)(2,1)} %get-tuple-element.62), channel_id=1, source_target_pairs={{0,2},{2,0},{1,3},{3,1},{4,6},{6,4},{5,7},{7,5},{8,10},{10,8},{9,1... | collective-permute-start | bytes 3538952 | tf_op jit(solution)/shard_map/ppermute | solution.py:229
  356.9 18.7 %copy-start.13 = (f32[1536,768]{0,1:T(8,128)}, f32[1536,768]{0,1:T(8,128)S(1)}, u32[]{:S(2)}) copy-start(f32[1536,768]{0,1:T(8,128)S(1)} %fusion.31) | copy-start | bytes 14155780
  358.1 48.0 %collective-permute-start.9 = (bf16[768,768]{0,1:T(8,128)(2,1)}, bf16[768,768]{0,1:T(8,128)(2,1)}, u32[]{:S(2)}, u32[]{:S(2)}) collective-permute-start(bf16[768,768]{0,1:T(8,128)(2,1)} %dynamic-slice_convert_fusion), channel_id=1, source_target_pairs={{0,1},{1,0},{2,3},{3,2},{4,5},{5,4},{6,7},{7,6},{8,9},{9,8},{10,11... | collective-permute-start | bytes 3538952 | tf_op jit(solution)/shard_map/ppermute | solution.py:233
  372.5 22.1 %copy-start.19 = (f32[768,768]{1,0:T(8,128)S(1)}, f32[768,768]{1,0:T(8,128)}, u32[]{:S(2)}) copy-start(f32[768,768]{1,0:T(8,128)} %get-tuple-element.61) | copy-start | bytes 7077892
  (52 other events, 236.5 us)
Sparse Core Ops, SparseCore 0:
  399.9 41.8 all-gather.1

commit v3 on v2

--- a/solution.py
+++ b/solution.py
@@ -26,7 +26,6 @@
 ACROSS = [(0, 2), (2, 0), (1, 3), (3, 1)]
 BESIDE = [(0, 1), (1, 0), (2, 3), (3, 2)]
 LATER = [(0, 2), (1, 3)]
-EARLIER = [(2, 0), (3, 1)]
 
 
 def dot(left, right, dims=NN):
@@ -38,18 +37,6 @@
     inverse = lax.rsqrt(jnp.mean(centre * centre, axis=-1, keepdims=True) + norm_epsilon)
     scaled = centre * inverse
     return (scaled * gain_vec + shift_vec, scaled, inverse)
-
-
-def norm_backward(d_normed, scaled, inverse, gain_vec):
-    d_scaled = d_normed * gain_vec
-    correction = jnp.mean(d_scaled, axis=-1, keepdims=True) + scaled * jnp.mean(
-        d_scaled * scaled, axis=-1, keepdims=True
-    )
-    return (
-        inverse * (d_scaled - correction),
-        jnp.sum(d_normed * scaled, axis=0),
-        jnp.sum(d_normed, axis=0),
-    )
 
 
 def plan(chip, run):
@@ -143,102 +130,482 @@
     )(chip, qkv, qkv, qkv, ext, ext)
 
 
-def attend_back_kernel(
-    chip_ref, q_ref, k_ref, v_ref, ke_ref, ve_ref, d_ref, o_ref, l_ref,
-    dq_ref, dk_ref, dv_ref, dke_ref, dve_ref, keys, values, d_keys, d_values,
+def across(value):
+    return lax.ppermute(value, "mp", ACROSS)
+
+
+def beside(value):
+    return lax.ppermute(value, "mp", BESIDE)
+
+
+def in_order(first, own, other):
+    return jnp.where(first, own, other), jnp.where(first, other, own)
+
+
+def exchange(rows):
+    return lax.all_to_all(rows, "dp", split_axis=0, concat_axis=0, tiled=True)
+
+
+def remote(src, dst, send, recv, device):
+    return pltpu.make_async_remote_copy(
+        src_ref=src, dst_ref=dst, send_sem=send, recv_sem=recv, device_id=device, device_id_type=MESH
+    )
+
+
+def greet(devices):
+    barrier = pltpu.get_barrier_semaphore()
+    for device in devices:
+        pl.semaphore_signal(barrier, inc=1, device_id=device, device_id_type=MESH)
+    pl.semaphore_wait(barrier, len(devices))
+
+
+def normalise(values):
+    centre = values - jnp.mean(values, axis=-1, keepdims=True)
+    inverse = lax.rsqrt(jnp.mean(centre * centre, axis=-1, keepdims=True) + norm_epsilon)
+    return centre * inverse, inverse
+
+
+def norm_pull(d_normed, scaled, inverse, gain):
+    d_scaled = d_normed * gain
+    return inverse * (
+        d_scaled
+        - jnp.mean(d_scaled, axis=-1, keepdims=True)
+        - scaled * jnp.mean(d_scaled * scaled, axis=-1, keepdims=True)
+    )
+
+
+PAIRS = 3
+PAIR = 2 * HEAD_DIM
+STRIP = 256
+
+
+def backward_kernel(
+    experts, slots,
+    x_ref, cot_ref, factor_ref, hidden_ref, gain_one_ref, gain_two_ref, placing_ref, d_returned_ref,
+    result_ref, normed_ref, qkv_ref, ext_ref, mixed_ref, log_ref, heads_ref, proj_ref,
+    output_ref, input_grad_ref, sums_ref, norms_ref,
+    returned, d_hidden, d_branch, d_mixed, keys, values, d_keys, d_values, d_qkv, d_last,
+    ext_send, ext_recv, grads, grads_send, grads_recv, d_norm, norm_send, norm_recv,
+    row_send, row_recv, ext_sems, branch_sems, grad_sems, norm_sems, local_sem,
 ):
-    chip = chip_ref[0]
-    lane = lax.broadcasted_iota(jnp.int32, (1, 128), 1)
-    keys[0:HALF] = ke_ref[...]
-    keys[HALF:] = k_ref[...]
-    values[0:HALF] = ve_ref[...]
-    values[HALF:] = v_ref[...]
-    d_keys[...] = jnp.zeros_like(d_keys)
-    d_values[...] = jnp.zeros_like(d_values)
-
-    def run(first, whole):
-        span = (whole + 1) * BLOCK
-        start = pl.multiple_of(first + HALF - whole * BLOCK, BLOCK)
-        queries = q_ref[pl.ds(first, BLOCK)] * bf16(0.125)
-        d_mixed = d_ref[pl.ds(first, BLOCK)]
-        near = keys[pl.ds(start, span)]
-        near_values = values[pl.ds(start, span)]
-        product = (d_mixed.astype(f32) * o_ref[pl.ds(first, BLOCK)].astype(f32)).T
-        dq = dk = dv = 0.0
-        for head in range(2):
-            here = (lane // HEAD_DIM) == head
-            own = jnp.where(here, queries, bf16(0))
-            d_own = jnp.where(here, d_mixed, bf16(0))
-            delta = jnp.sum(product[HEAD_DIM * head : HEAD_DIM * (head + 1)], axis=0, keepdims=True)
-            scores = mask_diagonal(dot(near, own, NT), whole)
-            probs = jnp.exp(scores - l_ref[head : head + 1, pl.ds(first, BLOCK)])
-            d_probs = dot(near_values, d_own, NT)
-            d_scores = (probs * (d_probs - delta)).astype(bf16)
-            dv = dv + dot(probs.astype(bf16), d_own)
-            dk = dk + dot(d_scores, own)
-            dq = dq + dot(d_scores, jnp.where(here, near, bf16(0)), TN)
-        dq_ref[pl.ds(first, BLOCK)] = (dq * 0.125).astype(bf16)
-        d_keys[pl.ds(start, span)] += dk
-        d_values[pl.ds(start, span)] += dv
-
-    plan(chip, run)
-    dk_ref[...] = d_keys[HALF:]
-    dv_ref[...] = d_values[HALF:]
-    dke_ref[...] = d_keys[:HALF].astype(bf16)
-    dve_ref[...] = d_values[:HALF].astype(bf16)
-
-
-def attend_back(chip, qkv, ext, d_mixed, mixed, log_total):
-    rows = qkv.shape[0]
-    pairs = qkv.shape[1] // 384
+    me, mp = lax.axis_index("dp"), lax.axis_index("mp")
+    chip, core = mp // 2, mp % 2
+    tok = x_ref.shape[0]
+    rows = 2 * tok
+    beside = {"mp": mp + 1 - 2 * core}
+    across = {"mp": (mp + 2) % 4}
+    greet([{"dp": (me + k) % experts} for k in range(1, experts)] + [beside, across])
+
+    def chunk(index):
+        return pl.ds(pl.multiple_of(index * slots, 16), slots)
+
+    def row_copy(target, source):
+        return remote(
+            result_ref.at[chunk(target)], returned.at[chunk(source)],
+            row_send.at[target], row_recv.at[source], {"dp": target},
+        )
+
+    own_rows = pltpu.make_async_copy(result_ref.at[chunk(me)], returned.at[chunk(me)], local_sem)
+    own_rows.start()
+    others = [(me + k) % experts for k in range(1, experts)]
+    for other in others:
+        row_copy(other, me).start()
+
+    norms_ref[...] = jnp.zeros_like(norms_ref)
+    mine = pl.multiple_of(core * tok, tok)
+
+    def second_norm(step, carry):
+        at = pl.ds(pl.multiple_of(step * STRIP, STRIP), STRIP)
+        scaled, inverse = normalise(hidden_ref[at])
+        d_normed = dot(placing_ref[at], d_returned_ref[...])
+        norms_ref[2:3] += jnp.sum(d_normed * scaled, axis=0, keepdims=True)
+        norms_ref[3:4] += jnp.sum(d_normed, axis=0, keepdims=True)
+        total = cot_ref[at].astype(f32) * factor_ref[at] + norm_pull(
+            d_normed, scaled, inverse, gain_two_ref[...]
+        )
+        d_hidden[at] = total
+        d_branch[pl.ds(pl.multiple_of(mine + step * STRIP, STRIP), STRIP)] = total.astype(bf16)
+        return carry
+
+    lax.fori_loop(0, tok // STRIP, second_norm, 0)
+    branch_copy = remote(
+        d_branch.at[pl.ds(mine, tok)], d_branch.at[pl.ds(mine, tok)],
+        branch_sems.at[0], branch_sems.at[1], beside,
+    )
+    branch_copy.start()
+    branch_copy.wait_recv()
+
+    def push_branch(step, carry):
+        at = pl.ds(pl.multiple_of(step * STRIP, STRIP), STRIP)
+        d_mixed[at] = dot(d_branch[at], proj_ref[...], NT).astype(bf16)
+        return carry
+
+    lax.fori_loop(0, rows // STRIP, push_branch, 0)
+    grads[3] = dot(mixed_ref[...], d_branch[...], TN)
+
+    lane = lax.broadcasted_iota(jnp.int32, (1, PAIR), 1)
+    second = chip == 1
+
+    def pair_of(step):
+        return (1 - chip) * (PAIRS - 1 - step) + chip * step
+
+    def ext_copy(pair):
+        return remote(ext_send.at[pair], ext_recv.at[pair], ext_sems.at[0, pair], ext_sems.at[1, pair], across)
+
+    def attention(step, carry):
+        pair = pair_of(step)
+
+        def column(offset):
+            return pl.ds(pl.multiple_of((offset * PAIRS + pair) * PAIR, PAIR), PAIR)
+
+        keys[0:HALF] = ext_ref[:, column(0)]
+        keys[HALF:] = qkv_ref[:, column(1)]
+        values[0:HALF] = ext_ref[:, column(1)]
+        values[HALF:] = qkv_ref[:, column(2)]
+        d_keys[...] = jnp.zeros_like(d_keys)
+        d_values[...] = jnp.zeros_like(d_values)
+
+        def run(first, whole):
+            span = (whole + 1) * BLOCK
+            start = pl.multiple_of(first + HALF - whole * BLOCK, BLOCK)
+            at = pl.ds(first, BLOCK)
+            queries = qkv_ref[at, column(0)] * bf16(0.125)
+            d_out = d_mixed[at, column(0)]
+            near = keys[pl.ds(start, span)]
+            near_values = values[pl.ds(start, span)]
+            product = (d_out.astype(f32) * mixed_ref[at, column(0)].astype(f32)).T
+            dq = dk = dv = 0.0
+            for head in range(2):
+                here = (lane // HEAD_DIM) == head
+                own = jnp.where(here, queries, bf16(0))
+                d_own = jnp.where(here, d_out, bf16(0))
+                delta = jnp.sum(product[HEAD_DIM * head : HEAD_DIM * (head + 1)], axis=0, keepdims=True)
+                scores = mask_diagonal(dot(near, own, NT), whole)
+                probs = jnp.exp(scores - log_ref[pair, head : head + 1, at])
+                d_probs = dot(near_values, d_own, NT)
+                d_scores = (probs * (d_probs - delta)).astype(bf16)
+                dv = dv + dot(probs.astype(bf16), d_own)
+                dk = dk + dot(d_scores, own)
+                dq = dq + dot(d_scores, jnp.where(here, near, bf16(0)), TN)
+            d_qkv[at, column(0)] = (dq * 0.125).astype(bf16)
+            d_keys[pl.ds(start, span)] += dk
+            d_values[pl.ds(start, span)] += dv
+
+        @pl.when(second)
+        def _():
+            run(0, 2)
+            run(BLOCK, 3)
+            ext_send[pair, :, 0:PAIR] = d_keys[0:HALF].astype(bf16)
+            ext_send[pair, :, PAIR:] = d_values[0:HALF].astype(bf16)
+            ext_copy(pair).start()
+            run(4 * BLOCK, 2)
+            run(5 * BLOCK, 3)
+
+        @pl.when(chip == 0)
+        def _():
+            run(2 * BLOCK, 2)
+            run(3 * BLOCK, 3)
+            run(4 * BLOCK, 0)
+            run(5 * BLOCK, 1)
+
+        run(pl.multiple_of(2 * chip * BLOCK, BLOCK), 0)
+        run(pl.multiple_of((2 * chip + 1) * BLOCK, BLOCK), 1)
+        d_qkv[:, column(1)] = d_keys[HALF:].astype(bf16)
+        d_qkv[:, column(2)] = d_values[HALF:].astype(bf16)
+
+        @pl.when(chip == 0)
+        def _():
+            d_last[pair, :, 0:PAIR] = d_keys[rows:]
+            d_last[pair, :, PAIR:] = d_values[rows:]
+
+        return carry
+
+    lax.fori_loop(0, PAIRS, attention, 0)
+
+    other_part = pl.ds(pl.multiple_of((1 - chip) * grads_send.shape[1], 16), grads_send.shape[1])
+    own_part = pl.ds(pl.multiple_of(chip * grads_send.shape[1], 16), grads_send.shape[1])
+
+    @pl.when(chip == 0)
+    def _():
+        for step in range(PAIRS):
+            pair = PAIRS - 1 - step
+            ext_copy(pair).wait_recv()
+            total = d_last[pair] + ext_recv[pair].astype(f32)
+            for index in range(2):
+                d_qkv[rows - HALF :, ((1 + index) * PAIRS + pair) * PAIR : ((1 + index) * PAIRS + pair + 1) * PAIR] = (
+                    total[:, index * PAIR : (index + 1) * PAIR].astype(bf16)
+                )
+
+    @pl.when(second)
+    def _():
+        for pair in range(PAIRS):
+            ext_copy(pair).wait_send()
+
+    for index in range(3):
+        grads[index] = dot(d_qkv[:, index * PAIRS * PAIR : (index + 1) * PAIRS * PAIR], normed_ref[...], TN)
+    for index in range(4):
+        grads_send[index] = grads[index, other_part].astype(bf16)
+    grad_copy = remote(grads_send, grads_recv, grad_sems.at[0], grad_sems.at[1], across)
+    grad_copy.start()
+
+    def pull_norm(step, carry):
+        at = pl.ds(pl.multiple_of(step * STRIP, STRIP), STRIP)
+        d_norm[at] = dot(d_qkv[at], heads_ref[...])
+        return carry
+
+    lax.fori_loop(0, rows // STRIP, pull_norm, 0)
+    norm_send[...] = d_norm[pl.ds(pl.multiple_of((1 - core) * tok, tok), tok)].astype(bf16)
+    norm_copy = remote(norm_send, norm_recv, norm_sems.at[0], norm_sems.at[1], beside)
+    norm_copy.start()
+    own_rows.wait()
+    for other in others:
+        row_copy(me, other).wait_recv()
+
+    def finish(step, carry):
+        at = pl.ds(pl.multiple_of(step * STRIP, STRIP), STRIP)
+        output_ref[at] = (hidden_ref[at] + dot(placing_ref[at], returned[...])).astype(bf16)
+        return carry
+
+    lax.fori_loop(0, tok // STRIP, finish, 0)
+    norm_copy.wait_recv()
+
+    def first_norm(step, carry):
+        at = pl.ds(pl.multiple_of(step * STRIP, STRIP), STRIP)
+        scaled, inverse = normalise(x_ref[at].astype(f32))
+        d_normed = d_norm[pl.ds(pl.multiple_of(mine + step * STRIP, STRIP), STRIP)] + norm_recv[at].astype(f32)
+        norms_ref[0:1] += jnp.sum(d_normed * scaled, axis=0, keepdims=True)
+        norms_ref[1:2] += jnp.sum(d_normed, axis=0, keepdims=True)
+        input_grad_ref[at] = (
+            d_hidden[at] + norm_pull(d_normed, scaled, inverse, gain_one_ref[...])
+        ).astype(bf16)
+        return carry
+
+    lax.fori_loop(0, tok // STRIP, first_norm, 0)
+    grad_copy.wait_recv()
+    part = grads_send.shape[1]
+    for index in range(4):
+        sums_ref[index * part : (index + 1) * part] = (
+            grads[index, own_part] + grads_recv[index].astype(f32)
+        ).astype(bf16)
+    if sums_ref.shape[0] > 4 * part:
+        sums_ref[4 * part :] = jnp.zeros((sums_ref.shape[0] - 4 * part, sums_ref.shape[1]), bf16)
+    for other in others:
+        row_copy(other, me).wait_send()
+    branch_copy.wait_send()
+    norm_copy.wait_send()
+    grad_copy.wait_send()
+
+
+def run_backward(
+    x, cotangent, factor, hidden, gain_one, gain_two, placing, d_returned, result, normed_chip, qkv, ext,
+    mixed, log_total, heads, proj, experts, sum_rows,
+):
+    tok, width = x.shape
+    rows = 2 * tok
+    total = d_returned.shape[0]
+    part = proj.shape[0] // 2
+    anyspace, vmem = pl.BlockSpec(memory_space=pl.ANY), pl.BlockSpec(memory_space=pltpu.VMEM)
+    dma = pltpu.SemaphoreType.DMA
     return pl.pallas_call(
-        attend_back_kernel,
-        grid=(pairs,),
-        in_specs=[
-            pl.BlockSpec(memory_space=pltpu.SMEM),
-            column_block(rows, 0),
-            column_block(rows, pairs),
-            column_block(rows, 2 * pairs),
-            column_block(HALF, 0),
-            column_block(HALF, pairs),
-            column_block(rows, 0),
-            column_block(rows, 0),
-            pl.BlockSpec((None, 8, rows), lambda pair: (pair, 0, 0)),
-        ],
-        out_specs=[column_block(rows, 0)] * 3 + [column_block(HALF, 0)] * 2,
+        functools.partial(backward_kernel, experts, total // experts),
+        in_specs=[vmem] * 8 + [anyspace] + [vmem] * 7,
+        out_specs=[vmem] * 4,
         out_shape=[
-            jax.ShapeDtypeStruct((rows, pairs * 128), bf16),
-            jax.ShapeDtypeStruct((rows, pairs * 128), f32),
-            jax.ShapeDtypeStruct((rows, pairs * 128), f32),
-            jax.ShapeDtypeStruct((HALF, pairs * 128), bf16),
-            jax.ShapeDtypeStruct((HALF, pairs * 128), bf16),
+            jax.ShapeDtypeStruct((tok, width), bf16),
+            jax.ShapeDtypeStruct((tok, width), bf16),
+            jax.ShapeDtypeStruct((sum_rows, width), bf16),
+            jax.ShapeDtypeStruct((8, width), f32),
         ],
         scratch_shapes=[
-            pltpu.VMEM((HALF + rows, 128), bf16),
-            pltpu.VMEM((HALF + rows, 128), bf16),
-            pltpu.VMEM((HALF + rows, 128), f32),
-            pltpu.VMEM((HALF + rows, 128), f32),
+            pltpu.VMEM((total, width), bf16),
+            pltpu.VMEM((tok, width), f32),
+            pltpu.VMEM((rows, width), bf16),
+            pltpu.VMEM((rows, PAIRS * PAIR), bf16),
+            pltpu.VMEM((HALF + rows, PAIR), bf16),
+            pltpu.VMEM((HALF + rows, PAIR), bf16),
+            pltpu.VMEM((HALF + rows, PAIR), f32),
+            pltpu.VMEM((HALF + rows, PAIR), f32),
+            pltpu.VMEM((rows, 3 * PAIRS * PAIR), bf16),
+            pltpu.VMEM((PAIRS, HALF, 2 * PAIR), f32),
+            pltpu.VMEM((PAIRS, HALF, 2 * PAIR), bf16),
+            pltpu.VMEM((PAIRS, HALF, 2 * PAIR), bf16),
+            pltpu.VMEM((4, 2 * part, width), f32),
+            pltpu.VMEM((4, part, width), bf16),
+            pltpu.VMEM((4, part, width), bf16),
+            pltpu.VMEM((rows, width), f32),
+            pltpu.VMEM((tok, width), bf16),
+            pltpu.VMEM((tok, width), bf16),
+            dma((experts,)), dma((experts,)), dma((2, PAIRS)), dma((2,)), dma((2,)), dma((2,)), dma,
         ],
-        compiler_params=pltpu.CompilerParams(vmem_limit_bytes=56 * 2**20),
-        cost_estimate=pl.CostEstimate(flops=20 * 10**9, bytes_accessed=12 * 10**6, transcendentals=8 * 10**6),
-        name="attend_back",
-    )(chip, qkv, qkv, qkv, ext, ext, d_mixed, mixed, log_total)
-
-
-def across(value):
-    return lax.ppermute(value, "mp", ACROSS)
-
-
-def beside(value):
-    return lax.ppermute(value, "mp", BESIDE)
-
-
-def in_order(first, own, other):
-    return jnp.where(first, own, other), jnp.where(first, other, own)
-
-
-def exchange(rows):
-    return lax.all_to_all(rows, "dp", split_axis=0, concat_axis=0, tiled=True)
+        compiler_params=pltpu.CompilerParams(
+            collective_id=2, has_side_effects=True, vmem_limit_bytes=60 * 2**20
+        ),
+        cost_estimate=pl.CostEstimate(flops=30 * 10**9, bytes_accessed=30 * 10**6, transcendentals=8 * 10**6),
+        name="backward",
+    )(
+        x, cotangent, factor, hidden, gain_one, gain_two, placing, d_returned, result, normed_chip, qkv, ext,
+        mixed, log_total, heads, proj,
+    )
+
+
+def reduce_kernel(
+    experts,
+    sums_ref, small_ref, here_in_ref, here_out_ref, there_in_ref, there_out_ref,
+    total_ref, small_total_ref, grad_in_ref, grad_out_ref,
+    half_recv, half, piece_recv, small_held, small_recv, small_pieces, far_in, far_out,
+    half_sems, piece_sems, gather_sems, back_sems, far_sems, small_sems, small_piece_sems,
+):
+    me, mp = lax.axis_index("dp"), lax.axis_index("mp")
+    beside = {"mp": mp + 1 - 2 * (mp % 2)}
+    across = {"mp": (mp + 2) % 4}
+    side, line = me % 2, me // 2
+    lines = experts // 2
+    partner = {"dp": me + 1 - 2 * side}
+    mates = [(line + k) % lines for k in range(1, lines)]
+    greet([beside, across, partner] + [{"dp": 2 * mate + side} for mate in mates])
+    half_rows = half.shape[0]
+    piece_rows = half_rows // lines
+    lanes = sums_ref.shape[1] // 2
+    own_half = pl.multiple_of(side * half_rows, 16)
+    far_half = pl.multiple_of((1 - side) * half_rows, 16)
+
+    far_copies = [
+        remote(there_out_ref, far_out, far_sems.at[0, 0], far_sems.at[1, 0], across),
+        remote(there_in_ref, far_in, far_sems.at[0, 1], far_sems.at[1, 1], across),
+    ]
+    def columns(index):
+        return pl.ds(index * lanes, lanes)
+
+    def piece(index, base=0):
+        return pl.ds(pl.multiple_of(base + index * piece_rows, 16), piece_rows)
+
+    def half_copy(part):
+        return remote(
+            sums_ref.at[pl.ds(far_half, half_rows), columns(part)], half_recv.at[:, columns(part)],
+            half_sems.at[0, part], half_sems.at[1, part], partner,
+        )
+
+    def piece_copy(part, target, source):
+        return remote(
+            half.at[piece(target), columns(part)], piece_recv.at[source, :, columns(part)],
+            piece_sems.at[0, part, target], piece_sems.at[1, part, source], {"dp": 2 * target + side},
+        )
+
+    def gather_copy(part, target, source):
+        block = total_ref.at[piece(source, own_half), columns(part)]
+        return remote(
+            block, block, gather_sems.at[0, part, target], gather_sems.at[1, part, source], {"dp": 2 * target + side}
+        )
+
+    def back_copy(part, which):
+        block = total_ref.at[pl.ds(which, half_rows), columns(part)]
+        return remote(block, block, back_sems.at[0, part], back_sems.at[1, part], partner)
+
+    small_held[0] = small_ref[...]
+
+    def small_step(index, device):
+        return remote(
+            small_held.at[index], small_recv.at[index], small_sems.at[0, index], small_sems.at[1, index], device
+        )
+
+    small_step(0, across).start()
+    for copy in far_copies:
+        copy.start()
+    for part in range(2):
+        half_copy(part).start()
+    for index, device in enumerate((across, beside, partner)):
+        if index:
+            small_step(index, device).start()
+        small_step(index, device).wait()
+        small_held[index + 1] = small_held[index] + small_recv[index]
+
+    def small_copy(target, source):
+        return remote(
+            small_held.at[3], small_pieces.at[source],
+            small_piece_sems.at[0, target], small_piece_sems.at[1, source], {"dp": 2 * target + side},
+        )
+
+    for mate in mates:
+        small_copy(mate, line).start()
+    small_pieces[line] = small_held[3]
+
+    for part in range(2):
+        at = slice(part * lanes, (part + 1) * lanes)
+        half_copy(part).wait_recv()
+        half[:, at] = (
+            sums_ref[pl.ds(own_half, half_rows), at].astype(f32) + half_recv[:, at].astype(f32)
+        ).astype(bf16)
+        for mate in mates:
+            piece_copy(part, mate, line).start()
+    for part in range(2):
+        at = slice(part * lanes, (part + 1) * lanes)
+        value = half[piece(line), at].astype(f32)
+        for mate in mates:
+            piece_copy(part, line, mate).wait_recv()
+            value += piece_recv[mate, :, at].astype(f32)
+        total_ref[piece(line, own_half), at] = value.astype(bf16)
+        for mate in mates:
+            gather_copy(part, mate, line).start()
+    for mate in mates:
+        small_copy(line, mate).wait_recv()
+    small_total = small_pieces[0]
+    for index in range(1, lines):
+        small_total += small_pieces[index]
+    small_total_ref[...] = small_total
+    far_copies[0].wait_recv()
+    grad_out_ref[...] = here_out_ref[...] + far_out[...].astype(f32)
+    for part in range(2):
+        for mate in mates:
+            gather_copy(part, line, mate).wait_recv()
+        back_copy(part, own_half).start()
+    far_copies[1].wait_recv()
+    grad_in_ref[...] = here_in_ref[...] + far_in[...].astype(f32)
+    for part in range(2):
+        back_copy(part, far_half).wait_recv()
+        back_copy(part, own_half).wait_send()
+        half_copy(part).wait_send()
+        for mate in mates:
+            piece_copy(part, mate, line).wait_send()
+            gather_copy(part, mate, line).wait_send()
+    for mate in mates:
+        small_copy(mate, line).wait_send()
+    for copy in far_copies:
+        copy.wait_send()
+
+
+def run_reduce(sums, small, here_in, here_out, there_in, there_out, experts):
+    rows, width = sums.shape
+    lines = experts // 2
+    vmem = pl.BlockSpec(memory_space=pltpu.VMEM)
+    dma = pltpu.SemaphoreType.DMA
+    return pl.pallas_call(
+        functools.partial(reduce_kernel, experts),
+        in_specs=[vmem] * 6,
+        out_specs=[vmem] * 4,
+        out_shape=[
+            jax.ShapeDtypeStruct((rows, width), bf16),
+            jax.ShapeDtypeStruct(small.shape, f32),
+            jax.ShapeDtypeStruct(here_in.shape, f32),
+            jax.ShapeDtypeStruct(here_out.shape, f32),
+        ],
+        scratch_shapes=[
+            pltpu.VMEM((rows // 2, width), bf16),
+            pltpu.VMEM((rows // 2, width), bf16),
+            pltpu.VMEM((lines, rows // experts, width), bf16),
+            pltpu.VMEM((4,) + small.shape, f32),
+            pltpu.VMEM((3,) + small.shape, f32),
+            pltpu.VMEM((lines,) + small.shape, f32),
+            pltpu.VMEM(there_in.shape, bf16),
+            pltpu.VMEM(there_out.shape, bf16),
+            dma((2, 2)), dma((2, 2, lines)), dma((2, 2, lines)), dma((2, 2)), dma((2, 2)),
+            dma((2, 3)), dma((2, lines)),
+        ],
+        compiler_params=pltpu.CompilerParams(
+            collective_id=3, has_side_effects=True, vmem_limit_bytes=48 * 2**20
+        ),
+        cost_estimate=pl.CostEstimate(flops=10**7, bytes_accessed=20 * 10**6, transcendentals=0),
+        name="reduce",
+    )(sums, small, here_in, here_out, there_in, there_out)
 
 
 def gelu_parts(pre):
@@ -337,21 +704,24 @@
         router_grad_ref[...] += jnp.sum(features * d_logit, axis=0, keepdims=True)
 
     def stage_of(step):
-        return jnp.where(step < 6, step // 2, jnp.where(step < 12, (step - 6) // 2, 3))
+        return jnp.where(
+            (step < 2) | (step >= 14), 0, jnp.where(step < 6, 3, jnp.where(step < 10, 2, 1))
+        )
 
     def step_body(step, carry):
         stage = stage_of(step)
-        part = jnp.where(step < 6, step % 2, jnp.where(step < 12, 2 + step % 2, step - 12))
+        part = jnp.where(step < 4, step % 2, jnp.where(step < 6, step - 2, (step - 6) % 4))
+        part = jnp.where(step >= 14, step - 12, part)
         rows = group_rows(group_of(stage))
 
-        for static, at in enumerate((0, 2, 4, 12)):
+        for static, at in enumerate((0, 10, 6, 2)):
             @pl.when(step == at)
             def _():
                 if static == 0:
                     own_rows.wait()
                 for other in partners(static):
                     row_copy(me, other).wait_recv()
-        @pl.when((step == 0) | (step == 2) | (step == 4) | (step == 12))
+        @pl.when((step == 0) | (step == 2) | (step == 6) | (step == 10))
         def _():
             prepare(stage, rows)
 
@@ -365,13 +735,13 @@
             near_in.wait_recv()
             near_out.wait_recv()
 
-        @pl.when(step == 6)
+        @pl.when(step == 4)
         def _():
             far_in.wait()
             far_out.wait_recv()
             far_near_out.start()
 
-        @pl.when(step == 7)
+        @pl.when(step == 5)
         def _():
             far_near_in.wait_recv()
             far_near_out.wait_recv()
@@ -385,11 +755,11 @@
         d_pre[part, rows] = d_value
         d_x[rows] += dot(d_value, wi[part], NT)
 
-        @pl.when((step == 7) | (step == 9) | (step == 11) | (step == 15))
+        @pl.when((step == 5) | (step == 9) | (step == 13) | (step == 15))
         def _():
             finish(stage, rows)
 
-        for static, at in enumerate((7, 9, 11, 15)):
+        for static, at in enumerate((15, 13, 9, 5)):
             @pl.when(step == at)
             def _():
                 for other in partners(static):
@@ -549,71 +919,31 @@
         rows, cot_rows.reshape(experts * slots, width), cot_factor, router_row,
         w_in[0], w_out[0], across(w_in[0]), experts,
     )
-    router_grad = router_grad[0]
-    grad_w_out = here_out + across(there_out).astype(f32)
-    grad_w_in = here_in + across(there_in).astype(f32)
-    returned = exchange(result.reshape(experts, slots, width))
-
-    output = hidden + dot(placing, returned.reshape(experts * slots, width), TN)
-    d_output = cotangent.astype(f32) * row_factor[:, None]
-    d_norm_two = dot(placing, d_returned, TN)
-    d_back_two, grad_gain_two, grad_shift_two = norm_backward(
-        d_norm_two, scaled_two, inverse_two, gain_two
+
+    piece = (4 * w_proj.shape[0] // experts + 15) // 16 * 16
+    output, input_grad, sums, norms = run_backward(
+        inputs, cotangent, row_factor[:, None], hidden, gain_one[None], gain_two[None], placing.T, d_returned,
+        result, normed_chip, qkv, ext, mixed, log_total, w_heads, proj_own,
+        experts, experts * piece,
     )
-    d_hidden = d_output + d_back_two
-
-    d_branch = d_hidden.astype(bf16)
-    d_branch = jnp.concatenate(in_order(on_first_core, d_branch, beside(d_branch)))
-    grad_proj = dot(mixed, d_branch, TN)
-    d_mixed = dot(d_branch, proj_own, NT).astype(bf16)
-    dq, dk, dv, dk_ext, dv_ext = attend_back(chip_scalar, qkv, ext, d_mixed, mixed, log_total)
-    ext_back = lax.ppermute(jnp.concatenate([dk_ext, dv_ext], axis=1), "mp", EARLIER).astype(f32)
-    d_kv = jnp.concatenate([dk, dv], axis=1)
-    d_kv = jnp.concatenate([d_kv[:-HALF], d_kv[-HALF:] + ext_back])
-    d_qkv = jnp.concatenate([dq, d_kv.astype(bf16)], axis=1)
-    grad_heads = dot(d_qkv, normed_chip, TN).reshape(3, features, width)
-    d_norm_chip = dot(d_qkv, w_heads)
-    d_norm_own = lax.dynamic_slice_in_dim(d_norm_chip, core * tok, tok, 0)
-    d_norm_other = lax.dynamic_slice_in_dim(d_norm_chip, (1 - core) * tok, tok, 0).astype(bf16)
-    d_norm_one = d_norm_own + beside(d_norm_other).astype(f32)
-    d_back_one, grad_gain_one, grad_shift_one = norm_backward(
-        d_norm_one, scaled_one, inverse_one, gain_one
+    own_expert = (expert_ids == expert)[:, None]
+    small = jnp.concatenate([norms, jnp.where(own_expert, router_grad, 0.0)])
+    sums, small, grad_w_in, grad_w_out = run_reduce(
+        sums, small, here_in, here_out, there_in, there_out, experts
     )
-    input_grad = d_hidden + d_back_one
-
-    def own_and_other(grads, axis):
-        first, second = jnp.split(grads, 2, axis=axis)
-        return in_order(on_first_chip, first, second)
-
-    heads_own, heads_other = own_and_other(grad_heads, 1)
-    proj_grad_own, proj_grad_other = own_and_other(grad_proj, 0)
-    heads_sum = heads_own + across(heads_other.astype(bf16)).astype(f32)
-    proj_sum = proj_grad_own + across(proj_grad_other.astype(bf16)).astype(f32)
-    sums = jnp.concatenate([heads_sum.reshape(-1, width), proj_sum]).astype(bf16)
-    groups = experts
-    pieces = exchange(sums.reshape(groups, -1, width))
-    piece = jnp.sum(pieces.astype(f32), axis=0).astype(bf16)
-    sums = lax.all_gather(piece, "dp", axis=0, tiled=True).astype(f32)
-    grad_w_qkv = jnp.transpose(sums[: -w_proj.shape[0]].reshape(w_own.shape), (2, 0, 1))
-    grad_w_proj = sums[-w_proj.shape[0] :]
-    own_expert = (expert_ids == expert)[:, None]
-    small = jnp.concatenate(
-        [
-            jnp.stack([grad_gain_one, grad_shift_one, grad_gain_two, grad_shift_two]),
-            jnp.where(own_expert, router_grad[None, :], 0.0),
-        ]
-    )
-    small = lax.psum(small, ("dp", "mp"))
+    split = 3 * w_proj.shape[0]
+    grad_w_qkv = jnp.transpose(sums[:split].astype(f32).reshape(w_own.shape), (2, 0, 1))
+    grad_w_proj = sums[split : split + w_proj.shape[0]].astype(f32)
     return (
-        output.astype(bf16),
-        input_grad.astype(bf16),
+        output,
+        input_grad,
         small[0],
         small[1],
         grad_w_qkv,
         grad_w_proj,
         small[2],
         small[3],
-        small[4:].T,
+        small[8:].T,
         grad_w_in[None],
         grad_w_out[None],
     )

time: 478 us -> 359 us (0.75)
  Pallas kernels: 140 us -> 251 us
  waiting for transfers between devices: 106 us -> 30 us
  blocking collectives: 73.7 us -> 0 us
  matrix products: 35.4 us -> 14.9 us
  local copies, waits for them, and re-layouts: 37.2 us -> 20.6 us
  other arithmetic: 39 us -> 23.8 us
  between operations: 15.2 us -> 1.38 us
  starting transfers between devices: 23.2 us -> 10.4 us
    pallas_call x1 -> x2, Pallas kernels: 22.9 us -> 146 us  [the longest x1 83.6 us: run_backward(): pl.pallas_call(functools.partial(backward_kernel, experts, total // exper...]
    ppermute x7 -> x3, waiting for transfers between devices: 72 us -> 0.01 us  [across(): return lax.ppermute(value, 'mp', ACROSS)]
    psum x1 -> x0, blocking collectives: 41.7 us -> none  [shards(): small = lax.psum(small, ('dp', 'mp'))]
    all_to_all x1 -> x0, blocking collectives: 32 us -> none  [exchange(): return lax.all_to_all(rows, 'dp', split_axis=0, concat_axis=0, tiled=True)]
    dot_general x12 -> x6, matrix products: 35.4 us -> 14.9 us  [dot(): return lax.dot_general(left, right, dims, preferred_element_type=f32)]
    ppermute x1 -> x0, waiting for transfers between devices: 14.4 us -> none  [shards(): lax.ppermute(jnp.concatenate([dk_ext, dv_ext], axis=1), 'mp', EARLIER)]
    ppermute x1, waiting for transfers between devices: 16.8 us -> 29.9 us  [shards(): ext = lax.ppermute(qkv[-HALF:, features:], 'mp', LATER)]
    pallas_call x1, Pallas kernels: 96.5 us -> 83.9 us  [run_expert(): pl.pallas_call(functools.partial(expert_kernel, experts, slots, 0), in_sp...]
  transfers between devices with their start and end apart: 17 -> 8, of which waited for: 7 -> 1; matrix products, arithmetic and copies ran while one was open for 17% -> 12% of each run, Pallas kernels for 4% -> 6%
where the time goes in v3:
time: 359 us; the launch traced here: 352 us
  Pallas kernels  251 us (70%)
  waiting for transfers between devices  30 us (8%)
  other arithmetic  23.8 us (7%)
  local copies, waits for them, and re-layouts  20.6 us (6%)
  matrix products  14.9 us (4%)
  starting transfers between devices  10.4 us (3%)
    pallas_call x1, Pallas kernels, run_expert(): pl.pallas_call(functools.partial(expert_kernel, experts, slots, 0), in_sp...  83.9 us
    pallas_call x1, Pallas kernels, run_backward(): pl.pallas_call(functools.partial(backward_kernel, experts, total // exper...  83.6 us
    pallas_call x1, Pallas kernels, run_reduce(): pl.pallas_call(functools.partial(reduce_kernel, experts), in_specs=[vmem]...  62.8 us
    ppermute x1, waiting for transfers between devices, shards(): ext = lax.ppermute(qkv[-HALF:, features:], 'mp', LATER)  29.9 us
    pallas_call x1, Pallas kernels, attend(): pl.pallas_call(attend_kernel, grid=(pairs,), in_specs=[pl.BlockSpec(memor...  20.7 us
    dot_general x6, matrix products, dot(): return lax.dot_general(left, right, dims, preferred_element_type=f32)  14.9 us
    unnamed x73, local copies, waits for them, and re-layouts  12.3 us
  transfers between devices with their start and end apart: 8, of which 1 were waited for; matrix products, arithmetic and copies ran while one was open for 12% of the time, Pallas kernels for 6%

profile of v3, /device:TPU:12, one launch (start us, length us, event | category | flops | bytes accessed | tf_op | source)
XLA Modules:
  0.0 352.1 jit_solution(1501675851295654471)
XLA Ops:
  1.3 1.5 convert_reduce_fusion
  2.8 1.8 fusion.5
  5.7 1.6 collective-permute-start.3
  12.5 4.0 %fusion.12 = bf16[1024,768]{1,0:T(8,128)(2,1)} fusion(bf16[768,768]{1,0:T(8,128)(2,1)} %cot_ref.1, s32[768]{0:T(1024)S(1)} %convert_add_fusion.2), kind=kOutput, calls=%fused_computation.25 | convolution fusion | flops 1209532416 | bytes 2755584 | tf_op jit(solution)/shard_map/dot_general | solution.py:32
  16.4 1.5 scatter.6
  17.9 1.5 scatter.9
  19.3 6.3 %all-to-all-start = ((bf16[8,128,768]{2,1,0:T(8,128)(2,1)}), bf16[8,128,768]{2,1,0:T(8,128)(2,1)}, u32[]{:S(2)}, u32[]{:S(2)}) async-start(bf16[8,128,768]{2,1,0:T(8,128)(2,1)} %scatter.9), calls=%async_computation | async-start | bytes 3145728 | tf_op jit(solution)/shard_map/all_to_all | solution.py:146
  26.1 1.6 broadcast_select_fusion.3
  29.2 4.7 %convolution_convert_fusion.q_ref.k_ref.v_ref.qkv_ref = bf16[1536,1152]{1,0:T(8,128)(2,1)S(1)} fusion(bf16[1152,768]{1,0:T(8,128)(2,1)S(1)} %bitcast.37, bf16[768,768]{1,0:T(8,128)(2,1)S(1)} %get-tuple-element.76, bf16[768,768]{1,0:T(8,128)(2,1)S(1)} %get-tuple-element.75), kind=kOutput, calls=%fused_computation | convolution fusion | flops 2724397056 | bytes 7667712 | tf_op jit(solution)/shard_map/dot_general | solution.py:32
  34.0 1.7 copy-done.6
  35.7 1.5 collective-permute-start.2
  37.2 1.6 fusion.2.placing_ref
  40.9 29.9 %collective-permute-done.2.ke_ref.ve_ref.ext_ref = bf16[512,768]{1,0:T(8,128)(2,1)S(1)} collective-permute-done((bf16[512,768]{1,0:T(8,128)(2,1)S(1)}, bf16[512,768]{1,0:T(8,128)(2,1)S(1)}, u32[]{:S(2)}, u32[]{:S(2)}) %collective-permute-start.2) | collective-permute-done | bytes 786464 | tf_op jit(solution)/shard_map/ppermute | solution.py:900
  70.8 20.7 %attend.1 = (bf16[1536,384]{1,0:T(8,128)(2,1)S(1)}, f32[3,8,1536]{2,1,0:T(8,128)S(1)}) custom-call(s32[1]{0:T(128)} %bitcast.chip_ref, bf16[1536,1152]{1,0:T(8,128)(2,1)S(1)} %copy-done.7, bf16[1536,1152]{1,0:T(8,128)(2,1)S(1)} %copy-done.7, bf16[1536,1152]{1,0:T(8,128)(2,1)S(1)} %copy-done.7, ...), custom_call_target="tpu_custom_call" | custom-call | flops 16000000000 | bytes 8000000 | tf_op jit(solution)/shard_map/attend/pallas_call | solution.py:104
  94.9 1.3 bitcast_convert_fusion.router_ref
  96.2 2.9 pad_maximum_fusion.normed_ref
  100.4 2.1 fusion.28
  104.0 3.0 fusion.11.rows_ref
  108.9 83.9 %expert.1 = (bf16[1024,768]{1,0:T(8,128)(2,1)}, bf16[1024,768]{1,0:T(8,128)(2,1)}, f32[1,768]{1,0:T(1,128)}, f32[768,768]{1,0:T(8,128)}, f32[768,768]{1,0:T(8,12...) custom-call(bf16[1024,768]{1,0:T(8,128)(2,1)} %fusion.11.rows_ref, bf16[1024,768]{1,0:T(8,128)(2,1)} %bitcast.5.cot_ref, ...), custom_call_target="tpu_custom_call" | custom-call | flops 30000001024 | bytes 40000000 | tf_op jit(solution)/shard_map/expert/pallas_call | solution.py:814
  193.6 83.6 %backward.1 = (bf16[768,768]{1,0:T(8,128)(2,1)}, bf16[768,768]{1,0:T(8,128)(2,1)}, bf16[768,768]{1,0:T(8,128)(2,1)}, f32[8,768]{1,0:T(8,128)}) custom-call(bf16[768,768]{1,0:T(8,128)(2,1)} %x_ref.1, bf16[768,768]{1,0:T(8,128)(2,1)} %cot_ref.1, f32[768,1]{1,0:T(8,128)} %broadcast_in_dim.148.factor_ref, f32[768,768]{1,0:T(8,128)} %copy-done.12, ...), custom_call_target="tpu_custom_call" | custom-call | flops 30000001024 | bytes 30000000 | tf_op jit(solution)/shard_map/backward/pallas_call | solution.py:409
  279.2 62.8 %reduce.16 = (bf16[768,768]{1,0:T(8,128)(2,1)S(1)}, f32[16,768]{1,0:T(8,128)S(1)}, f32[768,768]{1,0:T(8,128)}, f32[768,768]{1,0:T(8,128)}) custom-call(bf16[768,768]{1,0:T(8,128)(2,1)S(1)} %copy-done.4, f32[16,768]{1,0:T(8,128)S(1)} %pad_maximum_fusion.3.small_ref, f32[768,768]{1,0:T(8,128)} %get-tuple-element.61.here_in_ref, ...), custom_call_target="tpu_custom_call" | custom-call | flops 10000000 | bytes 20000000 | tf_op jit(solution)/shard_map/reduce/pallas_call | solution.py:581
  344.1 1.4 convert_bitcast_fusion
  347.9 1.4 copy.70
  350.4 1.4 copy.71
  (122 shorter events, 27.3 us)
Async XLA Ops:
  0.6 7.3 %copy-start = (s32[3072,1]{0,1:T(1,128)S(1)}, s32[3072,1]{0,1:T(1,128)}, u32[]{:S(2)}) copy-start(s32[3072,1]{0,1:T(1,128)} %param.22) | copy-start | bytes 36868
  0.7 4.5 %copy-start.10 = (bf16[768,768]{1,0:T(8,128)(2,1)S(1)}, bf16[768,768]{1,0:T(8,128)(2,1)}, u32[]{:S(2)}) copy-start(bf16[768,768]{1,0:T(8,128)(2,1)} %x_ref.1) | copy-start | bytes 3538948
  0.7 4.5 %copy-start.23 = (f32[768]{0:T(1024)S(1)}, f32[768]{0:T(1024)}, u32[]{:S(2)}) copy-start(f32[768]{0:T(1024)} %param.27) | copy-start | bytes 9220
  0.7 4.5 %copy-start.29 = (f32[768]{0:T(1024)S(1)}, f32[768]{0:T(1024)}, u32[]{:S(2)}) copy-start(f32[768]{0:T(1024)} %param.28) | copy-start | bytes 9220
  0.7 25.4 %collective-permute-start.1 = (bf16[3,192,768]{2,1,0:T(8,128)(2,1)}, bf16[3,192,768]{2,1,0:T(8,128)(2,1)}, u32[]{:S(2)}, u32[]{:S(2)}) collective-permute-start(bf16[3,192,768]{2,1,0:T(8,128)(2,1)} %bitcast.39), channel_id=1, source_target_pairs={{0,2},{2,0},{1,3},{3,1},{4,6},{6,4},{5,7},{7,5},{8,10},{10,8},{9,1... | collective-permute-start | bytes 2654216 | tf_op jit(solution)/shard_map/ppermute | solution.py:134
  5.7 22.2 %collective-permute-start = (bf16[768,768]{1,0:T(8,128)(2,1)S(1)}, bf16[768,768]{1,0:T(8,128)(2,1)S(1)}, u32[]{:S(2)}, u32[]{:S(2)}) collective-permute-start(bf16[768,768]{1,0:T(8,128)(2,1)S(1)} %fusion.8), channel_id=1, source_target_pairs={{0,1},{1,0},{2,3},{3,2},{4,5},{5,4},{6,7},{7,6},{8,9},{9,8},{10,11... | collective-permute-start | bytes 3538952 | tf_op jit(solution)/shard_map/ppermute | solution.py:138
  5.7 33.0 %collective-permute-start.3 = (bf16[192,768]{1,0:T(8,128)(2,1)}, bf16[192,768]{1,0:T(8,128)(2,1)}, u32[]{:S(2)}, u32[]{:S(2)}) collective-permute-start(bf16[192,768]{1,0:T(8,128)(2,1)} %param.30), channel_id=1, source_target_pairs={{0,2},{2,0},{1,3},{3,1},{4,6},{6,4},{5,7},{7,5},{8,10},{10,8},{9,1... | collective-permute-start | bytes 884744 | tf_op jit(solution)/shard_map/ppermute | solution.py:134
  11.4 5.0 %copy-start.27 = (f32[768]{0:T(1024)}, f32[768]{0:T(1024)S(1)}, u32[]{:S(2)}) copy-start(f32[768]{0:T(1024)S(1)} %select_reduce_fusion.1) | copy-start | bytes 9220
  19.3 87.7 %all-to-all-start = ((bf16[8,128,768]{2,1,0:T(8,128)(2,1)}), bf16[8,128,768]{2,1,0:T(8,128)(2,1)}, u32[]{:S(2)}, u32[]{:S(2)}) async-start(bf16[8,128,768]{2,1,0:T(8,128)(2,1)} %scatter.9), calls=%async_computation | async-start | bytes 3145728 | tf_op jit(solution)/shard_map/all_to_all | solution.py:146
  25.6 83.3 %collective-permute-start.6 = (bf16[768,768]{1,0:T(8,128)(2,1)}, bf16[768,768]{1,0:T(8,128)(2,1)}, u32[]{:S(2)}, u32[]{:S(2)}) collective-permute-start(bf16[768,768]{1,0:T(8,128)(2,1)} %bitcast.44), channel_id=1, source_target_pairs={{0,2},{2,0},{1,3},{3,1},{4,6},{6,4},{5,7},{7,5},{8,10},{10,8},{9,1... | collective-permute-start | bytes 3538952 | tf_op jit(solution)/shard_map/ppermute | solution.py:134
  29.2 4.7 %copy-start.13 = (bf16[768,768]{1,0:T(8,128)(2,1)}, bf16[768,768]{1,0:T(8,128)(2,1)S(1)}, u32[]{:S(2)}) copy-start(bf16[768,768]{1,0:T(8,128)(2,1)S(1)} %get-tuple-element.76) | copy-start | bytes 3538948
  35.7 35.1 %collective-permute-start.2 = (bf16[512,768]{1,0:T(8,128)(2,1)S(1)}, bf16[512,768]{1,0:T(8,128)(2,1)S(1)}, u32[]{:S(2)}, u32[]{:S(2)}) collective-permute-start(bf16[512,768]{1,0:T(8,128)(2,1)S(1)} %slice.92), channel_id=1, source_target_pairs={{0,2},{1,3},{4,6},{5,7},{8,10},{9,11},{12,14},{13,15},{16,18},{17,... | collective-permute-start | bytes 2359304 | tf_op jit(solution)/shard_map/ppermute | solution.py:900
  37.2 33.6 %copy-start.7 = (bf16[1536,1152]{1,0:T(8,128)(2,1)S(1)}, bf16[1536,1152]{1,0:T(8,128)(2,1)}, u32[]{:S(2)}) copy-start(bf16[1536,1152]{1,0:T(8,128)(2,1)} %copy-done.6) | copy-start | bytes 10616836
  39.9 51.6 %copy-start.14 = (bf16[192,768]{1,0:T(8,128)(2,1)}, bf16[192,768]{1,0:T(8,128)(2,1)S(1)}, u32[]{:S(2)}) copy-start(bf16[192,768]{1,0:T(8,128)(2,1)S(1)} %get-tuple-element.81) | copy-start | bytes 884740
  39.9 51.6 %copy-start.16 = (bf16[192,768]{1,0:T(8,128)(2,1)}, bf16[192,768]{1,0:T(8,128)(2,1)S(1)}, u32[]{:S(2)}) copy-start(bf16[192,768]{1,0:T(8,128)(2,1)S(1)} %get-tuple-element.82) | copy-start | bytes 884740
  40.9 59.0 %collective-permute-start.5 = (bf16[384,768]{1,0:T(8,128)(2,1)}, bf16[384,768]{1,0:T(8,128)(2,1)}, u32[]{:S(2)}, u32[]{:S(2)}) collective-permute-start(bf16[384,768]{1,0:T(8,128)(2,1)} %pad_maximum_fusion.2.proj_ref), channel_id=1, source_target_pairs={{0,1},{1,0},{2,3},{3,2},{4,5},{5,4},{6,7},{7,6},{8,9},{9,8},{10,11... | collective-permute-start | bytes 1769480 | tf_op jit(solution)/shard_map/ppermute | solution.py:138
  70.8 20.7 %copy-start.8 = (bf16[512,768]{1,0:T(8,128)(2,1)}, bf16[512,768]{1,0:T(8,128)(2,1)S(1)}, u32[]{:S(2)}) copy-start(bf16[512,768]{1,0:T(8,128)(2,1)S(1)} %collective-permute-done.2.ke_ref.ve_ref.ext_ref) | copy-start | bytes 2359300
  70.8 21.7 %copy-start.28 = (f32[768]{0:T(1024)S(1)}, f32[768]{0:T(1024)}, u32[]{:S(2)}) copy-start(f32[768]{0:T(1024)} %copy-done.27) | copy-start | bytes 9220
  70.8 23.5 %copy-start.31 = (f32[768]{0:T(1024)S(1)}, f32[768]{0:T(1024)}, u32[]{:S(2)}) copy-start(f32[768]{0:T(1024)} %param.31) | copy-start | bytes 9220
  91.5 7.6 %copy-start.5 = (bf16[1536,384]{1,0:T(8,128)(2,1)}, bf16[1536,384]{1,0:T(8,128)(2,1)S(1)}, u32[]{:S(2)}) copy-start(bf16[1536,384]{1,0:T(8,128)(2,1)S(1)} %get-tuple-element.52.mixed_ref) | copy-start | bytes 3538948
  91.5 7.6 %copy-start.9 = (f32[3,8,1536]{2,1,0:T(8,128)}, f32[3,8,1536]{2,1,0:T(8,128)S(1)}, u32[]{:S(2)}) copy-start(f32[3,8,1536]{2,1,0:T(8,128)S(1)} %get-tuple-element.55.log_ref) | copy-start | bytes 442372
  92.5 7.4 %collective-permute-start.4 = (bf16[768,384]{1,0:T(8,128)(2,1)}, bf16[768,384]{1,0:T(8,128)(2,1)}, u32[]{:S(2)}, u32[]{:S(2)}) collective-permute-start(bf16[768,384]{1,0:T(8,128)(2,1)} %constant_dynamic-slice_fusion), channel_id=1, source_target_pairs={{0,1},{1,0},{2,3},{3,2},{4,5},{5,4},{6,7},{7,6},{8,9},{9,8},{10,11... | collective-permute-start | bytes 1769480 | tf_op jit(solution)/shard_map/ppermute | solution.py:138
  193.6 84.3 %copy-start.2 = (bf16[768,768]{1,0:T(8,128)(2,1)S(1)}, bf16[768,768]{1,0:T(8,128)(2,1)}, u32[]{:S(2)}) copy-start(bf16[768,768]{1,0:T(8,128)(2,1)} %get-tuple-element.63.there_in_ref) | copy-start | bytes 3538948
  193.6 84.3 %copy-start.3 = (bf16[768,768]{1,0:T(8,128)(2,1)S(1)}, bf16[768,768]{1,0:T(8,128)(2,1)}, u32[]{:S(2)}) copy-start(bf16[768,768]{1,0:T(8,128)(2,1)} %get-tuple-element.64.there_out_ref) | copy-start | bytes 3538948
  (17 other events, 31.7 us)

commit v4 on v3

v4 whole, which is shorter than its diff:
```python
import functools

import jax
import jax.numpy as jnp
from jax import lax
from jax.experimental import pallas as pl
from jax.experimental.pallas import tpu as pltpu
from jax.sharding import PartitionSpec as P

HEAD_DIM = 64
LEN = 1024
BLOCK = 256
HALF = LEN // 2

norm_epsilon = 1e-05
count_scale = 10.0
masked_score = -1e30

f32 = jnp.float32
bf16 = jnp.bfloat16
MESH = pl.DeviceIdType.MESH
NT = (((1,), (1,)), ((), ()))
NN = (((1,), (0,)), ((), ()))
TN = (((0,), (0,)), ((), ()))


def dot(left, right, dims=NN):
    return lax.dot_general(left, right, dims, preferred_element_type=f32)


def mask_diagonal(scores, whole):
    first = lax.broadcasted_iota(jnp.int32, (BLOCK, BLOCK), 0)
    second = lax.broadcasted_iota(jnp.int32, (BLOCK, BLOCK), 1)
    last = jnp.where(first <= second, scores[whole * BLOCK :], masked_score)
    if not whole:
        return last
    return jnp.concatenate([scores[: whole * BLOCK], last], axis=0)


def remote(src, dst, send, recv, device):
    return pltpu.make_async_remote_copy(
        src_ref=src, dst_ref=dst, send_sem=send, recv_sem=recv, device_id=device, device_id_type=MESH
    )


def greet(devices):
    barrier = pltpu.get_barrier_semaphore()
    for device in devices:
        pl.semaphore_signal(barrier, inc=1, device_id=device, device_id_type=MESH)
    pl.semaphore_wait(barrier, len(devices))


def normalise(values):
    centre = values - jnp.mean(values, axis=-1, keepdims=True)
    inverse = lax.rsqrt(jnp.mean(centre * centre, axis=-1, keepdims=True) + norm_epsilon)
    return centre * inverse, inverse


def norm_pull(d_normed, scaled, inverse, gain):
    d_scaled = d_normed * gain
    return inverse * (
        d_scaled
        - jnp.mean(d_scaled, axis=-1, keepdims=True)
        - scaled * jnp.mean(d_scaled * scaled, axis=-1, keepdims=True)
    )


PAIRS = 3
PAIR = 2 * HEAD_DIM
STRIP = 256


def pick_sequence(positions, factor_ref):
    value = jnp.full(positions.shape, factor_ref[0], f32)
    for index in range(1, factor_ref.shape[0]):
        value = jnp.where(positions >= index * LEN, factor_ref[index], value)
    return value


def forward_kernel(
    experts, slots, cap,
    x_ref, cot_ref, routes_ref, factor_ref, gain_one_ref, shift_one_ref, gain_two_ref, shift_two_ref,
    w_ref, proj_ref, w_in_ref,
    normed_out, qkv_out, ext_out, mixed_out, log_out, heads_out, proj_out, hidden_out, rows_out, cot_out,
    placing_t_out, w_in_far_out,
    normed, qkv, ext, mixed, logs, heads, proj, hidden, rows, placing, placing_t, cot_send, mixed_far, normed_two,
    keys, values,
    w_sems, pass_sems, proj_sems, w_in_sems, normed_sems, ext_sems, mixed_sems, row_send, row_recv, local_sems,
    save_sems,
):
    me, mp = lax.axis_index("dp"), lax.axis_index("mp")
    chip, core = mp // 2, mp % 2
    tok, width = x_ref.shape
    part = proj_ref.shape[0]
    total = experts * slots
    beside = {"mp": mp + 1 - 2 * core}
    across = {"mp": (mp + 2) % 4}
    side = me % 2
    partner = {"dp": me + 1 - 2 * side}
    second = chip == 1
    others = [(me + k) % experts for k in range(1, experts)]
    greet([{"dp": other} for other in others] + [beside, across])

    own_part = pl.ds(pl.multiple_of(chip * part, 16), part)
    other_part = pl.ds(pl.multiple_of((1 - chip) * part, 16), part)
    half = pl.ds(pl.multiple_of(side * (width // 2), 128), width // 2)

    def w_copy(index):
        if index == 3:
            source, target = proj_ref.at[:, half], proj.at[0, own_part, half]
        else:
            source, target = w_ref.at[index, :, half], heads.at[index, own_part, half]
        return remote(source, target, w_sems.at[0, index], w_sems.at[1, index], across)

    def w_pass(index):
        block = proj.at[0, other_part, half] if index == 3 else heads.at[index, other_part, half]
        return remote(block, block, pass_sems.at[0, index], pass_sems.at[1, index], partner)

    proj_pass = remote(proj.at[0], proj.at[1], proj_sems.at[0], proj_sems.at[1], beside)
    w_in_copy = remote(w_in_ref, w_in_far_out, w_in_sems.at[0], w_in_sems.at[1], across)
    for index in range(4):
        w_copy(index).start()
    w_local = pltpu.make_async_copy(w_ref, heads.at[:, own_part], local_sems.at[0])
    proj_local = pltpu.make_async_copy(proj_ref, proj.at[0, own_part], local_sems.at[1])
    w_local.start()
    proj_local.start()

    mine = pl.multiple_of(core * tok, tok)

    def first_norm(step, carry):
        at = pl.ds(pl.multiple_of(step * STRIP, STRIP), STRIP)
        scaled, _ = normalise(x_ref[at].astype(f32))
        normed[pl.ds(pl.multiple_of(HALF + mine + step * STRIP, STRIP), STRIP)] = (
            scaled * gain_one_ref[...][None, :] + shift_one_ref[...][None, :]
        ).astype(bf16)
        return carry

    lax.fori_loop(0, tok // STRIP, first_norm, 0)
    own_normed = normed.at[pl.ds(pl.multiple_of(HALF + mine, STRIP), tok)]
    normed_copy = remote(own_normed, own_normed, normed_sems.at[0], normed_sems.at[1], beside)
    normed_copy.start()

    wide = max(16, experts)
    own_routes = routes_ref[:, pl.ds(pl.multiple_of(mp * tok, tok), tok)]
    picked = own_routes == lax.broadcasted_iota(jnp.int32, (wide, tok), 0)
    earlier = lax.broadcasted_iota(jnp.int32, (tok, tok), 0) < lax.broadcasted_iota(jnp.int32, (tok, tok), 1)
    counts = dot(jnp.where(picked, 1.0, 0.0).astype(bf16), jnp.where(earlier, 1.0, 0.0).astype(bf16))
    rank = jnp.sum(jnp.where(picked, counts, 0.0), axis=0, keepdims=True)
    slot_of = own_routes.astype(f32) * slots + rank
    for strip in range(total // STRIP):
        ids = lax.broadcasted_iota(jnp.int32, (STRIP, tok), 0) + strip * STRIP
        placing[strip * STRIP : (strip + 1) * STRIP] = jnp.where(ids.astype(f32) == slot_of, 1.0, 0.0).astype(bf16)

    positions = mp * tok + lax.broadcasted_iota(jnp.int32, (1, tok), 1)
    factors = pick_sequence(positions, factor_ref)
    high = factors.astype(bf16)
    low = (factors - high.astype(f32)).astype(bf16)
    which = lax.broadcasted_iota(jnp.int32, (16, tok), 0)
    both = jnp.where(which == 0, high, jnp.where(which == 1, low, bf16(0)))
    spread = dot(both, placing[...], NT)

    def place_cot(step, carry):
        at = pl.ds(pl.multiple_of(step * STRIP, STRIP), STRIP)
        cot_send[at] = dot(placing[at], cot_ref[...]).astype(bf16)
        return carry

    lax.fori_loop(0, total // STRIP, place_cot, 0)
    spare = lax.broadcasted_iota(jnp.int32, (16, slots), 0) == cap - (slots - 16)
    for expert in range(experts):
        at = slice((expert + 1) * slots - 16, (expert + 1) * slots)
        here = slice(expert * slots, (expert + 1) * slots)
        for term, column in ((0, 0), (1, width // 2)):
            cot_send[at, column : column + slots] = jnp.where(
                spare, spread[term : term + 1, here], cot_send[at, column : column + slots].astype(f32)
            ).astype(bf16)

    def chunk(index):
        return pl.ds(pl.multiple_of(index * slots, 16), slots)

    def row_copy(target, source):
        return remote(
            cot_send.at[chunk(target)], cot_out.at[chunk(source)],
            row_send.at[target], row_recv.at[source], {"dp": target},
        )

    own_rows = pltpu.make_async_copy(cot_send.at[chunk(me)], cot_out.at[chunk(me)], local_sems.at[2])
    own_rows.start()
    for other in others:
        row_copy(other, me).start()
    for strip in range(total // STRIP):
        at = slice(strip * STRIP, (strip + 1) * STRIP)
        placing_t[:, at] = placing[at].T

    saves = []

    def save(source, target):
        copy = pltpu.make_async_copy(source, target, save_sems.at[len(saves)])
        copy.start()
        saves.append(copy)

    save(placing_t, placing_t_out)

    def pair_of(step):
        return (1 - chip) * step + chip * (PAIRS - 1 - step)

    def column(offset, pair):
        return pl.ds(pl.multiple_of((offset * PAIRS + pair) * PAIR, PAIR), PAIR)

    def project(step):
        pair = pair_of(step)
        weights = jnp.concatenate([heads[index, column(0, pair)] for index in range(3)])

        def strip_of(strip, carry):
            at = pl.ds(pl.multiple_of(strip * 512, 512), 512)
            value = dot(normed[pl.ds(pl.multiple_of(HALF + strip * 512, 512), 512)], weights, NT).astype(bf16)
            for index in range(3):
                qkv[at, column(index, pair)] = value[:, index * PAIR : (index + 1) * PAIR]
            return carry

        lax.fori_loop(0, 2 * tok // 512, strip_of, 0)

    lane = lax.broadcasted_iota(jnp.int32, (1, PAIR), 1)
    row = lax.broadcasted_iota(jnp.int32, (PAIR, 1), 0)

    def attend_block(pair, first, whole):
        span = (whole + 1) * BLOCK
        start = pl.multiple_of(first + HALF - whole * BLOCK, BLOCK)
        at = pl.ds(first, BLOCK)
        queries = qkv[at, column(0, pair)] * bf16(0.125)
        near = keys[pl.ds(start, span)]
        near_values = values[:, pl.ds(start, span)]
        parts = []
        for head in range(2):
            own = jnp.where((lane // HEAD_DIM) == head, queries, bf16(0))
            scores = mask_diagonal(dot(near, own, NT), whole)
            largest = jnp.max(scores, axis=0, keepdims=True)
            expo = jnp.exp(scores - largest)
            summed = jnp.sum(expo, axis=0, keepdims=True)
            parts.append(dot(near_values, expo.astype(bf16)) / summed)
            logs[pair, head : head + 1, at] = largest + jnp.log(summed)
        mixed[at, column(0, pair)] = jnp.where(row < HEAD_DIM, parts[0], parts[1]).T.astype(bf16)

    quarter = HALF // 2
    ext_rows = pl.ds(pl.multiple_of(core * quarter, quarter), quarter)
    ext_copy = remote(
        normed.at[pl.ds(pl.multiple_of(2 * tok + core * quarter, quarter), quarter)], normed.at[ext_rows],
        ext_sems.at[0, 0], ext_sems.at[1, 0], across,
    )
    ext_pass = remote(normed.at[ext_rows], normed.at[ext_rows], ext_sems.at[0, 1], ext_sems.at[1, 1], beside)
    w_local.wait()
    normed_copy.wait_recv()

    @pl.when(chip == 0)
    def _():
        ext_copy.start()

    w_in_copy.start()
    project(0)
    for index in range(4):
        w_copy(index).wait_recv()
        w_pass(index).start()

    def attention(step, carry):
        pair = pair_of(step)

        @pl.when(step == 1)
        def _():
            for index in range(3):
                w_pass(index).wait_recv()
            project(1)
            project(2)

        keys[HALF:] = qkv[:, column(1, pair)]
        values[:, HALF:] = qkv[:, column(2, pair)].T
        for whole in range(4):
            attend_block(pair, pl.multiple_of((2 * chip + whole) * BLOCK, BLOCK), whole)

        @pl.when(chip == 0)
        def _():
            attend_block(pair, 4 * BLOCK, 0)
            attend_block(pair, 5 * BLOCK, 1)

        return carry

    lax.fori_loop(0, PAIRS, attention, 0)
    save(qkv, qkv_out)
    save(heads, heads_out)
    proj_local.wait()
    w_pass(3).wait_recv()
    proj_pass.start()
    save(proj.at[0], proj_out)

    @pl.when(second)
    def _():
        ext_copy.wait_recv()
        ext_pass.start()
        ext_pass.wait_recv()
        for index in range(2):
            ext[:, index * PAIRS * PAIR : (index + 1) * PAIRS * PAIR] = dot(
                normed[0:HALF], heads[1 + index], NT
            ).astype(bf16)

        def late(pair, carry):
            keys[0:HALF] = ext[:, column(0, pair)]
            keys[HALF : 2 * HALF] = qkv[0:HALF, column(1, pair)]
            values[:, 0:HALF] = ext[:, column(1, pair)].T
            values[:, HALF : 2 * HALF] = qkv[0:HALF, column(2, pair)].T
            attend_block(pair, 0, 2)
            attend_block(pair, BLOCK, 3)
            return carry

        lax.fori_loop(0, PAIRS, late, 0)

    @pl.when(chip == 0)
    def _():
        ext_copy.wait_send()
        ext[...] = jnp.zeros_like(ext)
        normed[0:HALF] = jnp.zeros((HALF, width), bf16)

    @pl.when(second)
    def _():
        ext_pass.wait_send()

    save(normed, normed_out)
    save(ext, ext_out)
    save(mixed, mixed_out)
    save(logs, log_out)
    mixed_copy = remote(
        mixed.at[pl.ds(pl.multiple_of((1 - core) * tok, tok), tok)], mixed_far,
        mixed_sems.at[0], mixed_sems.at[1], beside,
    )
    mixed_copy.start()
    proj_pass.wait_recv()
    mixed_copy.wait_recv()

    def second_norm(step, carry):
        at = pl.ds(pl.multiple_of(step * STRIP, STRIP), STRIP)
        value = x_ref[at].astype(f32) + (
            dot(mixed[pl.ds(pl.multiple_of(mine + step * STRIP, STRIP), STRIP)], proj[0])
            + dot(mixed_far[at], proj[1])
        )
        hidden[at] = value
        scaled, _ = normalise(value)
        normed_two[at] = (scaled * gain_two_ref[...][None, :] + shift_two_ref[...][None, :]).astype(bf16)
        return carry

    lax.fori_loop(0, tok // STRIP, second_norm, 0)
    save(hidden, hidden_out)

    def place_rows(step, carry):
        at = pl.ds(pl.multiple_of(step * STRIP, STRIP), STRIP)
        rows[at] = dot(placing[at], normed_two[...]).astype(bf16)
        return carry

    lax.fori_loop(0, total // STRIP, place_rows, 0)
    save(rows, rows_out)
    own_rows.wait()
    for other in others:
        row_copy(me, other).wait_recv()
        row_copy(other, me).wait_send()
    for index in range(4):
        w_copy(index).wait_send()
        w_pass(index).wait_send()
    for copy in (proj_pass, normed_copy, mixed_copy):
        copy.wait_send()
    for copy in saves:
        copy.wait()
    w_in_copy.wait()


def run_forward(
    x, cotangent, routes, factor, gain_one, shift_one, gain_two, shift_two, w_heads, w_proj, w_in, experts, cap, slots
):
    tok, width = x.shape
    rows = 2 * tok
    total = experts * slots
    part = w_proj.shape[0]
    anyspace, vmem = pl.BlockSpec(memory_space=pl.ANY), pl.BlockSpec(memory_space=pltpu.VMEM)
    smem = pl.BlockSpec(memory_space=pltpu.SMEM)
    dma = pltpu.SemaphoreType.DMA
    kept = [
        ((HALF + rows, width), bf16),
        ((rows, 3 * PAIRS * PAIR), bf16),
        ((HALF, 2 * PAIRS * PAIR), bf16),
        ((rows, PAIRS * PAIR), bf16),
        ((PAIRS, 8, rows), f32),
        ((3, 2 * part, width), bf16),
    ]
    late = [((tok, width), f32), ((total, width), bf16)]
    return pl.pallas_call(
        functools.partial(forward_kernel, experts, slots, cap),
        in_specs=[vmem, vmem, vmem, smem] + [vmem] * 4 + [anyspace] * 3,
        out_specs=[anyspace] * 12,
        out_shape=[
            jax.ShapeDtypeStruct(*item)
            for item in kept
            + [((2 * part, width), bf16)]
            + late
            + [((total, width), bf16), ((tok, total), bf16), (w_in.shape, bf16)]
        ],
        scratch_shapes=[pltpu.VMEM(*item) for item in kept + [((2, 2 * part, width), bf16)] + late]
        + [
            pltpu.VMEM((total, tok), bf16),
            pltpu.VMEM((tok, total), bf16),
            pltpu.VMEM((total, width), bf16),
            pltpu.VMEM((tok, PAIRS * PAIR), bf16),
            pltpu.VMEM((tok, width), bf16),
            pltpu.VMEM((HALF + rows, PAIR), bf16),
            pltpu.VMEM((PAIR, HALF + rows), bf16),
            dma((2, 4)), dma((2, 4)), dma((2,)), dma((2,)), dma((2,)), dma((2, 2)), dma((2,)),
            dma((experts,)), dma((experts,)), dma((3,)), dma((10,)),
        ],
        compiler_params=pltpu.CompilerParams(
            collective_id=4, has_side_effects=True, vmem_limit_bytes=56 * 2**20
        ),
        cost_estimate=pl.CostEstimate(flops=30 * 10**9, bytes_accessed=30 * 10**6, transcendentals=8 * 10**6),
        name="forward",
    )(x, cotangent, routes, factor, gain_one, shift_one, gain_two, shift_two, w_heads, w_proj, w_in)


def backward_kernel(
    experts, slots,
    x_ref, cot_ref, factor_ref, hidden_ref, gain_one_ref, gain_two_ref, placing_ref, d_returned_ref,
    result_ref, normed_ref, qkv_ref, ext_ref, mixed_ref, log_ref, heads_ref, proj_ref, router_ref,
    there_in_ref, there_out_ref,
    output_ref, input_grad_ref, total_ref, small_ref, far_in_ref, far_out_ref,
    returned, d_hidden, d_branch, d_mixed, keys, values, d_keys, d_values, d_qkv, d_ext,
    grads_own, grads_send, grads_recv, d_norm, norm_recv, ext_recv,
    held, half_recv, piece_recv, small_held, small_recv,
    row_send, row_recv, branch_sems, norm_sems, ext_sems, far_sems, grad_sems,
    half_sems, piece_sems, gather_sems, back_sems, small_sems, local_sems,
):
    me, mp = lax.axis_index("dp"), lax.axis_index("mp")
    chip, core = mp // 2, mp % 2
    tok, width = x_ref.shape
    rows = 2 * tok
    part = grads_own.shape[1]
    all_heads = PAIRS * PAIR
    beside = {"mp": mp + 1 - 2 * core}
    across = {"mp": (mp + 2) % 4}
    second = chip == 1
    others = [(me + k) % experts for k in range(1, experts)]
    greet([{"dp": other} for other in others] + [beside, across])

    def chunk(index):
        return pl.ds(pl.multiple_of(index * slots, 16), slots)

    def row_copy(target, source):
        return remote(
            result_ref.at[chunk(target)], returned.at[chunk(source)],
            row_send.at[target], row_recv.at[source], {"dp": target},
        )

    def far_copy(index):
        source, target = ((there_out_ref, far_out_ref), (there_in_ref, far_in_ref))[index]
        return remote(source, target, far_sems.at[0, index], far_sems.at[1, index], across)

    far_copy(0).start()
    own_rows = pltpu.make_async_copy(result_ref.at[chunk(me)], returned.at[chunk(me)], local_sems.at[0])
    own_rows.start()
    for other in others:
        row_copy(other, me).start()

    cot_copy = pltpu.make_async_copy(cot_ref, grads_send, local_sems.at[1])
    cot_copy.start()
    cot_copy.wait()
    small_held[...] = jnp.zeros_like(small_held)
    mine = pl.multiple_of(core * tok, tok)

    def second_norm(step, carry):
        at = pl.ds(pl.multiple_of(step * STRIP, STRIP), STRIP)
        scaled, inverse = normalise(hidden_ref[at])
        d_normed = dot(placing_ref[at], d_returned_ref[...])
        small_held[0, 2:3] += jnp.sum(d_normed * scaled, axis=0, keepdims=True)
        small_held[0, 3:4] += jnp.sum(d_normed, axis=0, keepdims=True)
        positions = mp * tok + step * STRIP + lax.broadcasted_iota(jnp.int32, (STRIP, 1), 0)
        total = grads_send[at].astype(f32) * pick_sequence(positions, factor_ref) + norm_pull(
            d_normed, scaled, inverse, gain_two_ref[...][None, :]
        )
        d_hidden[at] = total
        d_branch[pl.ds(pl.multiple_of(mine + step * STRIP, STRIP), STRIP)] = total.astype(bf16)
        return carry

    lax.fori_loop(0, tok // STRIP, second_norm, 0)
    own_branch = d_branch.at[pl.ds(mine, tok)]
    branch_copy = remote(own_branch, own_branch, branch_sems.at[0], branch_sems.at[1], beside)
    branch_copy.start()
    branch_copy.wait()

    def push_branch(step, carry):
        at = pl.ds(pl.multiple_of(step * STRIP, STRIP), STRIP)
        d_mixed[at] = dot(d_branch[at], proj_ref[...], NT).astype(bf16)
        return carry

    lax.fori_loop(0, rows // STRIP, push_branch, 0)

    side, line = me % 2, me // 2
    lines = experts // 2
    partner = {"dp": me + 1 - 2 * side}
    mates = [(line + k) % lines for k in range(1, lines)]
    piece_rows = held.shape[1] // lines
    own_columns = pl.ds(pl.multiple_of(side * (width // 2), 128), width // 2)
    other_columns = pl.ds(pl.multiple_of((1 - side) * (width // 2), 128), width // 2)

    def piece(index):
        return pl.ds(pl.multiple_of(index * piece_rows, 16), piece_rows)

    def sent(index):
        return slice(index * part, (index + 1) * part)

    def grad_copy(index):
        return remote(
            grads_send.at[sent(index)], grads_recv.at[index], grad_sems.at[0, index], grad_sems.at[1, index], across
        )

    def half_copy(index):
        return remote(
            held.at[index, :, other_columns], half_recv.at[index],
            half_sems.at[0, index], half_sems.at[1, index], partner,
        )

    def piece_copy(index, target, source):
        return remote(
            held.at[index, piece(target), own_columns], piece_recv.at[index, source],
            piece_sems.at[0, index, target], piece_sems.at[1, index, source], {"dp": 2 * target + side},
        )

    def gather_copy(index, target, source):
        block = total_ref.at[index, piece(source), own_columns]
        return remote(
            block, block,
            gather_sems.at[0, index, target], gather_sems.at[1, index, source], {"dp": 2 * target + side},
        )

    def back_copy(index):
        block = total_ref.at[index, :, own_columns]
        return remote(block, block, back_sems.at[0, index], back_sems.at[1, index], partner)

    def send_grad(index, grad):
        for own in range(2):

            @pl.when(chip == own)
            def _():
                grads_own[index] = grad[own * part : (own + 1) * part]
                grads_send[sent(index)] = grad[(1 - own) * part : (2 - own) * part].astype(bf16)

        grad_copy(index).start()

    chunks = held.shape[0]
    parts = 4 // chunks

    def stage_one(index):
        if index >= chunks:
            return
        for at in range(parts):
            number = index * parts + at
            grad_copy(number).wait_recv()
            held[index, at * part : (at + 1) * part] = (
                grads_own[number] + grads_recv[number].astype(f32)
            ).astype(bf16)
        if held.shape[1] > parts * part:
            held[index, parts * part :] = jnp.zeros((held.shape[1] - parts * part, width), bf16)
        half_copy(index).start()

    def stage_two(index):
        if index >= chunks:
            return
        half_copy(index).wait_recv()
        held[index, :, own_columns] = (
            held[index, :, own_columns].astype(f32) + half_recv[index].astype(f32)
        ).astype(bf16)
        for mate in mates:
            piece_copy(index, mate, line).start()

    def stage_three(index):
        if index >= chunks:
            return
        value = held[index, piece(line), own_columns].astype(f32)
        for mate in mates:
            piece_copy(index, line, mate).wait_recv()
            value += piece_recv[index, mate].astype(f32)
        total_ref[index, piece(line), own_columns] = value.astype(bf16)
        for mate in mates:
            gather_copy(index, mate, line).start()

    def stage_four(index):
        if index >= chunks:
            return
        for mate in mates:
            gather_copy(index, line, mate).wait_recv()
        back_copy(index).start()

    send_grad(0, dot(mixed_ref[...], d_branch[...], TN))

    lane = lax.broadcasted_iota(jnp.int32, (1, PAIR), 1)

    def attention(pair, carry):
        def column(offset):
            return pl.ds(pl.multiple_of((offset * PAIRS + pair) * PAIR, PAIR), PAIR)

        keys[0:HALF] = ext_ref[:, column(0)]
        keys[HALF:] = qkv_ref[:, column(1)]
        values[0:HALF] = ext_ref[:, column(1)]
        values[HALF:] = qkv_ref[:, column(2)]
        d_keys[...] = jnp.zeros_like(d_keys)
        d_values[...] = jnp.zeros_like(d_values)

        def run(first, whole):
            span = (whole + 1) * BLOCK
            start = pl.multiple_of(first + HALF - whole * BLOCK, BLOCK)
            at = pl.ds(first, BLOCK)
            queries = qkv_ref[at, column(0)] * bf16(0.125)
            d_out = d_mixed[at, column(0)]
            near = keys[pl.ds(start, span)]
            near_values = values[pl.ds(start, span)]
            product = (d_out.astype(f32) * mixed_ref[at, column(0)].astype(f32)).T
            dq = dk = dv = 0.0
            for head in range(2):
                here = (lane // HEAD_DIM) == head
                own = jnp.where(here, queries, bf16(0))
                d_own = jnp.where(here, d_out, bf16(0))
                delta = jnp.sum(product[HEAD_DIM * head : HEAD_DIM * (head + 1)], axis=0, keepdims=True)
                scores = mask_diagonal(dot(near, own, NT), whole)
                probs = jnp.exp(scores - log_ref[pair, head : head + 1, at])
                d_probs = dot(near_values, d_own, NT)
                d_scores = (probs * (d_probs - delta)).astype(bf16)
                dv = dv + dot(probs.astype(bf16), d_own)
                dk = dk + dot(d_scores, own)
                dq = dq + dot(d_scores, jnp.where(here, near, bf16(0)), TN)
            d_qkv[at, column(0)] = (dq * 0.125).astype(bf16)
            d_keys[pl.ds(start, span)] += dk
            d_values[pl.ds(start, span)] += dv

        for whole in range(4):
            run(pl.multiple_of((2 * chip + whole) * BLOCK, BLOCK), whole)

        @pl.when(second)
        def _():
            run(0, 2)
            run(BLOCK, 3)

        @pl.when(chip == 0)
        def _():
            run(4 * BLOCK, 0)
            run(5 * BLOCK, 1)

        d_qkv[:, column(1)] = d_keys[HALF:].astype(bf16)
        d_qkv[:, column(2)] = d_values[HALF:].astype(bf16)
        d_ext[:, column(0)] = d_keys[0:HALF].astype(bf16)
        d_ext[:, column(1)] = d_values[0:HALF].astype(bf16)
        return carry

    lax.fori_loop(0, PAIRS, attention, 0)

    norm_send, ext_part = d_branch.at[0:tok], d_branch.at[tok : tok + HALF]

    ext_beside = remote(ext_part, ext_recv, ext_sems.at[0, 0], ext_sems.at[1, 0], beside)
    ext_across = remote(ext_part, ext_recv, ext_sems.at[0, 1], ext_sems.at[1, 1], across)

    @pl.when(second)
    def _():
        ext_part[...] = dot(d_ext[...], heads_ref[1:3].reshape(2 * all_heads, width)).astype(bf16)

    @pl.when(mp == 2)
    def _():
        ext_beside.start()

    send_grad(1, dot(d_qkv[:, 0:all_heads], normed_ref[HALF:], TN))

    @pl.when(mp == 3)
    def _():
        ext_beside.wait_recv()
        ext_part[...] = (ext_part[...].astype(f32) + ext_recv[...].astype(f32)).astype(bf16)
        ext_across.start()

    for index in (1, 2):
        at = slice(index * all_heads, (index + 1) * all_heads)
        send_grad(
            1 + index,
            dot(d_qkv[:, at], normed_ref[HALF:], TN)
            + dot(d_ext[:, (index - 1) * all_heads : index * all_heads], normed_ref[0:HALF], TN),
        )
    stage_one(0)

    weights = heads_ref[...].reshape(3 * all_heads, width)

    def push_norm(step, carry):
        at = pl.ds(pl.multiple_of((1 - core) * tok + step * STRIP, STRIP), STRIP)
        norm_send[pl.ds(pl.multiple_of(step * STRIP, STRIP), STRIP)] = dot(d_qkv[at], weights).astype(bf16)
        return carry

    def pull_norm(step, carry):
        at = pl.ds(pl.multiple_of(mine + step * STRIP, STRIP), STRIP)
        d_norm[pl.ds(pl.multiple_of(step * STRIP, STRIP), STRIP)] = dot(d_qkv[at], weights)
        return carry

    lax.fori_loop(0, tok // STRIP, push_norm, 0)
    norm_copy = remote(norm_send, norm_recv, norm_sems.at[0], norm_sems.at[1], beside)
    norm_copy.start()
    lax.fori_loop(0, tok // STRIP, pull_norm, 0)
    stage_two(0)
    own_rows.wait()
    for other in others:
        row_copy(me, other).wait_recv()

    def finish(step, carry):
        at = pl.ds(pl.multiple_of(step * STRIP, STRIP), STRIP)
        output_ref[at] = (hidden_ref[at] + dot(placing_ref[at], returned[...])).astype(bf16)
        return carry

    lax.fori_loop(0, tok // STRIP, finish, 0)
    stage_three(0)
    norm_copy.wait_recv()

    @pl.when(mp == 1)
    def _():
        ext_across.wait_recv()
        d_norm[tok - HALF :] += ext_recv[...].astype(f32)

    def first_norm(step, carry):
        at = pl.ds(pl.multiple_of(step * STRIP, STRIP), STRIP)
        scaled, inverse = normalise(x_ref[at].astype(f32))
        d_normed = d_norm[at] + norm_recv[at].astype(f32)
        small_held[0, 0:1] += jnp.sum(d_normed * scaled, axis=0, keepdims=True)
        small_held[0, 1:2] += jnp.sum(d_normed, axis=0, keepdims=True)
        input_grad_ref[at] = (
            d_hidden[at] + norm_pull(d_normed, scaled, inverse, gain_one_ref[...][None, :])
        ).astype(bf16)
        return carry

    lax.fori_loop(0, tok // STRIP, first_norm, 0)

    small_rows = lax.broadcasted_iota(jnp.int32, small_ref.shape, 0)
    small_held[0] = jnp.where(small_rows == 8 + me, router_ref[...], small_held[0])

    small_devices = [across, beside, partner]
    stride = 1
    while stride < lines:
        mate = line + stride * (1 - 2 * (line // stride % 2))
        small_devices.append({"dp": 2 * mate + side})
        stride *= 2

    def small_step(index):
        return remote(
            small_held.at[index], small_recv.at[index],
            small_sems.at[0, index], small_sems.at[1, index], small_devices[index],
        )

    def small_sum(index):
        small_step(index).wait_recv()
        small_held[index + 1] = small_held[index] + small_recv[index]

    small_step(0).start()
    far_copy(1).start()
    stage_one(1)
    stage_four(0)
    stage_two(1)
    stage_one(2)
    small_sum(0)
    small_step(1).start()
    stage_three(1)
    stage_two(2)
    stage_one(3)
    small_sum(1)
    small_step(2).start()
    stage_four(1)
    stage_three(2)
    stage_two(3)
    small_sum(2)
    small_step(3).start()
    stage_four(2)
    small_sum(3)
    for index in range(4, len(small_devices)):
        small_step(index).start()
        if index == 4:
            stage_three(3)
        small_sum(index)
    small_ref[...] = small_held[len(small_devices)]
    stage_four(3)
    for index in range(chunks):
        other = total_ref.at[index, :, other_columns]
        remote(other, other, back_sems.at[0, index], back_sems.at[1, index], partner).wait_recv()

    for other in others:
        row_copy(other, me).wait_send()
    for mate in mates:
        for index in range(chunks):
            piece_copy(index, mate, line).wait_send()
            gather_copy(index, mate, line).wait_send()
    for index in range(4):
        grad_copy(index).wait_send()
    for index in range(chunks):
        half_copy(index).wait_send()
        back_copy(index).wait_send()
    for index in range(len(small_devices)):
        small_step(index).wait_send()
    norm_copy.wait_send()

    @pl.when(mp == 2)
    def _():
        ext_beside.wait_send()

    @pl.when(mp == 3)
    def _():
        ext_across.wait_send()

    for index in range(2):
        far_copy(index).wait()


def run_backward(
    x, cotangent, factor, hidden, gain_one, gain_two, placing, d_returned, result, normed, qkv, ext,
    mixed, log_total, heads, proj, router_grad, there_in, there_out, experts,
):
    tok, width = x.shape
    rows = 2 * tok
    total = d_returned.shape[0]
    part = proj.shape[0] // 2
    lines = experts // 2
    steps = 3 + (lines - 1).bit_length()
    chunks = 4 if part % (16 * lines) == 0 else 2
    padded = (4 // chunks * part + 16 * lines - 1) // (16 * lines) * (16 * lines)
    small = (8 + max(8, experts), width)
    anyspace, vmem = pl.BlockSpec(memory_space=pl.ANY), pl.BlockSpec(memory_space=pltpu.VMEM)
    smem = pl.BlockSpec(memory_space=pltpu.SMEM)
    dma = pltpu.SemaphoreType.DMA
    return pl.pallas_call(
        functools.partial(backward_kernel, experts, total // experts),
        in_specs=[vmem, anyspace, smem] + [vmem] * 5 + [anyspace] + [vmem] * 8 + [anyspace] * 2,
        out_specs=[vmem] * 4 + [anyspace] * 2,
        out_shape=[
            jax.ShapeDtypeStruct((tok, width), bf16),
            jax.ShapeDtypeStruct((tok, width), bf16),
            jax.ShapeDtypeStruct((chunks, padded, width), bf16),
            jax.ShapeDtypeStruct(small, f32),
            jax.ShapeDtypeStruct(there_in.shape, bf16),
            jax.ShapeDtypeStruct(there_out.shape, bf16),
        ],
        scratch_shapes=[
            pltpu.VMEM((total, width), bf16),
            pltpu.VMEM((tok, width), f32),
            pltpu.VMEM((rows, width), bf16),
            pltpu.VMEM((rows, PAIRS * PAIR), bf16),
            pltpu.VMEM((HALF + rows, PAIR), bf16),
            pltpu.VMEM((HALF + rows, PAIR), bf16),
            pltpu.VMEM((HALF + rows, PAIR), f32),
            pltpu.VMEM((HALF + rows, PAIR), f32),
            pltpu.VMEM((rows, 3 * PAIRS * PAIR), bf16),
            pltpu.VMEM((HALF, 2 * PAIRS * PAIR), bf16),
            pltpu.VMEM((4, part, width), f32),
            pltpu.VMEM((4 * part, width), bf16),
            pltpu.VMEM((4, part, width), bf16),
            pltpu.VMEM((tok, width), f32),
            pltpu.VMEM((tok, width), bf16),
            pltpu.VMEM((HALF, width), bf16),
            pltpu.VMEM((chunks, padded, width), bf16),
            pltpu.VMEM((chunks, padded, width // 2), bf16),
            pltpu.VMEM((chunks, lines, padded // lines, width // 2), bf16),
            pltpu.VMEM((steps + 1,) + small, f32),
            pltpu.VMEM((steps,) + small, f32),
            dma((experts,)), dma((experts,)), dma((2,)), dma((2,)), dma((2, 2)), dma((2, 2)), dma((2, 4)),
            dma((2, chunks)), dma((2, chunks, lines)), dma((2, chunks, lines)), dma((2, chunks)),
            dma((2, steps)), dma((2,)),
        ],
        compiler_params=pltpu.CompilerParams(
            collective_id=2, has_side_effects=True, vmem_limit_bytes=62 * 2**20
        ),
        cost_estimate=pl.CostEstimate(flops=30 * 10**9, bytes_accessed=30 * 10**6, transcendentals=8 * 10**6),
        name="backward",
    )(
        x, cotangent, factor, hidden, gain_one, gain_two, placing, d_returned, result, normed, qkv, ext,
        mixed, log_total, heads, proj, router_grad, there_in, there_out,
    )


def gelu_parts(pre):
    scale = 0.7978845608028654
    square = pre * pre
    inner = jnp.tanh(pre * (scale + (scale * 0.044715) * square))
    half = 0.5 * (1.0 + inner)
    slope = half + (0.5 * pre) * (1.0 - inner * inner) * (scale + (3.0 * scale * 0.044715) * square)
    return pre * half, slope

STAGES = 4

def expert_kernel(
    experts, slots, cap,
    rows_ref, cot_ref, router_ref, w_in_ref, w_out_ref, w_in_far_ref,
    back_ref, result_ref, router_grad_ref, here_in_ref, here_out_ref, there_in_ref, there_out_ref,
    router, factor, x, wi, wo, d_out, act, d_pre, total, d_x, give, g_send, g_recv,
    row_send, row_recv, back_send, back_recv, w_send, w_recv, g_send_sem, g_recv_sem, local_sem,
):
    me = lax.axis_index("dp")
    mp = lax.axis_index("mp")
    beside = {"mp": mp + 1 - 2 * (mp % 2)}
    across = {"mp": (mp + 2) % 4}
    members = experts // STAGES
    span = members * slots
    own_group, own_member = me // members, me % members

    def group_of(stage):
        return 2 * ((own_group // 2 + stage // 2) % 2) + (own_group % 2 + stage % 2) % 2

    def chunk(index):
        return pl.ds(pl.multiple_of(index * slots, 16), slots)

    def group_rows(group):
        return pl.ds(pl.multiple_of(group * span, 16), span)

    barrier = pltpu.get_barrier_semaphore()

    def greet(step, carry):
        pl.semaphore_signal(barrier, inc=1, device_id={"dp": (me + step) % experts}, device_id_type=MESH)
        return carry

    lax.fori_loop(1, experts, greet, 0)
    pl.semaphore_signal(barrier, inc=1, device_id=beside, device_id_type=MESH)
    pl.semaphore_signal(barrier, inc=1, device_id=across, device_id_type=MESH)
    pl.semaphore_wait(barrier, experts + 1)

    def remote(src, dst, send, recv, device):
        return pltpu.make_async_remote_copy(
            src_ref=src, dst_ref=dst, send_sem=send, recv_sem=recv, device_id=device, device_id_type=MESH
        )

    def row_copy(target, source):
        return remote(rows_ref.at[chunk(target)], x.at[chunk(source)], row_send.at[target], row_recv.at[source], {"dp": target})

    def back_copy(target, source):
        return remote(give.at[chunk(target)], back_ref.at[chunk(source)], back_send.at[target], back_recv.at[source], {"dp": target})

    def partners(stage):
        group = group_of(stage)
        if stage == 0:
            return [group * members + (own_member + k) % members for k in range(1, members)]
        return [group * members + (own_member + k) % members for k in range(members)]

    for stage in reversed(range(STAGES)):
        for other in partners(stage):
            row_copy(other, me).start()
    own_rows = pltpu.make_async_copy(rows_ref.at[chunk(me)], x.at[chunk(me)], local_sem.at[0])
    own_in = pltpu.make_async_copy(w_in_ref, wi.at[0], local_sem.at[1])
    own_out = pltpu.make_async_copy(w_out_ref, wo.at[0], local_sem.at[2])
    far_in = pltpu.make_async_copy(w_in_far_ref, wi.at[2], local_sem.at[3])
    near_in = remote(w_in_ref, wi.at[1], w_send.at[0], w_recv.at[0], beside)
    near_out = remote(w_out_ref, wo.at[1], w_send.at[1], w_recv.at[1], beside)
    far_near_in = remote(w_in_far_ref, wi.at[3], w_send.at[2], w_recv.at[2], beside)
    far_out = remote(w_out_ref, wo.at[2], w_send.at[3], w_recv.at[3], across)
    far_near_out = remote(wo.at[2], wo.at[3], w_send.at[4], w_recv.at[4], beside)
    for copy in (own_rows, own_in, own_out, near_in, near_out, far_in, far_out, far_near_in):
        copy.start()
    router_grad_ref[...] = jnp.zeros_like(router_grad_ref)
    router[...] = router_ref[...].astype(f32)

    diagonal = lax.broadcasted_iota(jnp.int32, (slots, slots), 0) == lax.broadcasted_iota(
        jnp.int32, (slots, slots), 1
    )

    def prepare(stage, rows):
        for member in range(members):
            index = group_of(stage) * members + member
            spare = cot_ref[pl.ds(pl.multiple_of((index + 1) * slots - 16, 16), 16)].astype(f32)
            spare = spare[cap - slots + 16 : cap - slots + 17]
            value = spare[:, 0:slots] + spare[:, x.shape[1] // 2 : x.shape[1] // 2 + slots]
            factor[chunk(index)] = jnp.sum(jnp.where(diagonal, value, 0.0), axis=1, keepdims=True)
        features = x[rows].astype(f32)
        gate = jax.nn.sigmoid(jnp.sum(features * router[pl.ds(me, 1)], axis=1, keepdims=True))
        d_out[rows] = (gate * (cot_ref[rows].astype(f32) * factor[rows])).astype(bf16)
        total[rows] = jnp.zeros((span, x.shape[1]), f32)
        d_x[rows] = jnp.zeros((span, x.shape[1]), f32)

    def finish(stage, rows):
        features = x[rows].astype(f32)
        gate = jax.nn.sigmoid(jnp.sum(features * router[pl.ds(me, 1)], axis=1, keepdims=True))
        value = total[rows]
        d_gate = jnp.sum(cot_ref[rows].astype(f32) * factor[rows] * value, axis=1, keepdims=True)
        d_logit = (d_gate * gate * (1.0 - gate)).astype(bf16).astype(f32)
        give[rows] = (d_x[rows] + d_logit * router[pl.ds(me, 1)]).astype(bf16)
        result_ref[rows] = (gate * value).astype(bf16)
        router_grad_ref[...] += jnp.sum(features * d_logit, axis=0, keepdims=True)

    def stage_of(step):
        return jnp.where(
            (step < 2) | (step >= 14), 0, jnp.where(step < 6, 3, jnp.where(step < 10, 2, 1))
        )

    def step_body(step, carry):
        stage = stage_of(step)
        part = jnp.where(step < 4, step % 2, jnp.where(step < 6, step - 2, (step - 6) % 4))
        part = jnp.where(step >= 14, step - 12, part)
        rows = group_rows(group_of(stage))

        for static, at in enumerate((0, 10, 6, 2)):
            @pl.when(step == at)
            def _():
                if static == 0:
                    own_rows.wait()
                for other in partners(static):
                    row_copy(me, other).wait_recv()
        @pl.when((step == 0) | (step == 2) | (step == 6) | (step == 10))
        def _():
            prepare(stage, rows)

        @pl.when(step == 0)
        def _():
            own_in.wait()
            own_out.wait()

        @pl.when(step == 1)
        def _():
            near_in.wait_recv()
            near_out.wait_recv()

        @pl.when(step == 4)
        def _():
            far_in.wait()
            far_out.wait_recv()
            far_near_out.start()

        @pl.when(step == 5)
        def _():
            far_near_in.wait_recv()
            far_near_out.wait_recv()

        pre = dot(x[rows], wi[part])
        value, slope = gelu_parts(pre)
        value = value.astype(bf16)
        act[part, rows] = value
        total[rows] += dot(value, wo[part])
        d_value = (dot(d_out[rows], wo[part], NT) * slope).astype(bf16)
        d_pre[part, rows] = d_value
        d_x[rows] += dot(d_value, wi[part], NT)

        @pl.when((step == 5) | (step == 9) | (step == 13) | (step == 15))
        def _():
            finish(stage, rows)

        for static, at in enumerate((15, 13, 9, 5)):
            @pl.when(step == at)
            def _():
                for other in partners(static):
                    back_copy(other, me).start()
        return carry

    lax.fori_loop(0, 16, step_body, 0)
    own_back = pltpu.make_async_copy(give.at[chunk(me)], back_ref.at[chunk(me)], local_sem.at[4])
    own_back.start()

    def grad_copy(index):
        return remote(outgoing[index], g_recv.at[index], g_send_sem.at[index], g_recv_sem.at[index], beside)

    kept = pl.ds(0, x.shape[1])
    outgoing = [g_send, act.at[3, kept], d_pre.at[3, kept], act.at[1, kept]]
    for index, part in enumerate((3, 1)):
        outgoing[2 * index][...] = dot(act[part], d_out[...], TN).astype(bf16)
        grad_copy(2 * index).start()
        outgoing[2 * index + 1][...] = dot(x[...], d_pre[part], TN).astype(bf16)
        grad_copy(2 * index + 1).start()
    grad = dot(act[2], d_out[...], TN)
    grad_copy(0).wait_recv()
    there_out_ref[...] = (grad + g_recv[0].astype(f32)).astype(bf16)
    grad = dot(x[...], d_pre[2], TN)
    grad_copy(1).wait_recv()
    there_in_ref[...] = (grad + g_recv[1].astype(f32)).astype(bf16)
    grad = dot(act[0], d_out[...], TN)
    grad_copy(2).wait_recv()
    here_out_ref[...] = grad + g_recv[2].astype(f32)
    grad = dot(x[...], d_pre[0], TN)
    grad_copy(3).wait_recv()
    here_in_ref[...] = grad + g_recv[3].astype(f32)

    own_back.wait()
    for stage in range(STAGES):
        for other in partners(stage):
            back_copy(me, other).wait_recv()
            back_copy(other, me).wait_send()
            row_copy(other, me).wait_send()
    for copy in (near_in, near_out, far_near_in, far_out, far_near_out):
        copy.wait_send()
    for index in range(4):
        grad_copy(index).wait_send()


def run_expert(rows, cot_rows, router, w_in, w_out, w_in_far, experts, cap):
    total, width = rows.shape
    slots = total // experts
    hidden = w_in.shape[1]
    anyspace, vmem = pl.BlockSpec(memory_space=pl.ANY), pl.BlockSpec(memory_space=pltpu.VMEM)
    dma = pltpu.SemaphoreType.DMA
    return pl.pallas_call(
        functools.partial(expert_kernel, experts, slots, cap),
        in_specs=[anyspace, vmem, vmem, anyspace, anyspace, anyspace],
        out_specs=[vmem] * 7,
        out_shape=[
            jax.ShapeDtypeStruct((total, width), bf16),
            jax.ShapeDtypeStruct((total, width), bf16),
            jax.ShapeDtypeStruct((1, width), f32),
            jax.ShapeDtypeStruct((width, hidden), f32),
            jax.ShapeDtypeStruct((hidden, width), f32),
            jax.ShapeDtypeStruct((width, hidden), bf16),
            jax.ShapeDtypeStruct((hidden, width), bf16),
        ],
        scratch_shapes=[
            pltpu.VMEM(router.shape, f32),
            pltpu.VMEM((total, 1), f32),
            pltpu.VMEM((total, width), bf16),
            pltpu.VMEM((4, width, hidden), bf16),
            pltpu.VMEM((4, hidden, width), bf16),
            pltpu.VMEM((total, width), bf16),
            pltpu.VMEM((4, total, hidden), bf16),
            pltpu.VMEM((4, total, hidden), bf16),
            pltpu.VMEM((total, width), f32),
            pltpu.VMEM((total, width), f32),
            pltpu.VMEM((total, width), bf16),
            pltpu.VMEM((width, width), bf16),
            pltpu.VMEM((4, width, width), bf16),
            dma((experts,)), dma((experts,)), dma((experts,)), dma((experts,)),
            dma((5,)), dma((5,)), dma((4,)), dma((4,)), dma((5,)),
        ],
        compiler_params=pltpu.CompilerParams(
            collective_id=1, has_side_effects=True, vmem_limit_bytes=60 * 2**20
        ),
        cost_estimate=pl.CostEstimate(flops=30 * 10**9, bytes_accessed=40 * 10**6, transcendentals=3 * 10**6),
        name="expert",
    )(rows, cot_rows, router, w_in, w_out, w_in_far)


def shards(
    inputs, cotangent, routes, domains, domain_counts, domain_weights, keep_mask, gain_one, shift_one,
    w_qkv, w_proj, gain_two, shift_two, w_router, w_in, w_out,
):
    tok, width = inputs.shape
    experts = w_router.shape[1]
    cap = max(2, tok * 5 // (4 * experts))
    slots = (cap + 16) // 16 * 16
    domain_ids = jnp.arange(domain_weights.shape[0], dtype=jnp.int32)
    same_domain = domains[:, None] == domain_ids[None, :]
    seq_weight = jnp.sum(jnp.where(same_domain, domain_weights[None, :], 0.0), axis=1)
    seq_counts = jnp.sum(jnp.where(same_domain, domain_counts[None, :], 0), axis=1).astype(f32)
    factor = keep_mask.astype(f32) * seq_weight * count_scale / seq_counts

    w_own = jnp.transpose(w_qkv, (1, 2, 0))
    normed, qkv, ext, mixed, log_total, heads, proj, hidden, rows, cot_rows, placing_t, w_in_far = run_forward(
        inputs, cotangent, routes.reshape(1, -1), factor, gain_one, shift_one, gain_two,
        shift_two, w_own, w_proj, w_in[0], experts, cap, slots,
    )
    d_returned, result, router_grad, here_in, here_out, there_in, there_out = run_expert(
        rows, cot_rows, w_router.T, w_in[0], w_out[0], w_in_far, experts, cap
    )
    output, input_grad, sums, small, far_in, far_out = run_backward(
        inputs, cotangent, factor, hidden, gain_one, gain_two, placing_t, d_returned, result,
        normed, qkv, ext, mixed, log_total, heads, proj, router_grad, there_in, there_out, experts,
    )
    part = w_proj.shape[0]
    sums = sums[:, : 4 * part // sums.shape[0]].reshape(4, part, -1)
    return (
        output,
        input_grad,
        small[0],
        small[1],
        jnp.transpose(sums[1:].astype(f32), (2, 0, 1)),
        sums[0].astype(f32),
        small[2],
        small[3],
        small[8 : 8 + experts].T,
        (here_in + far_in.astype(f32))[None],
        (here_out + far_out.astype(f32))[None],
    )


def solution(mesh):
    tokens, group = P(("dp", "mp"), None), P("dp")
    return jax.shard_map(
        shards,
        mesh=mesh,
        in_specs=(
            tokens, tokens, P("dp", None), group, P(), P(), group, P(), P(),
            P(None, None, "mp"), P("mp", None), P(), P(), P(),
            P("dp", None, "mp"), P("dp", "mp", None),
        ),
        out_specs=(
            tokens, tokens, P(), P(), P(None, None, "mp"), P("mp", None), P(), P(), P(),
            P("dp", None, "mp"), P("dp", "mp", None),
        ),
        check_vma=False,
    )
```

time: 359 us -> 292 us (0.81)
  the two profiles are of different devices: /device:TPU:12 before, /device:TPU:1 now
where the time goes in v4:
time: 292 us; the launch traced here: 289 us
  Pallas kernels  273 us (93%)
  other arithmetic  10.9 us (4%)
  local copies, waits for them, and re-layouts  3.96 us (1%)
    pallas_call x1, Pallas kernels, run_backward(): pl.pallas_call(functools.partial(backward_kernel, experts, total // exper...  123 us
    pallas_call x1, Pallas kernels, run_expert(): pl.pallas_call(functools.partial(expert_kernel, experts, slots, cap), in_...  88.1 us
    pallas_call x1, Pallas kernels, run_forward(): pl.pallas_call(functools.partial(forward_kernel, experts, slots, cap), in...  61.9 us

profile of v4, /device:TPU:1, one launch (start us, length us, event | category | flops | bytes accessed | tf_op | source)
XLA Modules:
  0.0 288.5 jit_solution(5222828976842639601)
XLA Ops:
  0.6 0.9 select_reduce_fusion
  1.5 0.9 select_reduce_fusion.1
  2.4 1.2 convert_divide_fusion.factor_ref
  3.5 61.9 %forward.1 = (bf16[2048,768]{1,0:T(8,128)(2,1)}, bf16[1536,1152]{1,0:T(8,128)(2,1)}, bf16[512,768]{1,0:T(8,128)(2,1)}, bf16[1536,384]{1,0:T(8,128)(2,1)}, f32[3,...) custom-call(bf16[768,768]{1,0:T(8,128)(2,1)} %x_ref.3, ...), custom_call_target="tpu_custom_call" | custom-call | flops 30000001024 | bytes 30000000 | tf_op jit(solution)/shard_map/forward/pallas_call | solution.py:390
  65.4 88.1 %expert.1 = (bf16[1024,768]{1,0:T(8,128)(2,1)}, bf16[1024,768]{1,0:T(8,128)(2,1)}, f32[1,768]{1,0:T(1,128)}, f32[768,768]{1,0:T(8,128)}, f32[768,768]{1,0:T(8,12...) custom-call(bf16[1024,768]{1,0:T(8,128)(2,1)} %get-tuple-element.38.rows_ref, ...), custom_call_target="tpu_custom_call" | custom-call | flops 30000001024 | bytes 40000000 | tf_op jit(solution)/shard_map/expert/pallas_call | solution.py:1090
  153.6 122.7 %backward.1 = (bf16[768,768]{1,0:T(8,128)(2,1)}, bf16[768,768]{1,0:T(8,128)(2,1)}, bf16[4,192,768]{2,1,0:T(8,128)(2,1)}, f32[16,768]{1,0:T(8,128)}, bf16[768,768]{1,0:T(8,128)(2,1)}, /*index=5*/bf16[768,768]{1,0:T(8,128)(2,1)}) custom-call(bf16[768,768]{1,0:T(8,128)(2,1)} %x_ref.3, bf16[768,768]{1,0:T(8,128)(2,1)} %cot_ref.3, ...), custom_call_target="tpu_custom_call" | custom-call | flops 30000001024 | bytes 30000000 | tf_op jit(solution)/shard_map/backward/pallas_call | solution.py:827
  276.3 0.0 copy-start.3
  276.4 0.0 copy-start.2
  276.4 5.8 %add_bitcast_fusion = (f32[1,768,768]{2,1,0:T(8,128)}, f32[1,768,768]{2,1,0:T(8,128)}) fusion(f32[768,768]{1,0:T(8,128)} %get-tuple-element.59, bf16[768,768]{1,0:T(8,128)(2,1)} %get-tuple-element.60, f32[768,768]{1,0:T(8,128)} %get-tuple-element.57, bf16[768,768]{1,0:T(8,128)(2,1)} %get-tuple-element.58), kind=kLoop, calls=%fused_computation | loop fusion | flops 2359296 | bytes 11796480 | tf_op jit(solution)/shard_map/broadcast_in_dim | solution.py:1167
  282.1 0.0 copy-done.3
  282.1 0.6 slice_reduce_fusion
  282.8 0.6 slice_bitcast_fusion
  283.4 0.0 copy-done.2
  283.4 0.0 copy-start.1
  283.4 0.9 bitcast_convert_fusion
  284.2 1.3 convert_bitcast_fusion
  285.6 0.0 copy-done.1
  285.6 0.0 copy-start
  285.6 1.0 copy.29
  286.6 0.7 copy-done
  287.3 1.0 copy.30
Async XLA Ops:
  276.3 5.8 %copy-start.3 = (f32[16,768]{1,0:T(8,128)S(1)}, f32[16,768]{1,0:T(8,128)}, u32[]{:S(2)}) copy-start(f32[16,768]{1,0:T(8,128)} %get-tuple-element.55) | copy-start | bytes 147460
  276.4 7.0 %copy-start.2 = (bf16[4,192,768]{2,1,0:T(8,128)(2,1)S(1)}, bf16[4,192,768]{2,1,0:T(8,128)(2,1)}, u32[]{:S(2)}) copy-start(bf16[4,192,768]{2,1,0:T(8,128)(2,1)} %get-tuple-element.56) | copy-start | bytes 3538948
  283.4 2.2 copy-start.1
  285.6 1.7 copy-start
